TPU v7x, 32 devices: a whole 2x2x4 slice. The times are simulated.
32 devices in a mesh: group: 2 (over y), expert: 4 (over z), replica: 2 (over x), tensor: 2 (over core).
Axes of the slice: x: 2, y: 2, z: 4, core: 2. Of those that a mesh axis runs over, the one named last changes fastest.
Arguments:
- tokens: bfloat16 [4, 960, 1024], P(('group', 'replica'), 'expert'), parts along dimension 0, may hold values from -6 to 6
- out_grad: bfloat16 [4, 960, 1024], P(('group', 'replica'), 'expert'), parts along dimension 0, may hold values from -6 to 6
- expert_ids: int32 [4, 960, 8], P(('group', 'replica'), 'expert'), parts along dimension 0, may hold values from 0 to 127, as said below
- route_weight: float32 [4, 960, 8], P(('group', 'replica'), 'expert'), parts along dimension 0, may hold values from 0.05 to 0.5
- gate_proj: bfloat16 [4, 768, 1024], P('expert', 'tensor'), may hold values from -0.1875 to 0.1875
- up_proj: bfloat16 [4, 768, 1024], P('expert', 'tensor'), may hold values from -0.1875 to 0.1875
- down_proj: bfloat16 [4, 768, 1024], P('expert', 'tensor'), may hold values from -0.21875 to 0.21875
- fragment: int32 [2], P('group'), parts along dimension 0, may hold values from 0 to 3
Outputs:
- grad_gate: bfloat16 [4, 4, 768, 1024], P(('group', 'replica'), 'expert', 'tensor'), parts along dimension 0
- grad_up: bfloat16 [4, 4, 768, 1024], P(('group', 'replica'), 'expert', 'tensor'), parts along dimension 0
- grad_down: bfloat16 [4, 4, 768, 1024], P(('group', 'replica'), 'expert', 'tensor'), parts along dimension 0
- expert_load: float32 [4, 4], P(('group', 'replica'), 'expert'), parts along dimension 0
There are 2 independent parts, one for each index of `group`. A program takes and returns all parts, laid end to end along the dimension named above; an argument that names none is the same for every part. Nothing has to cross between parts.
Inputs may be any that keep to these rules, and one draw needn't show every extreme that they name: `expert_ids`: each row names 8 different experts. Among the rows of one device (aligned blocks of 240 rows of a replica), each expert below 4 is named by at most 60 rows; in every draw one such expert is named by exactly 60 rows in every block.
All inputs are finite; a program needn't handle non-finite values.
Results may differ from a plain program's by a relative error of at most 0.0058.
Values may be sent and summed in bfloat16 or wider, within the bound.
No kernel may reach another device: no remote copies, remote signals or barrier semaphores. Data moves between devices by JAX's collectives and lax.ppermute only.
A program may use at most 64 MiB of HBM per device.

v0:
```python
import jax
import jax.numpy as jnp
from jax import lax
from jax.sharding import PartitionSpec as P

FRAGS = 4
CAP = 60


def for_sending(array):

    def short(part):
        return part.astype(jnp.bfloat16) if part.dtype == jnp.float32 else part

    return jax.tree.map(short, array)


def contract(left, right, left_dim, right_dim):
    return lax.dot_general(
        left, right, (((left_dim,), (right_dim,)), ((), ())), preferred_element_type=jnp.float32
    )


def add_terms(carried, x_block, q_block, w_gate, w_up, w_down):
    gate_pre = contract(x_block, w_gate, 1, 1)
    up_pre = contract(x_block, w_up, 1, 1)
    gate_sig = jax.nn.sigmoid(gate_pre)
    gate_act = gate_pre * gate_sig
    hidden = (gate_act * up_pre).astype(jnp.bfloat16)
    hidden_grad = contract(q_block, w_down, 1, 1)
    gate_grad = (hidden_grad * up_pre * gate_sig * (1.0 + gate_pre * (1.0 - gate_sig))).astype(
        jnp.bfloat16
    )
    up_grad = (hidden_grad * gate_act).astype(jnp.bfloat16)
    term_gate = contract(gate_grad, x_block, 0, 0)
    term_up = contract(up_grad, x_block, 0, 0)
    term_down = contract(hidden, q_block, 0, 0)
    return (carried[0] + term_gate, carried[1] + term_up, carried[2] + term_down)


def per_device(tokens, out_grad, expert_ids, route_weight, gate_proj, up_proj, down_proj, fragment):
    experts = lax.axis_size("expert")
    rows_in = tokens[0]
    grads_in = out_grad[0]
    routed = expert_ids[0]
    weights_in = route_weight[0]
    tok_count = rows_in.shape[0]
    width = rows_in.shape[1]
    column = jnp.arange(experts, dtype=jnp.int32)
    matches = routed[:, :, None] == column[None, None, :]
    member = jnp.any(matches, axis=1)
    token_weight = jnp.sum(jnp.where(matches, weights_in[:, :, None], 0.0), axis=1)
    member_int = member.astype(jnp.int32)
    counts = jnp.sum(member_int, axis=0)
    position = jnp.cumsum(member_int, axis=0) - 1
    slot_ids = jnp.arange(CAP, dtype=jnp.int32)
    placed = member[:, None, :] & (position[:, None, :] == slot_ids[None, :, None])
    token_ids = jnp.arange(tok_count, dtype=jnp.int32)
    source_row = jnp.sum(jnp.where(placed, token_ids[:, None, None], 0), axis=0).T
    filled = slot_ids[None, :] < counts[:, None]
    chosen_weight = jnp.take_along_axis(token_weight.T, source_row, axis=1)
    zero_half = jnp.zeros((), jnp.bfloat16)
    rows_x = jnp.where(filled[:, :, None], rows_in[source_row], zero_half)
    rows_q = jnp.where(
        filled[:, :, None], chosen_weight[:, :, None] * grads_in[source_row], 0.0
    ).astype(jnp.bfloat16)
    sent_counts = jnp.sum(filled.astype(jnp.int32), axis=1).astype(jnp.bfloat16)[:, None]
    got_x, got_q, got_counts = (
        lax.all_to_all(rows_x, "expert", split_axis=0, concat_axis=0, tiled=True),
        lax.all_to_all(rows_q, "expert", split_axis=0, concat_axis=0, tiled=True),
        lax.all_to_all(sent_counts, "expert", split_axis=0, concat_axis=0, tiled=True),
    )
    received = got_counts[:, 0].astype(jnp.int32)
    ends = jnp.cumsum(received)
    starts = ends - received
    total = ends[experts - 1]
    all_rows = experts * CAP
    block_rows = min(256, all_rows)
    padded_rows = (all_rows + block_rows - 1) // block_rows * block_rows
    row_ids = jnp.arange(padded_rows, dtype=jnp.int32)
    source = jnp.minimum(
        jnp.sum((row_ids[:, None] >= ends[None, :]).astype(jnp.int32), axis=1), experts - 1
    )
    source_hit = source[:, None] == column[None, :]
    offset = row_ids - jnp.sum(jnp.where(source_hit, starts[None, :], 0), axis=1)
    live = row_ids < total
    flat_index = jnp.where(live, source * CAP + offset, 0)
    compact_x = jnp.where(live[:, None], got_x.reshape(all_rows, width)[flat_index], zero_half)
    compact_q = jnp.where(live[:, None], got_q.reshape(all_rows, width)[flat_index], zero_half)
    w_gate = gate_proj[0]
    w_up = up_proj[0]
    w_down = down_proj[0]
    empty = jnp.zeros((w_gate.shape[0], width), jnp.float32)

    def one_block(block_index, carried):
        x_block = lax.dynamic_slice_in_dim(compact_x, block_index * block_rows, block_rows, 0)
        q_block = lax.dynamic_slice_in_dim(compact_q, block_index * block_rows, block_rows, 0)
        return add_terms(carried, x_block, q_block, w_gate, w_up, w_down)

    block_count = (total + block_rows - 1) // block_rows
    grads_sum = lax.fori_loop(0, block_count, one_block, (empty, empty, empty))
    load_rows = total.astype(jnp.float32)
    frag_width = width // FRAGS
    begin = fragment[0] * frag_width
    pieces = tuple(
        (lax.dynamic_slice_in_dim(grad_full, begin, frag_width, 1) for grad_full in grads_sum)
    )
    synced = jax.tree.map(
        lambda part: part.astype(jnp.float32), lax.psum(for_sending(pieces), "replica")
    )
    replicas = lax.axis_size("replica")
    results = tuple(
        (
            lax.dynamic_update_slice_in_dim(grad_full, piece / replicas, begin, 1).astype(
                jnp.bfloat16
            )[None, None]
            for grad_full, piece in zip(grads_sum, synced)
        )
    )
    expert_load = (load_rows / all_rows).reshape(1, 1)
    return (results[0], results[1], results[2], expert_load)


def solution(mesh):
    in_specs = (
        P(("group", "replica"), "expert", None),
        P(("group", "replica"), "expert", None),
        P(("group", "replica"), "expert", None),
        P(("group", "replica"), "expert", None),
        P("expert", "tensor", None),
        P("expert", "tensor", None),
        P("expert", "tensor", None),
        P("group"),
    )
    out_specs = (
        P(("group", "replica"), "expert", "tensor", None),
        P(("group", "replica"), "expert", "tensor", None),
        P(("group", "replica"), "expert", "tensor", None),
        P(("group", "replica"), "expert"),
    )
    return jax.shard_map(
        per_device, mesh=mesh, in_specs=in_specs, out_specs=out_specs, check_vma=False
    )
```

profile of v0, /device:TPU:0, one launch (start us, length us, event | category | flops | bytes accessed | tf_op | source)
XLA Modules:
  0.0 127.0 jit_solution(1549957427426781764)
XLA Ops:
  7.2 0.8 fusion.14
  8.1 0.2 convert_reduce_fusion.3
  8.3 0.7 copy.51
  9.0 6.3 %all-to-all-start = ((bf16[4,1,1]{2,1,0:T(2,128)(2,1)}), bf16[4,1,1]{2,1,0:T(2,128)(2,1)S(1)}, u32[]{:S(2)}, u32[]{:S(2)}) async-start(bf16[4,1,1]{2,1,0:T(2,128)(2,1)} %copy.51), calls=%async_computation | async-start | bytes 4096 | tf_op jit(solution)/shard_map/all_to_all | solution.py:71
  15.4 1.2 reduce-window.11
  17.0 1.1 select_reduce_fusion
  18.3 0.7 select_reduce_fusion.1
  19.1 0.1 copy.55
  19.2 2.8 %gather_fusion.4 = f32[240]{0:T(256)S(1)} fusion(f32[4,240]{0,1:T(8,128)S(1)} %bitcast.51, s32[240]{0:T(256)S(1)} %reshape.194), kind=kCustom, calls=%fused_computation.4 | custom fusion | bytes 3840 | tf_op jit(solution)/shard_map/jit(take_along_axis)/gather | solution.py:61
  22.2 1.1 gather_fusion
  23.5 1.0 select_convert_fusion
  24.4 5.1 %all-to-all-start.1 = ((bf16[4,60,1024]{2,1,0:T(8,128)(2,1)}), bf16[4,60,1024]{2,1,0:T(8,128)(2,1)S(1)}, u32[]{:S(2)}, u32[]{:S(2)}) async-start(bf16[4,60,1024]{2,1,0:T(8,128)(2,1)} %select_convert_fusion), calls=%async_computation.1 | async-start | bytes 1048576 | tf_op jit(solution)/shard_map/all_to_all | solution.py:70
  29.5 1.1 gather_fusion.2
  31.4 0.9 broadcast_select_fusion
  32.3 0.2 convert_reduce_fusion.2
  32.5 0.2 reduce-window.10
  32.7 0.6 slice.13
  34.1 9.4 %all-to-all-done.1 = bf16[4,60,1024]{2,1,0:T(8,128)(2,1)S(1)} async-done(((bf16[4,60,1024]{2,1,0:T(8,128)(2,1)}), bf16[4,60,1024]{2,1,0:T(8,128)(2,1)S(1)}, u32[]{:S(2)}, u32[]{:S(2)}) %all-to-all-start.1) | async-done | bytes 491552 | tf_op jit(solution)/shard_map/all_to_all | solution.py:70
  43.5 3.5 %all-to-all-start.2 = ((bf16[4,60,1024]{2,1,0:T(8,128)(2,1)}), bf16[4,60,1024]{2,1,0:T(8,128)(2,1)S(1)}, u32[]{:S(2)}, u32[]{:S(2)}) async-start(bf16[4,60,1024]{2,1,0:T(8,128)(2,1)} %broadcast_select_fusion), calls=%async_computation.2 | async-start | bytes 1048576 | tf_op jit(solution)/shard_map/all_to_all | solution.py:69
  47.0 0.6 iota_compare_fusion.5
  47.7 0.6 compare_select_fusion
  48.5 1.1 gather_fusion.1
  49.6 11.3 %all-to-all-done.2 = bf16[4,60,1024]{2,1,0:T(8,128)(2,1)S(1)} async-done(((bf16[4,60,1024]{2,1,0:T(8,128)(2,1)}), bf16[4,60,1024]{2,1,0:T(8,128)(2,1)S(1)}, u32[]{:S(2)}, u32[]{:S(2)}) %all-to-all-start.2) | async-done | bytes 491552 | tf_op jit(solution)/shard_map/all_to_all | solution.py:69
  61.0 1.1 gather_fusion.3
  62.2 0.5 fusion
  62.6 0.6 copy-done.9
  63.3 0.5 fusion.2
  63.8 0.5 fusion.4
  64.2 1.6 %fusion.10 = f32[384,1024]{1,0:T(8,128)} fusion(f32[240,384]{1,0:T(8,128)S(1)} %fusion.4, f32[240,384]{1,0:T(8,128)S(1)} %fusion, bf16[240,1024]{1,0:T(8,128)(2,1)S(1)} %gather_fusion.3, pred[240]{0:T(512)(128)(4,1)S(1)} %iota_compare_fusion.5), kind=kOutput, calls=%fused_computation.34 | convolution fusion | flops 189542400 | bytes 2801904 | tf_op jit(solution)/shard_map/while/body/dot_general | solution.py:19
  65.9 1.7 %fusion.9 = f32[384,1024]{1,0:T(8,128)} fusion(f32[240,384]{1,0:T(8,128)S(1)} %fusion, f32[240,384]{1,0:T(8,128)S(1)} %fusion.4, f32[240,384]{1,0:T(8,128)S(1)} %fusion.2, bf16[240,1024]{1,0:T(8,128)(2,1)S(1)} %gather_fusion.3, pred[240]{0:T(512)(128)(4,1)S(1)} %iota_compare_fusion.5), kind=kOutput, calls=%fused_computation.33 | convolution fusion | flops 189911040 | bytes 3170544 | tf_op jit(solution)/shard_map/while/body/dot_general | solution.py:19
  67.5 1.6 %fusion.8 = f32[384,1024]{1,0:T(8,128)} fusion(bf16[240,1024]{1,0:T(8,128)(2,1)S(1)} %gather_fusion.1, pred[240]{0:T(512)(128)(4,1)S(1)} %iota_compare_fusion.5, f32[240,384]{1,0:T(8,128)S(1)} %fusion.2, f32[240,384]{1,0:T(8,128)S(1)} %fusion), kind=kOutput, calls=%fused_computation.32 | convolution fusion | flops 189542400 | bytes 2801904 | tf_op jit(solution)/shard_map/while/body/dot_general | solution.py:19
  69.1 0.2 broadcast_in_dim.120
  69.3 1.4 %broadcast_in_dim.120.clone = f32[384,1024]{1,0:T(8,128)} broadcast(f32[]{:T(128)} %constant.67.clone.1), dimensions={} | broadcast | bytes 1572868 | tf_op jit(solution)/shard_map/broadcast_in_dim | solution.py:93
  70.7 1.3 %broadcast_in_dim.120.clone.1 = f32[384,1024]{1,0:T(8,128)} broadcast(f32[]{:T(128)} %constant.67.clone.1), dimensions={} | broadcast | bytes 1572868 | tf_op jit(solution)/shard_map/broadcast_in_dim | solution.py:93
  72.0 6.6 %while.18 = (s32[]{:T(128)}, f32[384,1024]{1,0:T(8,128)S(1)}, f32[384,1024]{1,0:T(8,128)}, f32[384,1024]{1,0:T(8,128)}, s32[]{:T(128)}, /*index=5*/f32[384,1024]...) while((s32[]{:T(128)}, f32[384,1024]{1,0:T(8,128)S(1)}, f32[384,1024]{1,0:T(8,128)}, ...), condition=%wide.region_11.12_spmd, body=%wide.region_10.11_spmd.sunk | while | flops 1179650 | bytes 39321804 | solution.py:101
  72.0 2.0 %add.127 = f32[384,1024]{1,0:T(8,128)S(1)} add(f32[384,1024]{1,0:T(8,128)S(1)} %get-tuple-element.298, f32[384,1024]{1,0:T(8,128)} %get-tuple-element.311) | non-fusion elementwise | flops 393216 | bytes 4718592 | tf_op jit(solution)/shard_map/while/body/add | solution.py:38
  74.0 0.4 copy-done.4
  74.4 0.5 add.128
  74.9 0.9 copy-done.5
  75.8 2.8 %add.129 = f32[384,1024]{1,0:T(8,128)} add(f32[384,1024]{1,0:T(8,128)} %get-tuple-element.300, f32[384,1024]{1,0:T(8,128)S(1)} %copy-done.5) | non-fusion elementwise | flops 393216 | bytes 4718592 | tf_op jit(solution)/shard_map/while/body/add | solution.py:38
  78.6 1.7 %dynamic-slice_convert_fusion = bf16[384,256]{1,0:T(8,128)(2,1)} fusion(f32[384,1024]{1,0:T(8,128)} %get-tuple-element.214, s32[]{:T(128)S(6)} %select_n.88), kind=kLoop, calls=%fused_computation.19 | loop fusion | bytes 393220 | tf_op jit(solution)/shard_map/convert_element_type | solution.py:13
  80.3 1.7 %dynamic-slice_convert_fusion.1 = bf16[384,256]{1,0:T(8,128)(2,1)} fusion(f32[384,1024]{1,0:T(8,128)} %get-tuple-element.213, s32[]{:T(128)S(6)} %select_n.88), kind=kLoop, calls=%fused_computation.21 | loop fusion | bytes 393220 | tf_op jit(solution)/shard_map/convert_element_type | solution.py:13
  82.0 0.7 dynamic-slice_convert_fusion.2
  83.3 29.1 %all-reduce.4.cloned.1.call-done = (bf16[384,256]{1,0:T(8,128)(2,1)}, bf16[384,256]{1,0:T(8,128)(2,1)}, bf16[384,256]{1,0:T(8,128)(2,1)}) async-done(((bf16[384,256]{1,0:T(8,128)(2,1)}, bf16[384,256]{1,0:T(8,128)(2,1)}, bf16[384,256]{1,0:T(8,128)(2,1)}), (bf16[384,256]{1,0:T(8,128)(2,1)}, bf16[384,256]{1,0:T(8,128)(2,1)}, bf16[384,256]{1,0:T(8,128)(2,1)})) %all-reduce.4.cloned.1.call-update) | async-done | bytes 589840 | tf_op jit(solution)/shard_map/psum | solution.py:109
  112.4 2.0 %multiply_dynamic-update-slice_fusion = (f32[384,1024]{1,0:T(8,128)}, f32[384,1024]{1,0:T(8,128)}) fusion(f32[384,1024]{1,0:T(8,128)} %get-tuple-element.214, s32[]{:T(128)S(6)} %select_n.88, bf16[384,256]{1,0:T(8,128)(2,1)} %get-tuple-element.233, f32[384,1024]{1,0:T(8,128)} %get-tuple-element.213, bf16[384,256]{1,0:T(8,128)(2,1)} %get-tuple-element.232), kind=kLoop, calls=%fused_computation.18 | loop fusion | flops 393216 | bytes 1179652 | tf_op jit(solution)/shard_map/dynamic_update_slice | solution.py:114
  114.4 2.5 %convert_bitcast_fusion = bf16[1,1,384,1024]{3,2,1,0:T(8,128)(2,1)} fusion(f32[384,1024]{1,0:T(8,128)} %get-tuple-element.236), kind=kLoop, calls=%fused_computation.12 | loop fusion | flops 393216 | bytes 2359296 | tf_op jit(solution)/shard_map/broadcast_in_dim | solution.py:114
  117.0 1.0 convert_bitcast_fusion.1
  118.0 1.0 convert_bitcast_fusion.2
  (53 shorter events, 1.7 us)
Async XLA Ops:
  7.2 55.0 %copy-start = (bf16[1,384,1024]{2,1,0:T(8,128)(2,1)S(1)}, bf16[1,384,1024]{2,1,0:T(8,128)(2,1)}, u32[]{:S(2)}) copy-start(bf16[1,384,1024]{2,1,0:T(8,128)(2,1)} %param.14) | copy-start | bytes 2359300
  7.2 15.1 %copy-start.6 = (bf16[1,240,1024]{2,1,0:T(8,128)(2,1)S(1)}, bf16[1,240,1024]{2,1,0:T(8,128)(2,1)}, u32[]{:S(2)}) copy-start(bf16[1,240,1024]{2,1,0:T(8,128)(2,1)} %param.11) | copy-start | bytes 1474564
  9.0 15.4 %all-to-all-start = ((bf16[4,1,1]{2,1,0:T(2,128)(2,1)}), bf16[4,1,1]{2,1,0:T(2,128)(2,1)S(1)}, u32[]{:S(2)}, u32[]{:S(2)}) async-start(bf16[4,1,1]{2,1,0:T(2,128)(2,1)} %copy.51), calls=%async_computation | async-start | bytes 4096 | tf_op jit(solution)/shard_map/all_to_all | solution.py:71
  23.5 6.1 %copy-start.7 = (bf16[1,240,1024]{2,1,0:T(8,128)(2,1)S(1)}, bf16[1,240,1024]{2,1,0:T(8,128)(2,1)}, u32[]{:S(2)}) copy-start(bf16[1,240,1024]{2,1,0:T(8,128)(2,1)} %param.10) | copy-start | bytes 1474564
  24.4 19.0 %all-to-all-start.1 = ((bf16[4,60,1024]{2,1,0:T(8,128)(2,1)}), bf16[4,60,1024]{2,1,0:T(8,128)(2,1)S(1)}, u32[]{:S(2)}, u32[]{:S(2)}) async-start(bf16[4,60,1024]{2,1,0:T(8,128)(2,1)} %select_convert_fusion), calls=%async_computation.1 | async-start | bytes 1048576 | tf_op jit(solution)/shard_map/all_to_all | solution.py:70
  43.5 17.4 %all-to-all-start.2 = ((bf16[4,60,1024]{2,1,0:T(8,128)(2,1)}), bf16[4,60,1024]{2,1,0:T(8,128)(2,1)S(1)}, u32[]{:S(2)}, u32[]{:S(2)}) async-start(bf16[4,60,1024]{2,1,0:T(8,128)(2,1)} %broadcast_select_fusion), calls=%async_computation.2 | async-start | bytes 1048576 | tf_op jit(solution)/shard_map/all_to_all | solution.py:69
  46.9 65.5 %all-reduce.4.cloned.1.call-start = ((), (), s32[]{:S(2)}) async-start(), calls=%async_computation.3 | async-start | bytes 1179648 | tf_op jit(solution)/shard_map/psum | solution.py:109
  62.1 1.1 copy-start.9
  62.1 1.6 %copy-start.10 = (bf16[1,384,1024]{2,1,0:T(8,128)(2,1)S(1)}, bf16[1,384,1024]{2,1,0:T(8,128)(2,1)}, u32[]{:S(2)}) copy-start(bf16[1,384,1024]{2,1,0:T(8,128)(2,1)} %param.16) | copy-start | bytes 2359300
  72.0 2.0 %copy-start.1 = (f32[384,1024]{1,0:T(8,128)S(1)}, f32[384,1024]{1,0:T(8,128)}, u32[]{:S(2)}) copy-start(f32[384,1024]{1,0:T(8,128)} %get-tuple-element.299) | copy-start | bytes 4718596 | tf_op jit(solution)/shard_map/while
  72.0 2.4 %copy-start.4 = (f32[384,1024]{1,0:T(8,128)S(1)}, f32[384,1024]{1,0:T(8,128)}, u32[]{:S(2)}) copy-start(f32[384,1024]{1,0:T(8,128)} %get-tuple-element.312) | copy-start | bytes 4718596 | tf_op jit(solution)/shard_map/while
  74.4 1.4 %copy-start.5 = (f32[384,1024]{1,0:T(8,128)S(1)}, f32[384,1024]{1,0:T(8,128)}, u32[]{:S(2)}) copy-start(f32[384,1024]{1,0:T(8,128)} %get-tuple-element.313) | copy-start | bytes 4718596 | tf_op jit(solution)/shard_map/while
  74.9 3.7 %copy-start.2 = (f32[384,1024]{1,0:T(8,128)}, f32[384,1024]{1,0:T(8,128)S(1)}, u32[]{:S(2)}) copy-start(f32[384,1024]{1,0:T(8,128)S(1)} %add.128) | copy-start | bytes 4718596 | tf_op jit(solution)/shard_map/while
  114.4 2.5 %copy-start.3 = (f32[384,1024]{1,0:T(8,128)S(1)}, f32[384,1024]{1,0:T(8,128)}, u32[]{:S(2)}) copy-start(f32[384,1024]{1,0:T(8,128)} %get-tuple-element.237) | copy-start | bytes 4718596
  117.0 1.0 copy-start.8
Sparse Core Ops, SparseCore 0:
  82.8 29.5 all-reduce.3
where the time goes:
time: 128 us; the launch traced here: 127 us
  waiting for transfers between devices  49.8 us (39%)
  other arithmetic  19.9 us (16%)
  local copies, waits for them, and re-layouts  18.8 us (15%)
  between operations  17.3 us (14%)
  starting transfers between devices  14.9 us (12%)
  matrix products  6.34 us (5%)
    psum x1, waiting for transfers between devices, per_device(): lax.psum(for_sending(pieces), 'replica')  29.1 us
    all_to_all x1, waiting for transfers between devices, per_device(): lax.all_to_all(rows_x, 'expert', split_axis=0, concat_axis=0, tiled=True)  11.3 us
    all_to_all x1, waiting for transfers between devices, per_device(): lax.all_to_all(rows_q, 'expert', split_axis=0, concat_axis=0, tiled=True)  9.41 us
    dot_general x6, matrix products, contract(): lax.dot_general(left, right, (((left_dim,), (right_dim,)), ((), ())), pre...  6.34 us
    all_to_all x1, starting transfers between devices, per_device(): lax.all_to_all(sent_counts, 'expert', split_axis=0, concat_axis=0, tiled=...  6.32 us
    all_to_all x1, starting transfers between devices, per_device(): lax.all_to_all(rows_q, 'expert', split_axis=0, concat_axis=0, tiled=True)  5.09 us
    broadcast_in_dim x3, other arithmetic, per_device(): lax.dynamic_update_slice_in_dim(grad_full, piece / replicas, begin, 1)  4.53 us
    convert_element_type x3, local copies, waits for them, and re-layouts, short(): return part.astype(jnp.bfloat16) if part.dtype == jnp.float32 else part  4.09 us
  transfers between devices with their start and end apart: 4, of which 3 were waited for; matrix products, arithmetic and copies ran while one was open for 12% of the time, Pallas kernels for 0%

commit v1 on v0

v1 whole, which is shorter than its diff:
```python
import functools

import jax
import jax.numpy as jnp
from jax import lax
from jax.experimental import pallas as pl
from jax.experimental.pallas import tpu as pltpu
from jax.sharding import PartitionSpec as P

FRAGS = 4
CAP = 60
SLOTS = 64
F32 = jnp.float32
BF16 = jnp.bfloat16
VMEM = pl.BlockSpec(memory_space=pltpu.VMEM)
SMEM = pl.BlockSpec(memory_space=pltpu.SMEM)
ANY = pl.BlockSpec(memory_space=pl.ANY)


def dot(left, right, left_dim=1, right_dim=0):
    return lax.dot_general(
        left, right, (((left_dim,), (right_dim,)), ((), ())), preferred_element_type=F32
    )


def swap_to_lanes(eye, array):
    return dot(eye, array, 1, 1)


def pack_kernel(experts, tok_ref, grad_ref, ids_ref, weight_ref, *out_refs):
    me = lax.axis_index("expert")
    first = lax.axis_index("tensor") == 0
    tokens, top = ids_ref.shape
    eye = (
        lax.broadcasted_iota(jnp.int32, (top, top), 0)
        == lax.broadcasted_iota(jnp.int32, (top, top), 1)
    ).astype(F32).astype(BF16)
    ids = swap_to_lanes(eye, ids_ref[...].astype(F32).astype(BF16))
    weight = weight_ref[...]
    high = weight.astype(BF16)
    rest = weight - high.astype(F32)
    middle = rest.astype(BF16)
    low = (rest - middle.astype(F32)).astype(BF16)
    weight = (swap_to_lanes(eye, high) + swap_to_lanes(eye, middle)) + swap_to_lanes(eye, low)
    members, weights = [], []
    for step in range(experts):
        expert = lax.rem(me + step, experts).astype(F32)
        match = ids == expert
        members.append(jnp.max(jnp.where(match, 1.0, 0.0), axis=0, keepdims=True))
        weights.append(jnp.sum(jnp.where(match, weight, 0.0), axis=0, keepdims=True))
    member = jnp.concatenate(members, axis=0)
    earlier = (
        lax.broadcasted_iota(jnp.int32, (tokens, tokens), 0)
        < lax.broadcasted_iota(jnp.int32, (tokens, tokens), 1)
    ).astype(F32).astype(BF16)
    position = dot(member.astype(BF16), earlier)
    slot = lax.broadcasted_iota(jnp.int32, (SLOTS, tokens), 0).astype(F32)
    rows = lax.broadcasted_iota(jnp.int32, (SLOTS, 1), 0)
    source = jnp.where(first, tok_ref[...], grad_ref[...])
    for step in range(experts):
        hit = (slot == position[step : step + 1, :]) & (member[step : step + 1, :] > 0.5)
        pick = jnp.where(hit, 1.0, 0.0)
        scale = jnp.sum(pick * weights[step], axis=1, keepdims=True)
        scale = jnp.where(first, 1.0, scale)
        packed = dot(pick.astype(BF16), source) * scale
        count = jnp.sum(members[step], axis=1, keepdims=True)
        packed = jnp.where((rows == CAP) & first, count, packed)
        out_refs[step][...] = packed.astype(BF16)


def pack(experts, tokens, out_grad, ids, weight):
    width = tokens.shape[1]
    return pl.pallas_call(
        functools.partial(pack_kernel, experts),
        out_shape=[jax.ShapeDtypeStruct((SLOTS, width), BF16)] * experts,
        in_specs=[VMEM] * 4,
        out_specs=[VMEM] * experts,
        name="pack",
    )(tokens, out_grad, ids, weight)


def join(mine, theirs, x_rows, q_rows):
    first = lax.axis_index("tensor") == 0
    for step, (here, there) in enumerate(zip(mine, theirs)):
        place = pl.ds(step * SLOTS, SLOTS)
        x_rows[place, :] = jnp.where(first, here[...], there[...])
        q_rows[place, :] = jnp.where(first, there[...], here[...])


def activations(x_rows, q_rows, w_gate, w_up, w_down):
    gate_pre = dot(w_gate[...], x_rows[...], 1, 1)
    up_pre = dot(w_up[...], x_rows[...], 1, 1)
    hidden_grad = dot(w_down[...], q_rows[...], 1, 1)
    gate_sig = jax.nn.sigmoid(gate_pre)
    gate_act = gate_pre * gate_sig
    hidden = (gate_act * up_pre).astype(BF16)
    gate_grad = (hidden_grad * up_pre * gate_sig * (1.0 + gate_pre * (1.0 - gate_sig))).astype(BF16)
    up_grad = (hidden_grad * gate_act).astype(BF16)
    return gate_grad, up_grad, hidden


def own_kernel(experts, frag_ref, *refs):
    mine, theirs = refs[:experts], refs[experts : 2 * experts]
    w_gate, w_up, w_down = refs[2 * experts : 2 * experts + 3]
    outs = refs[2 * experts + 3 : 2 * experts + 6]
    frag_out, load_out, x_rows, q_rows = refs[2 * experts + 6 :]
    join(mine, theirs, x_rows, q_rows)
    total = jnp.zeros((1, 128), F32)
    for step in range(experts):
        total += x_rows[pl.ds(step * SLOTS + CAP, 1), pl.ds(0, 128)].astype(F32)
    load_out[...] = total / (experts * CAP)
    acts = activations(x_rows, q_rows, w_gate, w_up, w_down)
    frag = frag_ref[0]
    cut = frag_out.shape[2]
    for piece, (act, rows, out) in enumerate(zip(acts, (x_rows, x_rows, q_rows), outs)):
        for at in range(FRAGS):
            columns = pl.ds(at * cut, cut)
            grad = dot(act, rows[:, columns])
            out[:, columns] = grad.astype(BF16)

            @pl.when(frag == at)
            def _():
                frag_out[piece] = grad


def own(experts, fragment, mine, theirs, weights):
    units, width = weights[0].shape
    cut = width // FRAGS
    return pl.pallas_call(
        functools.partial(own_kernel, experts),
        out_shape=[jax.ShapeDtypeStruct((units, width), BF16)] * 3
        + [jax.ShapeDtypeStruct((3, units, cut), F32), jax.ShapeDtypeStruct((1, 128), F32)],
        in_specs=[SMEM] + [VMEM] * (2 * experts + 3),
        out_specs=[VMEM] * 5,
        scratch_shapes=[pltpu.VMEM((experts * SLOTS, width), BF16)] * 2,
        name="own",
    )(fragment, *mine, *theirs, *weights)


def other_kernel(experts, frag_ref, *refs):
    mine, theirs = refs[:experts], refs[experts : 2 * experts]
    w_gate, w_up, w_down = refs[2 * experts : 2 * experts + 3]
    frag_in = refs[2 * experts + 3]
    outs = refs[2 * experts + 7 : 2 * experts + 10]
    x_rows, q_rows, cuts, sems = refs[2 * experts + 10 :]
    join(mine, theirs, x_rows, q_rows)
    acts = activations(x_rows, q_rows, w_gate, w_up, w_down)
    cut = frag_in.shape[2]
    columns = pl.ds(pl.multiple_of(frag_ref[0] * cut, cut), cut)
    copies = []
    for piece, (act, rows) in enumerate(zip(acts, (x_rows, x_rows, q_rows))):
        grad = dot(act, rows[:, columns])
        cuts[piece] = ((frag_in[piece] + grad) * 0.5).astype(BF16)
        copies.append(
            pltpu.make_async_copy(cuts.at[piece], outs[piece].at[:, columns], sems.at[piece])
        )
        copies[-1].start()
    for copy in copies:
        copy.wait()


def other(experts, fragment, mine, theirs, weights, frag_grad, grads):
    units, width = weights[0].shape
    cut = width // FRAGS
    at = 1 + 2 * experts + 4
    return pl.pallas_call(
        functools.partial(other_kernel, experts),
        out_shape=[jax.ShapeDtypeStruct((units, width), BF16)] * 3,
        in_specs=[SMEM] + [VMEM] * (2 * experts + 4) + [ANY] * 3,
        out_specs=[ANY] * 3,
        scratch_shapes=[pltpu.VMEM((experts * SLOTS, width), BF16)] * 2
        + [pltpu.VMEM((3, units, cut), BF16), pltpu.SemaphoreType.DMA((3,))],
        input_output_aliases={at: 0, at + 1: 1, at + 2: 2},
        name="other",
    )(fragment, *mine, *theirs, *weights, frag_grad, *grads)


def shift(axis, step):
    size = lax.axis_size(axis)
    return [(index, (index + step) % size) for index in range(size)]


def send(array, axis, step):
    return lax.ppermute(array, axis, shift(axis, step))


def per_device(tokens, out_grad, expert_ids, route_weight, gate_proj, up_proj, down_proj, fragment):
    experts = lax.axis_size("expert")
    replicas = lax.axis_size("replica")
    weights = (gate_proj[0], up_proj[0], down_proj[0])
    packed = pack(experts, tokens[0], out_grad[0], expert_ids[0], route_weight[0])
    mine = [packed[0]] + [send(packed[step], "expert", step) for step in range(1, experts)]
    theirs = [send(rows, "tensor", 1) for rows in mine]
    *grads, frag_grad, load = own(experts, fragment, mine, theirs, weights)
    if replicas == 2:
        far = [send(rows, "replica", 1) for rows in mine]
        far_theirs = [send(rows, "tensor", 1) for rows in far]
        grads = other(experts, fragment, far, far_theirs, weights, frag_grad, grads)
    else:
        synced = lax.psum(frag_grad.astype(BF16), "replica").astype(F32)
        begin = fragment[0] * (weights[0].shape[1] // FRAGS)
        grads = [
            lax.dynamic_update_slice_in_dim(grad, (piece / replicas).astype(BF16), begin, 1)
            for grad, piece in zip(grads, synced)
        ]
    return tuple(grad[None, None] for grad in grads) + (load[:, :1],)


def solution(mesh):
    rows = P(("group", "replica"), "expert", None)
    units = P("expert", "tensor", None)
    grad = P(("group", "replica"), "expert", "tensor", None)
    return jax.shard_map(
        per_device,
        mesh=mesh,
        in_specs=(rows, rows, rows, rows, units, units, units, P("group")),
        out_specs=(grad, grad, grad, P(("group", "replica"), "expert")),
        check_vma=False,
    )
```

time: 128 us -> 46.5 us (0.36)
  waiting for transfers between devices: 49.8 us -> 12.8 us
  other arithmetic: 19.9 us -> 0 us
  between operations: 17.3 us -> 1.48 us
  Pallas kernels: 0 us -> 15 us
  local copies, waits for them, and re-layouts: 18.8 us -> 4.31 us
  matrix products: 6.34 us -> 0 us
  starting transfers between devices: 14.9 us -> 12.6 us
    psum x1 -> x0, waiting for transfers between devices: 29.1 us -> none  [per_device(): lax.psum(for_sending(pieces), 'replica')]
    all_to_all x3 -> x0, waiting for transfers between devices: 20.7 us -> none  [the longest x1 11.3 us: per_device(): lax.all_to_all(rows_x, 'expert', split_axis=0, concat_axis=0, tiled=True)]
    pallas_call x0 -> x3, Pallas kernels: none -> 15 us  [the longest x1 7.82 us: own(): pl.pallas_call(functools.partial(own_kernel, experts), out_shape=[jax.Sha...]
    all_to_all x3 -> x0, starting transfers between devices: 14.9 us -> none  [the longest x1 6.32 us: per_device(): lax.all_to_all(sent_counts, 'expert', split_axis=0, concat_axis=0, tiled=...]
    ppermute x0 -> x15, waiting for transfers between devices: none -> 12.8 us  [send(): return lax.ppermute(array, axis, shift(axis, step))]
    ppermute x0 -> x15, starting transfers between devices: none -> 12.6 us  [send(): return lax.ppermute(array, axis, shift(axis, step))]
    gather x8 -> x0, local copies, waits for them, and re-layouts: 7.62 us -> none  [the longest x3 3 us: per_device(): chosen_weight = jnp.take_along_axis(token_weight.T, source_row, axis=1)]
    dot_general x6 -> x0, matrix products: 6.34 us -> none  [contract(): lax.dot_general(left, right, (((left_dim,), (right_dim,)), ((), ())), pre...]
  transfers between devices with their start and end apart: 4 -> 15, of which waited for: 3 -> 5; matrix products, arithmetic and copies ran while one was open for 12% -> 0% of each run, Pallas kernels for 0% -> 17%
where the time goes in v1:
time: 46.5 us; the launch traced here: 46.2 us
  Pallas kernels  15 us (32%)
  waiting for transfers between devices  12.8 us (28%)
  starting transfers between devices  12.6 us (27%)
  local copies, waits for them, and re-layouts  4.31 us (9%)
  between operations  1.48 us (3%)
    ppermute x15, waiting for transfers between devices, send(): return lax.ppermute(array, axis, shift(axis, step))  12.8 us
    ppermute x15, starting transfers between devices, send(): return lax.ppermute(array, axis, shift(axis, step))  12.6 us
    pallas_call x1, Pallas kernels, own(): pl.pallas_call(functools.partial(own_kernel, experts), out_shape=[jax.Sha...  7.82 us
    pallas_call x1, Pallas kernels, other(): pl.pallas_call(functools.partial(other_kernel, experts), out_shape=[jax.S...  4.51 us
    unnamed x32, local copies, waits for them, and re-layouts  4.31 us
    pallas_call x1, Pallas kernels, pack(): pl.pallas_call(functools.partial(pack_kernel, experts), out_shape=[jax.Sh...  2.7 us
  transfers between devices with their start and end apart: 15, of which 5 were waited for; matrix products, arithmetic and copies ran while one was open for 0% of the time, Pallas kernels for 17%

profile of v1, /device:TPU:0, one launch (start us, length us, event | category | flops | bytes accessed | tf_op | source)
XLA Modules:
  0.0 46.2 jit_solution(13079252121547606805)
XLA Ops:
  0.6 1.5 %copy.15 = s32[1,240,8]{2,1,0:T(8,128)} copy(s32[1,240,8]{1,2,0:T(8,128)} %param.10) | data formatting | bytes 15360 | tf_op args[2]
  2.1 1.5 %copy.16 = f32[1,240,8]{2,1,0:T(8,128)} copy(f32[1,240,8]{1,2,0:T(8,128)} %param.11) | data formatting | bytes 15360 | tf_op args[3]
  3.6 2.7 %pack.1 = (bf16[64,1024]{1,0:T(8,128)(2,1)}, bf16[64,1024]{1,0:T(8,128)(2,1)}, bf16[64,1024]{1,0:T(8,128)(2,1)}, bf16[64,1024]{1,0:T(8,128)(2,1)}) custom-call(bf16[240,1024]{1,0:T(8,128)(2,1)} %bitcast.20, bf16[240,1024]{1,0:T(8,128)(2,1)} %bitcast.21, s32[240,8]{1,0:T(8,128)} %bitcast.22, f32[240,8]{1,0:T(8,128)} %bitcast.23), custom_call_target="tpu_custom_call" | custom-call | tf_op jit(solution)/shard_map/pack/pallas_call | solution.py:73
  6.3 3.0 %collective-permute-start.1 = (bf16[64,1024]{1,0:T(8,128)(2,1)}, bf16[64,1024]{1,0:T(8,128)(2,1)S(1)}, u32[]{:S(2)}, u32[]{:S(2)}) collective-permute-start(bf16[64,1024]{1,0:T(8,128)(2,1)} %get-tuple-element.17), channel_id=1, source_target_pairs={{0,4},{4,8},{8,12},{12,0},{1,5},{5,9},{9,13},{13,1},{2,6},{6,10},{... | collective-permute-start | bytes 393224 | tf_op jit(solution)/shard_map/ppermute | solution.py:184
  9.3 2.6 %collective-permute-start.3 = (bf16[64,1024]{1,0:T(8,128)(2,1)}, bf16[64,1024]{1,0:T(8,128)(2,1)S(1)}, u32[]{:S(2)}, u32[]{:S(2)}) collective-permute-start(bf16[64,1024]{1,0:T(8,128)(2,1)} %get-tuple-element.18), channel_id=1, source_target_pairs={{0,8},{4,12},{8,0},{12,4},{1,9},{5,13},{9,1},{13,5},{2,10},{6,14},... | collective-permute-start | bytes 393224 | tf_op jit(solution)/shard_map/ppermute | solution.py:184
  11.9 1.3 %collective-permute-start.5 = (bf16[64,1024]{1,0:T(8,128)(2,1)}, bf16[64,1024]{1,0:T(8,128)(2,1)S(1)}, u32[]{:S(2)}, u32[]{:S(2)}) collective-permute-start(bf16[64,1024]{1,0:T(8,128)(2,1)} %get-tuple-element.19), channel_id=1, source_target_pairs={{0,12},{4,0},{8,4},{12,8},{1,13},{5,1},{9,5},{13,9},{2,14},{6,2},{... | collective-permute-start | bytes 393224 | tf_op jit(solution)/shard_map/ppermute | solution.py:184
  13.2 0.0 collective-permute-start.11
  13.2 1.5 %collective-permute-start = (bf16[64,1024]{1,0:T(8,128)(2,1)}, bf16[64,1024]{1,0:T(8,128)(2,1)S(1)}, u32[]{:S(2)}, u32[]{:S(2)}) collective-permute-start(bf16[64,1024]{1,0:T(8,128)(2,1)} %get-tuple-element.16.refs_0_), channel_id=1, source_target_pairs={{0,2},{2,0},{1,3},{3,1},{4,6},{6,4},{5,7},{7,5},{8,10},{10,8},{9,1... | collective-permute-start | bytes 393224 | tf_op jit(solution)/shard_map/ppermute | solution.py:184
  14.7 1.2 %collective-permute-done.1.refs_1_ = bf16[64,1024]{1,0:T(8,128)(2,1)S(1)} collective-permute-done((bf16[64,1024]{1,0:T(8,128)(2,1)}, bf16[64,1024]{1,0:T(8,128)(2,1)S(1)}, u32[]{:S(2)}, u32[]{:S(2)}) %collective-permute-start.1) | collective-permute-done | bytes 131104 | tf_op jit(solution)/shard_map/ppermute | solution.py:184
  16.0 0.0 collective-permute-start.12
  16.0 4.8 %collective-permute-done.3.refs_2_ = bf16[64,1024]{1,0:T(8,128)(2,1)S(1)} collective-permute-done((bf16[64,1024]{1,0:T(8,128)(2,1)}, bf16[64,1024]{1,0:T(8,128)(2,1)S(1)}, u32[]{:S(2)}, u32[]{:S(2)}) %collective-permute-start.3) | collective-permute-done | bytes 131104 | tf_op jit(solution)/shard_map/ppermute | solution.py:184
  20.7 1.5 %collective-permute-start.2 = (bf16[64,1024]{1,0:T(8,128)(2,1)S(1)}, bf16[64,1024]{1,0:T(8,128)(2,1)S(1)}, u32[]{:S(2)}, u32[]{:S(2)}) collective-permute-start(bf16[64,1024]{1,0:T(8,128)(2,1)S(1)} %collective-permute-done.1.refs_1_), channel_id=1, source_target_pairs={{0,2},{2,0},{1,3},{3,1},{4,6},{6,4},{5,7},{7,5},{8,10},{10,8},{9,1... | collective-permute-start | bytes 393224 | tf_op jit(solution)/shard_map/ppermute | solution.py:184
  22.2 0.0 collective-permute-done.5.refs_3_
  22.2 0.0 collective-permute-start.13
  22.2 0.0 collective-permute-done.11.refs_4_
  22.3 0.0 copy-start.5
  22.3 0.6 %collective-permute-start.4 = (bf16[64,1024]{1,0:T(8,128)(2,1)S(1)}, bf16[64,1024]{1,0:T(8,128)(2,1)S(1)}, u32[]{:S(2)}, u32[]{:S(2)}) collective-permute-start(bf16[64,1024]{1,0:T(8,128)(2,1)S(1)} %collective-permute-done.3.refs_2_), channel_id=1, source_target_pairs={{0,2},{2,0},{1,3},{3,1},{4,6},{6,4},{5,7},{7,5},{8,10},{10,8},{9,1... | collective-permute-start | bytes 393224 | tf_op jit(solution)/shard_map/ppermute | solution.py:184
  22.9 0.0 collective-permute-done.refs_0_
  22.9 1.5 %collective-permute-start.6 = (bf16[64,1024]{1,0:T(8,128)(2,1)S(1)}, bf16[64,1024]{1,0:T(8,128)(2,1)S(1)}, u32[]{:S(2)}, u32[]{:S(2)}) collective-permute-start(bf16[64,1024]{1,0:T(8,128)(2,1)S(1)} %collective-permute-done.5.refs_3_), channel_id=1, source_target_pairs={{0,2},{2,0},{1,3},{3,1},{4,6},{6,4},{5,7},{7,5},{8,10},{10,8},{9,1... | collective-permute-start | bytes 393224 | tf_op jit(solution)/shard_map/ppermute | solution.py:184
  24.4 0.0 collective-permute-done.12.refs_5_
  24.4 0.0 collective-permute-start.14
  24.4 2.4 %collective-permute-done.2.refs_1_ = bf16[64,1024]{1,0:T(8,128)(2,1)S(1)} collective-permute-done((bf16[64,1024]{1,0:T(8,128)(2,1)S(1)}, bf16[64,1024]{1,0:T(8,128)(2,1)S(1)}, u32[]{:S(2)}, u32[]{:S(2)}) %collective-permute-start.2) | collective-permute-done | bytes 131104 | tf_op jit(solution)/shard_map/ppermute | solution.py:184
  26.8 0.0 collective-permute-start.7
  26.8 0.0 collective-permute-done.13.refs_6_
  26.8 0.0 copy-start.9
  26.8 0.5 %collective-permute-start.8 = (bf16[64,1024]{1,0:T(8,128)(2,1)S(1)}, bf16[64,1024]{1,0:T(8,128)(2,1)S(1)}, u32[]{:S(2)}, u32[]{:S(2)}) collective-permute-start(bf16[64,1024]{1,0:T(8,128)(2,1)S(1)} %collective-permute-done.2.refs_1_), channel_id=1, source_target_pairs={{0,1},{1,0},{2,3},{3,2},{4,5},{5,4},{6,7},{7,6},{8,9},{9,8},{10,11... | collective-permute-start | bytes 393224 | tf_op jit(solution)/shard_map/ppermute | solution.py:184
  27.3 2.3 %collective-permute-done.4.refs_2_ = bf16[64,1024]{1,0:T(8,128)(2,1)S(1)} collective-permute-done((bf16[64,1024]{1,0:T(8,128)(2,1)S(1)}, bf16[64,1024]{1,0:T(8,128)(2,1)S(1)}, u32[]{:S(2)}, u32[]{:S(2)}) %collective-permute-start.4) | collective-permute-done | bytes 131104 | tf_op jit(solution)/shard_map/ppermute | solution.py:184
  29.6 0.0 collective-permute-start.9
  29.6 2.1 %collective-permute-done.6.refs_3_ = bf16[64,1024]{1,0:T(8,128)(2,1)S(1)} collective-permute-done((bf16[64,1024]{1,0:T(8,128)(2,1)S(1)}, bf16[64,1024]{1,0:T(8,128)(2,1)S(1)}, u32[]{:S(2)}, u32[]{:S(2)}) %collective-permute-start.6) | collective-permute-done | bytes 131104 | tf_op jit(solution)/shard_map/ppermute | solution.py:184
  31.7 0.0 collective-permute-start.10
  32.3 0.0 collective-permute-done.14.refs_7_
  32.4 0.0 copy-start.13
  32.4 0.0 copy-done.1
  32.4 0.0 copy-done.2
  32.4 0.0 copy-done.3
  32.4 0.6 %copy-done.13 = bf16[64,1024]{1,0:T(8,128)(2,1)} copy-done((bf16[64,1024]{1,0:T(8,128)(2,1)}, bf16[64,1024]{1,0:T(8,128)(2,1)S(1)}, u32[]{:S(2)}) %copy-start.13) | copy-done | bytes 131096
  33.0 7.8 %own.1 = (bf16[384,1024]{1,0:T(8,128)(2,1)}, bf16[384,1024]{1,0:T(8,128)(2,1)}, bf16[384,1024]{1,0:T(8,128)(2,1)}, f32[3,384,256]{2,1,0:T(8,128)}, f32[1,128]{1,0:T(1,128)}) custom-call(s32[1]{0:T(128)S(6)} %copy.20.frag_ref, bf16[64,1024]{1,0:T(8,128)(2,1)} %get-tuple-element.16.refs_0_, bf16[64,1024]{1,0:T(8,128)(2,1)} %copy-done.1, ...), custom_call_target="tpu_custom_call" | custom-call | tf_op jit(solution)/shard_map/own/pallas_call | solution.py:129
  40.8 0.0 copy-done.4
  40.9 0.0 collective-permute-done.7.refs_4_
  40.9 0.0 collective-permute-done.8.refs_5_
  40.9 0.0 copy-start.11
  40.9 0.0 collective-permute-done.9.refs_6_
  40.9 0.0 collective-permute-done.10.refs_7_
  40.9 0.6 %copy-done.10 = bf16[64,1024]{1,0:T(8,128)(2,1)} copy-done((bf16[64,1024]{1,0:T(8,128)(2,1)}, bf16[64,1024]{1,0:T(8,128)(2,1)S(1)}, u32[]{:S(2)}) %copy-start.10) | copy-done | bytes 131096
  41.5 0.1 copy-done.11
  41.6 0.1 copy-done.12
  41.6 0.1 copy-done.14
  41.7 4.5 %other.1 = (bf16[384,1024]{1,0:T(8,128)(2,1)}, bf16[384,1024]{1,0:T(8,128)(2,1)}, bf16[384,1024]{1,0:T(8,128)(2,1)}) custom-call(s32[1]{0:T(128)S(6)} %copy.20.frag_ref, bf16[64,1024]{1,0:T(8,128)(2,1)} %copy-done, bf16[64,1024]{1,0:T(8,128)(2,1)} %copy-done.4, ...), custom_call_target="tpu_custom_call", output_to_operand_aliasing={{0}: (13, {}), {1}: (14, {}), {2}: (15, {})} | custom-call | tf_op jit(solution)/shard_map/other/pallas_call | solution.py:166
  (17 shorter events, 0.0 us)
Async XLA Ops:
  6.3 9.7 %collective-permute-start.1 = (bf16[64,1024]{1,0:T(8,128)(2,1)}, bf16[64,1024]{1,0:T(8,128)(2,1)S(1)}, u32[]{:S(2)}, u32[]{:S(2)}) collective-permute-start(bf16[64,1024]{1,0:T(8,128)(2,1)} %get-tuple-element.17), channel_id=1, source_target_pairs={{0,4},{4,8},{8,12},{12,0},{1,5},{5,9},{9,13},{13,1},{2,6},{6,10},{... | collective-permute-start | bytes 393224 | tf_op jit(solution)/shard_map/ppermute | solution.py:184
  9.3 11.4 %collective-permute-start.3 = (bf16[64,1024]{1,0:T(8,128)(2,1)}, bf16[64,1024]{1,0:T(8,128)(2,1)S(1)}, u32[]{:S(2)}, u32[]{:S(2)}) collective-permute-start(bf16[64,1024]{1,0:T(8,128)(2,1)} %get-tuple-element.18), channel_id=1, source_target_pairs={{0,8},{4,12},{8,0},{12,4},{1,9},{5,13},{9,1},{13,5},{2,10},{6,14},... | collective-permute-start | bytes 393224 | tf_op jit(solution)/shard_map/ppermute | solution.py:184
  11.9 10.3 %collective-permute-start.5 = (bf16[64,1024]{1,0:T(8,128)(2,1)}, bf16[64,1024]{1,0:T(8,128)(2,1)S(1)}, u32[]{:S(2)}, u32[]{:S(2)}) collective-permute-start(bf16[64,1024]{1,0:T(8,128)(2,1)} %get-tuple-element.19), channel_id=1, source_target_pairs={{0,12},{4,0},{8,4},{12,8},{1,13},{5,1},{9,5},{13,9},{2,14},{6,2},{... | collective-permute-start | bytes 393224 | tf_op jit(solution)/shard_map/ppermute | solution.py:184
  13.2 9.0 %collective-permute-start.11 = (bf16[64,1024]{1,0:T(8,128)(2,1)}, bf16[64,1024]{1,0:T(8,128)(2,1)S(1)}, u32[]{:S(2)}, u32[]{:S(2)}) collective-permute-start(bf16[64,1024]{1,0:T(8,128)(2,1)} %get-tuple-element.16.refs_0_), channel_id=1, source_target_pairs={{0,1},{1,0},{2,3},{3,2},{4,5},{5,4},{6,7},{7,6},{8,9},{9,8},{10,11... | collective-permute-start | bytes 393224 | tf_op jit(solution)/shard_map/ppermute | solution.py:184
  13.2 9.6 %collective-permute-start = (bf16[64,1024]{1,0:T(8,128)(2,1)}, bf16[64,1024]{1,0:T(8,128)(2,1)S(1)}, u32[]{:S(2)}, u32[]{:S(2)}) collective-permute-start(bf16[64,1024]{1,0:T(8,128)(2,1)} %get-tuple-element.16.refs_0_), channel_id=1, source_target_pairs={{0,2},{2,0},{1,3},{3,1},{4,6},{6,4},{5,7},{7,5},{8,10},{10,8},{9,1... | collective-permute-start | bytes 393224 | tf_op jit(solution)/shard_map/ppermute | solution.py:184
  16.0 16.4 %copy-start.1 = (bf16[64,1024]{1,0:T(8,128)(2,1)}, bf16[64,1024]{1,0:T(8,128)(2,1)S(1)}, u32[]{:S(2)}) copy-start(bf16[64,1024]{1,0:T(8,128)(2,1)S(1)} %collective-permute-done.1.refs_1_) | copy-start | bytes 393220
  16.0 8.4 %collective-permute-start.12 = (bf16[64,1024]{1,0:T(8,128)(2,1)S(1)}, bf16[64,1024]{1,0:T(8,128)(2,1)S(1)}, u32[]{:S(2)}, u32[]{:S(2)}) collective-permute-start(bf16[64,1024]{1,0:T(8,128)(2,1)S(1)} %collective-permute-done.1.refs_1_), channel_id=1, source_target_pairs={{0,1},{1,0},{2,3},{3,2},{4,5},{5,4},{6,7},{7,6},{8,9},{9,8},{10,11... | collective-permute-start | bytes 393224 | tf_op jit(solution)/shard_map/ppermute | solution.py:184
  20.7 11.6 %copy-start.2 = (bf16[64,1024]{1,0:T(8,128)(2,1)}, bf16[64,1024]{1,0:T(8,128)(2,1)S(1)}, u32[]{:S(2)}) copy-start(bf16[64,1024]{1,0:T(8,128)(2,1)S(1)} %collective-permute-done.3.refs_2_) | copy-start | bytes 393220
  20.7 6.0 %collective-permute-start.2 = (bf16[64,1024]{1,0:T(8,128)(2,1)S(1)}, bf16[64,1024]{1,0:T(8,128)(2,1)S(1)}, u32[]{:S(2)}, u32[]{:S(2)}) collective-permute-start(bf16[64,1024]{1,0:T(8,128)(2,1)S(1)} %collective-permute-done.1.refs_1_), channel_id=1, source_target_pairs={{0,2},{2,0},{1,3},{3,1},{4,6},{6,4},{5,7},{7,5},{8,10},{10,8},{9,1... | collective-permute-start | bytes 393224 | tf_op jit(solution)/shard_map/ppermute | solution.py:184
  22.2 10.1 %copy-start.3 = (bf16[64,1024]{1,0:T(8,128)(2,1)}, bf16[64,1024]{1,0:T(8,128)(2,1)S(1)}, u32[]{:S(2)}) copy-start(bf16[64,1024]{1,0:T(8,128)(2,1)S(1)} %collective-permute-done.5.refs_3_) | copy-start | bytes 393220
  22.2 4.5 %collective-permute-start.13 = (bf16[64,1024]{1,0:T(8,128)(2,1)S(1)}, bf16[64,1024]{1,0:T(8,128)(2,1)S(1)}, u32[]{:S(2)}, u32[]{:S(2)}) collective-permute-start(bf16[64,1024]{1,0:T(8,128)(2,1)S(1)} %collective-permute-done.3.refs_2_), channel_id=1, source_target_pairs={{0,1},{1,0},{2,3},{3,2},{4,5},{5,4},{6,7},{7,6},{8,9},{9,8},{10,11... | collective-permute-start | bytes 393224 | tf_op jit(solution)/shard_map/ppermute | solution.py:184
  22.3 10.1 %copy-start.5 = (bf16[64,1024]{1,0:T(8,128)(2,1)}, bf16[64,1024]{1,0:T(8,128)(2,1)S(1)}, u32[]{:S(2)}) copy-start(bf16[64,1024]{1,0:T(8,128)(2,1)S(1)} %collective-permute-done.11.refs_4_) | copy-start | bytes 393220
  22.3 7.3 %collective-permute-start.4 = (bf16[64,1024]{1,0:T(8,128)(2,1)S(1)}, bf16[64,1024]{1,0:T(8,128)(2,1)S(1)}, u32[]{:S(2)}, u32[]{:S(2)}) collective-permute-start(bf16[64,1024]{1,0:T(8,128)(2,1)S(1)} %collective-permute-done.3.refs_2_), channel_id=1, source_target_pairs={{0,2},{2,0},{1,3},{3,1},{4,6},{6,4},{5,7},{7,5},{8,10},{10,8},{9,1... | collective-permute-start | bytes 393224 | tf_op jit(solution)/shard_map/ppermute | solution.py:184
  22.9 18.0 %copy-start = (bf16[64,1024]{1,0:T(8,128)(2,1)}, bf16[64,1024]{1,0:T(8,128)(2,1)S(1)}, u32[]{:S(2)}) copy-start(bf16[64,1024]{1,0:T(8,128)(2,1)S(1)} %collective-permute-done.refs_0_) | copy-start | bytes 393220
  22.9 8.8 %collective-permute-start.6 = (bf16[64,1024]{1,0:T(8,128)(2,1)S(1)}, bf16[64,1024]{1,0:T(8,128)(2,1)S(1)}, u32[]{:S(2)}, u32[]{:S(2)}) collective-permute-start(bf16[64,1024]{1,0:T(8,128)(2,1)S(1)} %collective-permute-done.5.refs_3_), channel_id=1, source_target_pairs={{0,2},{2,0},{1,3},{3,1},{4,6},{6,4},{5,7},{7,5},{8,10},{10,8},{9,1... | collective-permute-start | bytes 393224 | tf_op jit(solution)/shard_map/ppermute | solution.py:184
  24.4 8.0 %copy-start.6 = (bf16[64,1024]{1,0:T(8,128)(2,1)}, bf16[64,1024]{1,0:T(8,128)(2,1)S(1)}, u32[]{:S(2)}) copy-start(bf16[64,1024]{1,0:T(8,128)(2,1)S(1)} %collective-permute-done.12.refs_5_) | copy-start | bytes 393220
  24.4 8.0 %collective-permute-start.14 = (bf16[64,1024]{1,0:T(8,128)(2,1)S(1)}, bf16[64,1024]{1,0:T(8,128)(2,1)S(1)}, u32[]{:S(2)}, u32[]{:S(2)}) collective-permute-start(bf16[64,1024]{1,0:T(8,128)(2,1)S(1)} %collective-permute-done.5.refs_3_), channel_id=1, source_target_pairs={{0,1},{1,0},{2,3},{3,2},{4,5},{5,4},{6,7},{7,6},{8,9},{9,8},{10,11... | collective-permute-start | bytes 393224 | tf_op jit(solution)/shard_map/ppermute | solution.py:184
  26.8 14.1 %copy-start.4 = (bf16[64,1024]{1,0:T(8,128)(2,1)}, bf16[64,1024]{1,0:T(8,128)(2,1)S(1)}, u32[]{:S(2)}) copy-start(bf16[64,1024]{1,0:T(8,128)(2,1)S(1)} %collective-permute-done.2.refs_1_) | copy-start | bytes 393220
  26.8 14.1 %collective-permute-start.7 = (bf16[64,1024]{1,0:T(8,128)(2,1)S(1)}, bf16[64,1024]{1,0:T(8,128)(2,1)S(1)}, u32[]{:S(2)}, u32[]{:S(2)}) collective-permute-start(bf16[64,1024]{1,0:T(8,128)(2,1)S(1)} %collective-permute-done.refs_0_), channel_id=1, source_target_pairs={{0,1},{1,0},{2,3},{3,2},{4,5},{5,4},{6,7},{7,6},{8,9},{9,8},{10,11... | collective-permute-start | bytes 393224 | tf_op jit(solution)/shard_map/ppermute | solution.py:184
  26.8 5.6 %copy-start.9 = (bf16[64,1024]{1,0:T(8,128)(2,1)}, bf16[64,1024]{1,0:T(8,128)(2,1)S(1)}, u32[]{:S(2)}) copy-start(bf16[64,1024]{1,0:T(8,128)(2,1)S(1)} %collective-permute-done.13.refs_6_) | copy-start | bytes 393220
  26.8 14.1 %collective-permute-start.8 = (bf16[64,1024]{1,0:T(8,128)(2,1)S(1)}, bf16[64,1024]{1,0:T(8,128)(2,1)S(1)}, u32[]{:S(2)}, u32[]{:S(2)}) collective-permute-start(bf16[64,1024]{1,0:T(8,128)(2,1)S(1)} %collective-permute-done.2.refs_1_), channel_id=1, source_target_pairs={{0,1},{1,0},{2,3},{3,2},{4,5},{5,4},{6,7},{7,6},{8,9},{9,8},{10,11... | collective-permute-start | bytes 393224 | tf_op jit(solution)/shard_map/ppermute | solution.py:184
  29.6 11.3 %copy-start.7 = (bf16[64,1024]{1,0:T(8,128)(2,1)}, bf16[64,1024]{1,0:T(8,128)(2,1)S(1)}, u32[]{:S(2)}) copy-start(bf16[64,1024]{1,0:T(8,128)(2,1)S(1)} %collective-permute-done.4.refs_2_) | copy-start | bytes 393220
  29.6 11.3 %collective-permute-start.9 = (bf16[64,1024]{1,0:T(8,128)(2,1)S(1)}, bf16[64,1024]{1,0:T(8,128)(2,1)S(1)}, u32[]{:S(2)}, u32[]{:S(2)}) collective-permute-start(bf16[64,1024]{1,0:T(8,128)(2,1)S(1)} %collective-permute-done.4.refs_2_), channel_id=1, source_target_pairs={{0,1},{1,0},{2,3},{3,2},{4,5},{5,4},{6,7},{7,6},{8,9},{9,8},{10,11... | collective-permute-start | bytes 393224 | tf_op jit(solution)/shard_map/ppermute | solution.py:184
  31.7 9.2 %copy-start.8 = (bf16[64,1024]{1,0:T(8,128)(2,1)}, bf16[64,1024]{1,0:T(8,128)(2,1)S(1)}, u32[]{:S(2)}) copy-start(bf16[64,1024]{1,0:T(8,128)(2,1)S(1)} %collective-permute-done.6.refs_3_) | copy-start | bytes 393220
  31.7 9.2 %collective-permute-start.10 = (bf16[64,1024]{1,0:T(8,128)(2,1)S(1)}, bf16[64,1024]{1,0:T(8,128)(2,1)S(1)}, u32[]{:S(2)}, u32[]{:S(2)}) collective-permute-start(bf16[64,1024]{1,0:T(8,128)(2,1)S(1)} %collective-permute-done.6.refs_3_), channel_id=1, source_target_pairs={{0,1},{1,0},{2,3},{3,2},{4,5},{5,4},{6,7},{7,6},{8,9},{9,8},{10,11... | collective-permute-start | bytes 393224 | tf_op jit(solution)/shard_map/ppermute | solution.py:184
  32.4 0.6 %copy-start.13 = (bf16[64,1024]{1,0:T(8,128)(2,1)}, bf16[64,1024]{1,0:T(8,128)(2,1)S(1)}, u32[]{:S(2)}) copy-start(bf16[64,1024]{1,0:T(8,128)(2,1)S(1)} %collective-permute-done.14.refs_7_) | copy-start | bytes 393220
  40.9 0.7 %copy-start.10 = (bf16[64,1024]{1,0:T(8,128)(2,1)}, bf16[64,1024]{1,0:T(8,128)(2,1)S(1)}, u32[]{:S(2)}) copy-start(bf16[64,1024]{1,0:T(8,128)(2,1)S(1)} %collective-permute-done.7.refs_4_) | copy-start | bytes 393220
  40.9 0.7 %copy-start.11 = (bf16[64,1024]{1,0:T(8,128)(2,1)}, bf16[64,1024]{1,0:T(8,128)(2,1)S(1)}, u32[]{:S(2)}) copy-start(bf16[64,1024]{1,0:T(8,128)(2,1)S(1)} %collective-permute-done.8.refs_5_) | copy-start | bytes 393220
  40.9 0.7 %copy-start.12 = (bf16[64,1024]{1,0:T(8,128)(2,1)}, bf16[64,1024]{1,0:T(8,128)(2,1)S(1)}, u32[]{:S(2)}) copy-start(bf16[64,1024]{1,0:T(8,128)(2,1)S(1)} %collective-permute-done.9.refs_6_) | copy-start | bytes 393220
  40.9 0.8 %copy-start.14 = (bf16[64,1024]{1,0:T(8,128)(2,1)}, bf16[64,1024]{1,0:T(8,128)(2,1)S(1)}, u32[]{:S(2)}) copy-start(bf16[64,1024]{1,0:T(8,128)(2,1)S(1)} %collective-permute-done.10.refs_7_) | copy-start | bytes 393220

commit v2 on v1

--- a/solution.py
+++ b/solution.py
@@ -15,6 +15,7 @@
 VMEM = pl.BlockSpec(memory_space=pltpu.VMEM)
 SMEM = pl.BlockSpec(memory_space=pltpu.SMEM)
 ANY = pl.BlockSpec(memory_space=pl.ANY)
+HBM = pl.BlockSpec(memory_space=pltpu.HBM)
 
 
 def dot(left, right, left_dim=1, right_dim=0):
@@ -23,29 +24,48 @@
     )
 
 
-def swap_to_lanes(eye, array):
-    return dot(eye, array, 1, 1)
-
-
-def pack_kernel(experts, tok_ref, grad_ref, ids_ref, weight_ref, *out_refs):
+def peer(index, step, size):
+    return index ^ step if size & (size - 1) == 0 else (index + step) % size
+
+
+def pack_kernel(experts, parts, tok_hbm, grad_hbm, ids_hbm, weight_hbm, *refs):
+    out_refs, (source_ref, ids_ref, weight_ref, sems) = refs[:experts], refs[experts:]
     me = lax.axis_index("expert")
     first = lax.axis_index("tensor") == 0
-    tokens, top = ids_ref.shape
-    eye = (
-        lax.broadcasted_iota(jnp.int32, (top, top), 0)
-        == lax.broadcasted_iota(jnp.int32, (top, top), 1)
-    ).astype(F32).astype(BF16)
-    ids = swap_to_lanes(eye, ids_ref[...].astype(F32).astype(BF16))
+    tokens = ids_ref.shape[1]
+    ids_copy = pltpu.make_async_copy(ids_hbm, ids_ref, sems.at[parts])
+    weight_copy = pltpu.make_async_copy(weight_hbm, weight_ref, sems.at[parts + 1])
+    ids_copy.start()
+    weight_copy.start()
+    step_rows = tokens // parts
+
+    def fetch(hbm):
+        return [
+            pltpu.make_async_copy(
+                hbm.at[pl.ds(part * step_rows, step_rows), :],
+                source_ref.at[pl.ds(part * step_rows, step_rows), :],
+                sems.at[part],
+            )
+            for part in range(parts)
+        ]
+
+    @pl.when(first)
+    def _():
+        for copy in fetch(tok_hbm):
+            copy.start()
+
+    @pl.when(jnp.logical_not(first))
+    def _():
+        for copy in fetch(grad_hbm):
+            copy.start()
+
+    ids_copy.wait()
+    weight_copy.wait()
+    ids = ids_ref[...]
     weight = weight_ref[...]
-    high = weight.astype(BF16)
-    rest = weight - high.astype(F32)
-    middle = rest.astype(BF16)
-    low = (rest - middle.astype(F32)).astype(BF16)
-    weight = (swap_to_lanes(eye, high) + swap_to_lanes(eye, middle)) + swap_to_lanes(eye, low)
     members, weights = [], []
     for step in range(experts):
-        expert = lax.rem(me + step, experts).astype(F32)
-        match = ids == expert
+        match = ids == peer(me, step, experts)
         members.append(jnp.max(jnp.where(match, 1.0, 0.0), axis=0, keepdims=True))
         weights.append(jnp.sum(jnp.where(match, weight, 0.0), axis=0, keepdims=True))
     member = jnp.concatenate(members, axis=0)
@@ -56,7 +76,18 @@
     position = dot(member.astype(BF16), earlier)
     slot = lax.broadcasted_iota(jnp.int32, (SLOTS, tokens), 0).astype(F32)
     rows = lax.broadcasted_iota(jnp.int32, (SLOTS, 1), 0)
-    source = jnp.where(first, tok_ref[...], grad_ref[...])
+
+    @pl.when(first)
+    def _():
+        for copy in fetch(tok_hbm):
+            copy.wait()
+
+    @pl.when(jnp.logical_not(first))
+    def _():
+        for copy in fetch(grad_hbm):
+            copy.wait()
+
+    source = source_ref[...]
     for step in range(experts):
         hit = (slot == position[step : step + 1, :]) & (member[step : step + 1, :] > 0.5)
         pick = jnp.where(hit, 1.0, 0.0)
@@ -68,15 +99,53 @@
         out_refs[step][...] = packed.astype(BF16)
 
 
+def in_hbm(array):
+    return pltpu.with_memory_space_constraint(array, pltpu.HBM)
+
+
+def load_kernel(count, *refs):
+    sources, targets, sems = refs[:count], refs[count + 1 : 2 * count + 1], refs[-1]
+    copies = [
+        pltpu.make_async_copy(source, target, sems.at[index])
+        for index, (source, target) in enumerate(zip(sources, targets))
+    ]
+    for copy in copies:
+        copy.start()
+    for copy in copies:
+        copy.wait()
+
+
+def load(arrays, after):
+    count = len(arrays)
+    return pl.pallas_call(
+        functools.partial(load_kernel, count),
+        out_shape=[pltpu.VMEM(array.shape, array.dtype) for array in arrays],
+        in_specs=[HBM] * count + [ANY],
+        out_specs=[VMEM] * count,
+        scratch_shapes=[pltpu.SemaphoreType.DMA((count,))],
+        compiler_params=pltpu.CompilerParams(vmem_limit_bytes=8 << 20),
+        name="load",
+    )(*[in_hbm(array) for array in arrays], after)
+
+
 def pack(experts, tokens, out_grad, ids, weight):
-    width = tokens.shape[1]
+    count, width = tokens.shape
+    parts = 5 if count % 80 == 0 else 1
+    inputs = [in_hbm(array) for array in (tokens, out_grad, ids.T, weight.T)]
     return pl.pallas_call(
-        functools.partial(pack_kernel, experts),
-        out_shape=[jax.ShapeDtypeStruct((SLOTS, width), BF16)] * experts,
-        in_specs=[VMEM] * 4,
+        functools.partial(pack_kernel, experts, parts),
+        out_shape=[pltpu.VMEM((SLOTS, width), BF16)] * experts,
+        in_specs=[HBM] * 4,
         out_specs=[VMEM] * experts,
+        scratch_shapes=[
+            pltpu.VMEM((count, width), BF16),
+            pltpu.VMEM(ids.shape[::-1], jnp.int32),
+            pltpu.VMEM(ids.shape[::-1], F32),
+            pltpu.SemaphoreType.DMA((parts + 2,)),
+        ],
         name="pack",
-    )(tokens, out_grad, ids, weight)
+        compiler_params=pltpu.CompilerParams(vmem_limit_bytes=16 << 20),
+    )(*inputs)
 
 
 def join(mine, theirs, x_rows, q_rows):
@@ -103,24 +172,25 @@
     mine, theirs = refs[:experts], refs[experts : 2 * experts]
     w_gate, w_up, w_down = refs[2 * experts : 2 * experts + 3]
     outs = refs[2 * experts + 3 : 2 * experts + 6]
-    frag_out, load_out, x_rows, q_rows = refs[2 * experts + 6 :]
+    frag_out, load_out, x_rows, q_rows, stage, sems = refs[2 * experts + 6 :]
     join(mine, theirs, x_rows, q_rows)
     total = jnp.zeros((1, 128), F32)
     for step in range(experts):
         total += x_rows[pl.ds(step * SLOTS + CAP, 1), pl.ds(0, 128)].astype(F32)
     load_out[...] = total / (experts * CAP)
     acts = activations(x_rows, q_rows, w_gate, w_up, w_down)
-    frag = frag_ref[0]
     cut = frag_out.shape[2]
+    frag_columns = pl.ds(pl.multiple_of(frag_ref[0] * cut, cut), cut)
+    copies = []
     for piece, (act, rows, out) in enumerate(zip(acts, (x_rows, x_rows, q_rows), outs)):
         for at in range(FRAGS):
             columns = pl.ds(at * cut, cut)
-            grad = dot(act, rows[:, columns])
-            out[:, columns] = grad.astype(BF16)
-
-            @pl.when(frag == at)
-            def _():
-                frag_out[piece] = grad
+            stage[piece, :, columns] = dot(act, rows[:, columns]).astype(BF16)
+        copies.append(pltpu.make_async_copy(stage.at[piece], out, sems.at[piece]))
+        copies[-1].start()
+        frag_out[piece] = dot(act, rows[:, frag_columns])
+    for copy in copies:
+        copy.wait()
 
 
 def own(experts, fragment, mine, theirs, weights):
@@ -129,11 +199,16 @@
     return pl.pallas_call(
         functools.partial(own_kernel, experts),
         out_shape=[jax.ShapeDtypeStruct((units, width), BF16)] * 3
-        + [jax.ShapeDtypeStruct((3, units, cut), F32), jax.ShapeDtypeStruct((1, 128), F32)],
+        + [pltpu.VMEM((3, units, cut), F32), jax.ShapeDtypeStruct((1, 128), F32)],
         in_specs=[SMEM] + [VMEM] * (2 * experts + 3),
-        out_specs=[VMEM] * 5,
-        scratch_shapes=[pltpu.VMEM((experts * SLOTS, width), BF16)] * 2,
+        out_specs=[HBM] * 3 + [VMEM] * 2,
+        scratch_shapes=[pltpu.VMEM((experts * SLOTS, width), BF16)] * 2
+        + [pltpu.VMEM((3, units, width), BF16), pltpu.SemaphoreType.DMA((3,))],
         name="own",
+        compiler_params=pltpu.CompilerParams(vmem_limit_bytes=32 << 20),
+        cost_estimate=pl.CostEstimate(
+            flops=12 * units * width * experts * SLOTS, bytes_accessed=12 * units * width, transcendentals=0
+        ),
     )(fragment, *mine, *theirs, *weights)
 
 
@@ -172,16 +247,64 @@
         + [pltpu.VMEM((3, units, cut), BF16), pltpu.SemaphoreType.DMA((3,))],
         input_output_aliases={at: 0, at + 1: 1, at + 2: 2},
         name="other",
+        compiler_params=pltpu.CompilerParams(vmem_limit_bytes=32 << 20),
+        cost_estimate=pl.CostEstimate(
+            flops=8 * units * width * experts * SLOTS, bytes_accessed=8 * units * width, transcendentals=0
+        ),
     )(fragment, *mine, *theirs, *weights, frag_grad, *grads)
 
 
-def shift(axis, step):
+def send(array, axis, step):
     size = lax.axis_size(axis)
-    return [(index, (index + step) % size) for index in range(size)]
-
-
-def send(array, axis, step):
-    return lax.ppermute(array, axis, shift(axis, step))
+    return lax.ppermute(array, axis, [(index, peer(index, step, size)) for index in range(size)])
+
+
+def tie(*arrays):
+    return lax.optimization_barrier(arrays)
+
+
+def two_replicas(fragment, packed, weights):
+    r0 = packed[0]
+    r2 = send(packed[2], "expert", 2)
+    x0 = send(r0, "replica", 1)
+    r1 = send(packed[1], "expert", 1)
+    r3 = send(packed[3], "expert", 3)
+    x1 = send(packed[1], ("expert", "replica"), 3)
+    weights = load(weights, r0)
+    r2, x0, x1, *weights = tie(r2, x0, x1, *weights)
+    c0 = send(r0, "tensor", 1)
+    c1 = send(r1, "tensor", 1)
+    f0 = send(x0, "tensor", 1)
+    c2 = send(r2, "tensor", 1)
+    x2 = send(r2, "replica", 1)
+    r3, c0, c1, f0, x1 = tie(r3, c0, c1, f0, x1)
+    c3 = send(r3, "tensor", 1)
+    x3 = send(r3, "replica", 1)
+    c3, x2 = tie(c3, x2)
+    mine = [r0, r1, r2, r3]
+    theirs = [c0, c1, c2, c3]
+    *grads, frag_grad, filled = own(4, fragment, mine, theirs, weights)
+    x1, x2, x3, filled = tie(x1, x2, x3, filled)
+    f1 = send(x1, "tensor", 1)
+    f2 = send(x2, "tensor", 1)
+    f3 = send(x3, "tensor", 1)
+    far = [x0, x1, x2, x3]
+    far_theirs = [f0, f1, f2, f3]
+    grads = other(4, fragment, far, far_theirs, weights, frag_grad, grads)
+    return grads, filled
+
+
+def any_replicas(experts, replicas, fragment, packed, weights):
+    mine = [packed[0]] + [send(packed[step], "expert", step) for step in range(1, experts)]
+    theirs = [send(rows, "tensor", 1) for rows in mine]
+    *grads, frag_grad, filled = own(experts, fragment, mine, theirs, weights)
+    synced = lax.psum(frag_grad.astype(BF16), "replica").astype(F32)
+    begin = fragment[0] * (weights[0].shape[1] // FRAGS)
+    grads = [
+        lax.dynamic_update_slice_in_dim(grad, (piece / replicas).astype(BF16), begin, 1)
+        for grad, piece in zip(grads, synced)
+    ]
+    return grads, filled
 
 
 def per_device(tokens, out_grad, expert_ids, route_weight, gate_proj, up_proj, down_proj, fragment):
@@ -189,21 +312,11 @@
     replicas = lax.axis_size("replica")
     weights = (gate_proj[0], up_proj[0], down_proj[0])
     packed = pack(experts, tokens[0], out_grad[0], expert_ids[0], route_weight[0])
-    mine = [packed[0]] + [send(packed[step], "expert", step) for step in range(1, experts)]
-    theirs = [send(rows, "tensor", 1) for rows in mine]
-    *grads, frag_grad, load = own(experts, fragment, mine, theirs, weights)
-    if replicas == 2:
-        far = [send(rows, "replica", 1) for rows in mine]
-        far_theirs = [send(rows, "tensor", 1) for rows in far]
-        grads = other(experts, fragment, far, far_theirs, weights, frag_grad, grads)
+    if replicas == 2 and experts == 4:
+        grads, filled = two_replicas(fragment, packed, weights)
     else:
-        synced = lax.psum(frag_grad.astype(BF16), "replica").astype(F32)
-        begin = fragment[0] * (weights[0].shape[1] // FRAGS)
-        grads = [
-            lax.dynamic_update_slice_in_dim(grad, (piece / replicas).astype(BF16), begin, 1)
-            for grad, piece in zip(grads, synced)
-        ]
-    return tuple(grad[None, None] for grad in grads) + (load[:, :1],)
+        grads, filled = any_replicas(experts, replicas, fragment, packed, weights)
+    return tuple(grad[None, None] for grad in grads) + (filled[:, :1],)
 
 
 def solution(mesh):

time: 46.5 us -> 30.7 us (0.66)
  waiting for transfers between devices: 12.8 us -> 4.61 us
  Pallas kernels: 15 us -> 9.01 us
  local copies, waits for them, and re-layouts: 4.31 us -> 0 us
  starting transfers between devices: 12.6 us -> 15.5 us
    ppermute x15, waiting for transfers between devices: 12.8 us -> 4.61 us  [send(): lax.ppermute(array, axis, [(index, peer(index, step, size)) for index in...]
    unnamed x32 -> x0, local copies, waits for them, and re-layouts: 4.31 us -> none
    pallas_call x1, Pallas kernels: 7.82 us -> 3.6 us  [own(): pl.pallas_call(functools.partial(own_kernel, experts), out_shape=[jax.Sha...]
    ppermute x15, starting transfers between devices: 12.6 us -> 15.5 us  [send(): lax.ppermute(array, axis, [(index, peer(index, step, size)) for index in...]
    pallas_call x1, Pallas kernels: 4.51 us -> 2.11 us  [other(): pl.pallas_call(functools.partial(other_kernel, experts), out_shape=[jax.S...]
    pallas_call x1 -> x2, Pallas kernels: 2.7 us -> 3.3 us  [the longest x1 1.67 us: pack(): pl.pallas_call(functools.partial(pack_kernel, experts, parts), out_shape=...]
  transfers between devices with their start and end apart: 15 -> 15, of which waited for: 5 -> 6; matrix products, arithmetic and copies ran while one was open for 0% -> 0% of each run, Pallas kernels for 17% -> 17%
where the time goes in v2:
time: 30.7 us; the launch traced here: 30.5 us
  starting transfers between devices  15.5 us (50%)
  Pallas kernels  9.01 us (29%)
  waiting for transfers between devices  4.61 us (15%)
  between operations  1.37 us (4%)
    ppermute x15, starting transfers between devices, send(): lax.ppermute(array, axis, [(index, peer(index, step, size)) for index in...  15.5 us
    ppermute x15, waiting for transfers between devices, send(): lax.ppermute(array, axis, [(index, peer(index, step, size)) for index in...  4.61 us
    pallas_call x1, Pallas kernels, own(): pl.pallas_call(functools.partial(own_kernel, experts), out_shape=[jax.Sha...  3.6 us
    pallas_call x1, Pallas kernels, other(): pl.pallas_call(functools.partial(other_kernel, experts), out_shape=[jax.S...  2.11 us
    pallas_call x1, Pallas kernels, pack(): pl.pallas_call(functools.partial(pack_kernel, experts, parts), out_shape=...  1.67 us
    pallas_call x1, Pallas kernels, load(): pl.pallas_call(functools.partial(load_kernel, count), out_shape=[pltpu.VM...  1.63 us
  transfers between devices with their start and end apart: 15, of which 6 were waited for; matrix products, arithmetic and copies ran while one was open for 0% of the time, Pallas kernels for 17%

profile of v2, /device:TPU:0, one launch (start us, length us, event | category | flops | bytes accessed | tf_op | source)
XLA Modules:
  0.0 30.5 jit_solution(10848176773100082791)
XLA Ops:
  0.6 1.7 %pack.1 = (bf16[64,1024]{1,0:T(8,128)(2,1)S(1)}, bf16[64,1024]{1,0:T(8,128)(2,1)S(1)}, bf16[64,1024]{1,0:T(8,128)(2,1)S(1)}, bf16[64,1024]{1,0:T(8,128)(2,1)S(1)}) custom-call(bf16[240,1024]{1,0:T(8,128)(2,1)} %bitcast.21, bf16[240,1024]{1,0:T(8,128)(2,1)} %bitcast.22, s32[8,240]{1,0:T(8,128)} %bitcast.23, f32[8,240]{1,0:T(8,128)} %bitcast.24), custom_call_target="tpu_custom_call" | custom-call | tf_op jit(solution)/shard_map/pack/pallas_call | solution.py:135
  2.3 4.1 %collective-permute-start = (bf16[64,1024]{1,0:T(8,128)(2,1)S(1)}, bf16[64,1024]{1,0:T(8,128)(2,1)S(1)}, u32[]{:S(2)}, u32[]{:S(2)}) collective-permute-start(bf16[64,1024]{1,0:T(8,128)(2,1)S(1)} %get-tuple-element.36), channel_id=1, source_target_pairs={{0,8},{4,12},{8,0},{12,4},{1,9},{5,13},{9,1},{13,5},{2,10},{6,14},... | collective-permute-start | bytes 393224 | tf_op jit(solution)/shard_map/ppermute | solution.py:259
  6.4 2.5 %collective-permute-start.2 = (bf16[64,1024]{1,0:T(8,128)(2,1)S(1)}, bf16[64,1024]{1,0:T(8,128)(2,1)S(1)}, u32[]{:S(2)}, u32[]{:S(2)}) collective-permute-start(bf16[64,1024]{1,0:T(8,128)(2,1)S(1)} %get-tuple-element.38), channel_id=1, source_target_pairs={{0,6},{2,4},{4,2},{6,0},{8,14},{10,12},{12,10},{14,8},{1,7},{3,5},... | collective-permute-start | bytes 393224 | tf_op jit(solution)/shard_map/ppermute | solution.py:259
  8.9 0.5 %collective-permute-start.1 = (bf16[64,1024]{1,0:T(8,128)(2,1)S(1)}, bf16[64,1024]{1,0:T(8,128)(2,1)S(1)}, u32[]{:S(2)}, u32[]{:S(2)}) collective-permute-start(bf16[64,1024]{1,0:T(8,128)(2,1)S(1)} %get-tuple-element.37.refs_3_.refs_0_), channel_id=1, source_target_pairs={{0,2},{2,0},{1,3},{3,1},{4,6},{6,4},{5,7},{7,5},{8,10},{10,8},{9,1... | collective-permute-start | bytes 393224 | tf_op jit(solution)/shard_map/ppermute | solution.py:259
  9.5 0.4 %collective-permute-start.5 = (bf16[64,1024]{1,0:T(8,128)(2,1)S(1)}, bf16[64,1024]{1,0:T(8,128)(2,1)S(1)}, u32[]{:S(2)}, u32[]{:S(2)}) collective-permute-start(bf16[64,1024]{1,0:T(8,128)(2,1)S(1)} %get-tuple-element.38), channel_id=1, source_target_pairs={{0,4},{4,0},{8,12},{12,8},{1,5},{5,1},{9,13},{13,9},{2,6},{6,2},{1... | collective-permute-start | bytes 393224 | tf_op jit(solution)/shard_map/ppermute | solution.py:259
  9.9 0.0 collective-permute-start.4
  9.9 1.6 %load.1 = (bf16[384,1024]{1,0:T(8,128)(2,1)S(1)}, bf16[384,1024]{1,0:T(8,128)(2,1)S(1)}, bf16[384,1024]{1,0:T(8,128)(2,1)S(1)}) custom-call(bf16[384,1024]{1,0:T(8,128)(2,1)} %bitcast.15, bf16[384,1024]{1,0:T(8,128)(2,1)} %bitcast.16, bf16[384,1024]{1,0:T(8,128)(2,1)} %bitcast.17, bf16[64,1024]{1,0:T(8,128)(2,1)S(1)} %get-tuple-element.37.refs_3_.refs_0_), custom_call_target="tpu_custom_call" | custom-call | tf_op jit(solution)/shard_map/load/pallas_call | solution.py:120
  11.5 1.3 %collective-permute-done.refs_2_ = bf16[64,1024]{1,0:T(8,128)(2,1)S(1)} collective-permute-done((bf16[64,1024]{1,0:T(8,128)(2,1)S(1)}, bf16[64,1024]{1,0:T(8,128)(2,1)S(1)}, u32[]{:S(2)}, u32[]{:S(2)}) %collective-permute-start) | collective-permute-done | bytes 131104 | tf_op jit(solution)/shard_map/ppermute | solution.py:259
  12.8 3.5 %collective-permute-start.3 = (bf16[64,1024]{1,0:T(8,128)(2,1)S(1)}, bf16[64,1024]{1,0:T(8,128)(2,1)S(1)}, u32[]{:S(2)}, u32[]{:S(2)}) collective-permute-start(bf16[64,1024]{1,0:T(8,128)(2,1)S(1)} %get-tuple-element.43), channel_id=1, source_target_pairs={{0,12},{4,8},{8,4},{12,0},{1,13},{5,9},{9,5},{13,1},{2,14},{6,10},... | collective-permute-start | bytes 393224 | tf_op jit(solution)/shard_map/ppermute | solution.py:259
  16.4 0.0 collective-permute-done.2.refs_1_
  16.4 0.0 collective-permute-done.1.refs_0_
  16.4 0.4 %collective-permute-done.5.refs_1_ = bf16[64,1024]{1,0:T(8,128)(2,1)S(1)} collective-permute-done((bf16[64,1024]{1,0:T(8,128)(2,1)S(1)}, bf16[64,1024]{1,0:T(8,128)(2,1)S(1)}, u32[]{:S(2)}, u32[]{:S(2)}) %collective-permute-start.5) | collective-permute-done | bytes 131104 | tf_op jit(solution)/shard_map/ppermute | solution.py:259
  16.8 0.0 collective-permute-start.6
  16.8 0.5 %collective-permute-start.7 = (bf16[64,1024]{1,0:T(8,128)(2,1)S(1)}, bf16[64,1024]{1,0:T(8,128)(2,1)S(1)}, u32[]{:S(2)}, u32[]{:S(2)}) collective-permute-start(bf16[64,1024]{1,0:T(8,128)(2,1)S(1)} %collective-permute-done.1.refs_0_), channel_id=1, source_target_pairs={{0,1},{1,0},{2,3},{3,2},{4,5},{5,4},{6,7},{7,6},{8,9},{9,8},{10,11... | collective-permute-start | bytes 393224 | tf_op jit(solution)/shard_map/ppermute | solution.py:259
  17.3 1.2 %collective-permute-start.9 = (bf16[64,1024]{1,0:T(8,128)(2,1)S(1)}, bf16[64,1024]{1,0:T(8,128)(2,1)S(1)}, u32[]{:S(2)}, u32[]{:S(2)}) collective-permute-start(bf16[64,1024]{1,0:T(8,128)(2,1)S(1)} %collective-permute-done.refs_2_), channel_id=1, source_target_pairs={{0,2},{2,0},{1,3},{3,1},{4,6},{6,4},{5,7},{7,5},{8,10},{10,8},{9,1... | collective-permute-start | bytes 393224 | tf_op jit(solution)/shard_map/ppermute | solution.py:259
  18.4 1.6 %collective-permute-done.3.refs_3_ = bf16[64,1024]{1,0:T(8,128)(2,1)S(1)} collective-permute-done((bf16[64,1024]{1,0:T(8,128)(2,1)S(1)}, bf16[64,1024]{1,0:T(8,128)(2,1)S(1)}, u32[]{:S(2)}, u32[]{:S(2)}) %collective-permute-start.3) | collective-permute-done | bytes 131104 | tf_op jit(solution)/shard_map/ppermute | solution.py:259
  20.1 0.0 collective-permute-done.4.refs_4_
  20.1 0.0 collective-permute-done.6.refs_5_
  20.1 0.0 collective-permute-done.7.refs_4_
  20.1 0.1 collective-permute-start.8
  20.2 0.5 %collective-permute-start.11 = (bf16[64,1024]{1,0:T(8,128)(2,1)S(1)}, bf16[64,1024]{1,0:T(8,128)(2,1)S(1)}, u32[]{:S(2)}, u32[]{:S(2)}) collective-permute-start(bf16[64,1024]{1,0:T(8,128)(2,1)S(1)} %collective-permute-done.refs_2_), channel_id=1, source_target_pairs={{0,1},{1,0},{2,3},{3,2},{4,5},{5,4},{6,7},{7,6},{8,9},{9,8},{10,11... | collective-permute-start | bytes 393224 | tf_op jit(solution)/shard_map/ppermute | solution.py:259
  20.7 1.5 %collective-permute-start.10 = (bf16[64,1024]{1,0:T(8,128)(2,1)S(1)}, bf16[64,1024]{1,0:T(8,128)(2,1)S(1)}, u32[]{:S(2)}, u32[]{:S(2)}) collective-permute-start(bf16[64,1024]{1,0:T(8,128)(2,1)S(1)} %collective-permute-done.3.refs_3_), channel_id=1, source_target_pairs={{0,2},{2,0},{1,3},{3,1},{4,6},{6,4},{5,7},{7,5},{8,10},{10,8},{9,1... | collective-permute-start | bytes 393224 | tf_op jit(solution)/shard_map/ppermute | solution.py:259
  22.8 0.0 collective-permute-done.9.refs_2_
  22.8 0.0 collective-permute-done.8.refs_7_
  22.8 0.0 collective-permute-done.11.refs_6_
  22.8 3.6 %own.1 = (bf16[384,1024]{1,0:T(8,128)(2,1)}, bf16[384,1024]{1,0:T(8,128)(2,1)}, bf16[384,1024]{1,0:T(8,128)(2,1)}, f32[3,384,256]{2,1,0:T(8,128)S(1)}, f32[1,128]{1,0:T(1,128)}) custom-call(s32[1]{0:T(128)S(6)} %copy.18.frag_ref, bf16[64,1024]{1,0:T(8,128)(2,1)S(1)} %get-tuple-element.37.refs_3_.refs_0_, ...), custom_call_target="tpu_custom_call" | custom-call | flops 1207959552 | bytes 4718592 | tf_op jit(solution)/shard_map/own/pallas_call | solution.py:199
  26.5 0.0 collective-permute-done.10.refs_3_
  26.5 0.1 collective-permute-start.12
  26.5 0.5 %collective-permute-start.13 = (bf16[64,1024]{1,0:T(8,128)(2,1)S(1)}, bf16[64,1024]{1,0:T(8,128)(2,1)S(1)}, u32[]{:S(2)}, u32[]{:S(2)}) collective-permute-start(bf16[64,1024]{1,0:T(8,128)(2,1)S(1)} %collective-permute-done.9.refs_2_), channel_id=1, source_target_pairs={{0,1},{1,0},{2,3},{3,2},{4,5},{5,4},{6,7},{7,6},{8,9},{9,8},{10,11... | collective-permute-start | bytes 393224 | tf_op jit(solution)/shard_map/ppermute | solution.py:259
  27.0 0.1 collective-permute-start.14
  27.1 0.8 %collective-permute-done.12.refs_5_ = bf16[64,1024]{1,0:T(8,128)(2,1)S(1)} collective-permute-done((bf16[64,1024]{1,0:T(8,128)(2,1)S(1)}, bf16[64,1024]{1,0:T(8,128)(2,1)S(1)}, u32[]{:S(2)}, u32[]{:S(2)}) %collective-permute-start.12) | collective-permute-done | bytes 131104 | tf_op jit(solution)/shard_map/ppermute | solution.py:259
  27.9 0.2 collective-permute-done.13.refs_6_
  28.1 0.3 %collective-permute-done.14.refs_7_ = bf16[64,1024]{1,0:T(8,128)(2,1)S(1)} collective-permute-done((bf16[64,1024]{1,0:T(8,128)(2,1)S(1)}, bf16[64,1024]{1,0:T(8,128)(2,1)S(1)}, u32[]{:S(2)}, u32[]{:S(2)}) %collective-permute-start.14) | collective-permute-done | bytes 131104 | tf_op jit(solution)/shard_map/ppermute | solution.py:259
  28.4 2.1 %other.1 = (bf16[384,1024]{1,0:T(8,128)(2,1)}, bf16[384,1024]{1,0:T(8,128)(2,1)}, bf16[384,1024]{1,0:T(8,128)(2,1)}) custom-call(s32[1]{0:T(128)S(6)} %copy.18.frag_ref, bf16[64,1024]{1,0:T(8,128)(2,1)S(1)} %collective-permute-done.1.refs_0_, ...), custom_call_target="tpu_custom_call", output_to_operand_aliasing={{0}: (13, {}), {1}: (14, {}), {2}: (15, {})} | custom-call | flops 805306368 | bytes 3145728 | tf_op jit(solution)/shard_map/other/pallas_call | solution.py:241
Async XLA Ops:
  2.3 10.5 %collective-permute-start = (bf16[64,1024]{1,0:T(8,128)(2,1)S(1)}, bf16[64,1024]{1,0:T(8,128)(2,1)S(1)}, u32[]{:S(2)}, u32[]{:S(2)}) collective-permute-start(bf16[64,1024]{1,0:T(8,128)(2,1)S(1)} %get-tuple-element.36), channel_id=1, source_target_pairs={{0,8},{4,12},{8,0},{12,4},{1,9},{5,13},{9,1},{13,5},{2,10},{6,14},... | collective-permute-start | bytes 393224 | tf_op jit(solution)/shard_map/ppermute | solution.py:259
  6.4 9.9 %collective-permute-start.2 = (bf16[64,1024]{1,0:T(8,128)(2,1)S(1)}, bf16[64,1024]{1,0:T(8,128)(2,1)S(1)}, u32[]{:S(2)}, u32[]{:S(2)}) collective-permute-start(bf16[64,1024]{1,0:T(8,128)(2,1)S(1)} %get-tuple-element.38), channel_id=1, source_target_pairs={{0,6},{2,4},{4,2},{6,0},{8,14},{10,12},{12,10},{14,8},{1,7},{3,5},... | collective-permute-start | bytes 393224 | tf_op jit(solution)/shard_map/ppermute | solution.py:259
  8.9 7.4 %collective-permute-start.1 = (bf16[64,1024]{1,0:T(8,128)(2,1)S(1)}, bf16[64,1024]{1,0:T(8,128)(2,1)S(1)}, u32[]{:S(2)}, u32[]{:S(2)}) collective-permute-start(bf16[64,1024]{1,0:T(8,128)(2,1)S(1)} %get-tuple-element.37.refs_3_.refs_0_), channel_id=1, source_target_pairs={{0,2},{2,0},{1,3},{3,1},{4,6},{6,4},{5,7},{7,5},{8,10},{10,8},{9,1... | collective-permute-start | bytes 393224 | tf_op jit(solution)/shard_map/ppermute | solution.py:259
  9.5 7.3 %collective-permute-start.5 = (bf16[64,1024]{1,0:T(8,128)(2,1)S(1)}, bf16[64,1024]{1,0:T(8,128)(2,1)S(1)}, u32[]{:S(2)}, u32[]{:S(2)}) collective-permute-start(bf16[64,1024]{1,0:T(8,128)(2,1)S(1)} %get-tuple-element.38), channel_id=1, source_target_pairs={{0,4},{4,0},{8,12},{12,8},{1,5},{5,1},{9,13},{13,9},{2,6},{6,2},{1... | collective-permute-start | bytes 393224 | tf_op jit(solution)/shard_map/ppermute | solution.py:259
  9.9 10.2 %collective-permute-start.4 = (bf16[64,1024]{1,0:T(8,128)(2,1)S(1)}, bf16[64,1024]{1,0:T(8,128)(2,1)S(1)}, u32[]{:S(2)}, u32[]{:S(2)}) collective-permute-start(bf16[64,1024]{1,0:T(8,128)(2,1)S(1)} %get-tuple-element.37.refs_3_.refs_0_), channel_id=1, source_target_pairs={{0,1},{1,0},{2,3},{3,2},{4,5},{5,4},{6,7},{7,6},{8,9},{9,8},{10,11... | collective-permute-start | bytes 393224 | tf_op jit(solution)/shard_map/ppermute | solution.py:259
  12.8 7.3 %collective-permute-start.3 = (bf16[64,1024]{1,0:T(8,128)(2,1)S(1)}, bf16[64,1024]{1,0:T(8,128)(2,1)S(1)}, u32[]{:S(2)}, u32[]{:S(2)}) collective-permute-start(bf16[64,1024]{1,0:T(8,128)(2,1)S(1)} %get-tuple-element.43), channel_id=1, source_target_pairs={{0,12},{4,8},{8,4},{12,0},{1,13},{5,9},{9,5},{13,1},{2,14},{6,10},... | collective-permute-start | bytes 393224 | tf_op jit(solution)/shard_map/ppermute | solution.py:259
  16.8 3.3 %collective-permute-start.6 = (bf16[64,1024]{1,0:T(8,128)(2,1)S(1)}, bf16[64,1024]{1,0:T(8,128)(2,1)S(1)}, u32[]{:S(2)}, u32[]{:S(2)}) collective-permute-start(bf16[64,1024]{1,0:T(8,128)(2,1)S(1)} %collective-permute-done.5.refs_1_), channel_id=1, source_target_pairs={{0,1},{1,0},{2,3},{3,2},{4,5},{5,4},{6,7},{7,6},{8,9},{9,8},{10,11... | collective-permute-start | bytes 393224 | tf_op jit(solution)/shard_map/ppermute | solution.py:259
  16.8 3.3 %collective-permute-start.7 = (bf16[64,1024]{1,0:T(8,128)(2,1)S(1)}, bf16[64,1024]{1,0:T(8,128)(2,1)S(1)}, u32[]{:S(2)}, u32[]{:S(2)}) collective-permute-start(bf16[64,1024]{1,0:T(8,128)(2,1)S(1)} %collective-permute-done.1.refs_0_), channel_id=1, source_target_pairs={{0,1},{1,0},{2,3},{3,2},{4,5},{5,4},{6,7},{7,6},{8,9},{9,8},{10,11... | collective-permute-start | bytes 393224 | tf_op jit(solution)/shard_map/ppermute | solution.py:259
  17.3 5.6 %collective-permute-start.9 = (bf16[64,1024]{1,0:T(8,128)(2,1)S(1)}, bf16[64,1024]{1,0:T(8,128)(2,1)S(1)}, u32[]{:S(2)}, u32[]{:S(2)}) collective-permute-start(bf16[64,1024]{1,0:T(8,128)(2,1)S(1)} %collective-permute-done.refs_2_), channel_id=1, source_target_pairs={{0,2},{2,0},{1,3},{3,1},{4,6},{6,4},{5,7},{7,5},{8,10},{10,8},{9,1... | collective-permute-start | bytes 393224 | tf_op jit(solution)/shard_map/ppermute | solution.py:259
  20.1 2.7 %collective-permute-start.8 = (bf16[64,1024]{1,0:T(8,128)(2,1)S(1)}, bf16[64,1024]{1,0:T(8,128)(2,1)S(1)}, u32[]{:S(2)}, u32[]{:S(2)}) collective-permute-start(bf16[64,1024]{1,0:T(8,128)(2,1)S(1)} %collective-permute-done.3.refs_3_), channel_id=1, source_target_pairs={{0,1},{1,0},{2,3},{3,2},{4,5},{5,4},{6,7},{7,6},{8,9},{9,8},{10,11... | collective-permute-start | bytes 393224 | tf_op jit(solution)/shard_map/ppermute | solution.py:259
  20.2 2.7 %collective-permute-start.11 = (bf16[64,1024]{1,0:T(8,128)(2,1)S(1)}, bf16[64,1024]{1,0:T(8,128)(2,1)S(1)}, u32[]{:S(2)}, u32[]{:S(2)}) collective-permute-start(bf16[64,1024]{1,0:T(8,128)(2,1)S(1)} %collective-permute-done.refs_2_), channel_id=1, source_target_pairs={{0,1},{1,0},{2,3},{3,2},{4,5},{5,4},{6,7},{7,6},{8,9},{9,8},{10,11... | collective-permute-start | bytes 393224 | tf_op jit(solution)/shard_map/ppermute | solution.py:259
  20.7 5.8 %collective-permute-start.10 = (bf16[64,1024]{1,0:T(8,128)(2,1)S(1)}, bf16[64,1024]{1,0:T(8,128)(2,1)S(1)}, u32[]{:S(2)}, u32[]{:S(2)}) collective-permute-start(bf16[64,1024]{1,0:T(8,128)(2,1)S(1)} %collective-permute-done.3.refs_3_), channel_id=1, source_target_pairs={{0,2},{2,0},{1,3},{3,1},{4,6},{6,4},{5,7},{7,5},{8,10},{10,8},{9,1... | collective-permute-start | bytes 393224 | tf_op jit(solution)/shard_map/ppermute | solution.py:259
  26.5 1.4 %collective-permute-start.12 = (bf16[64,1024]{1,0:T(8,128)(2,1)S(1)}, bf16[64,1024]{1,0:T(8,128)(2,1)S(1)}, u32[]{:S(2)}, u32[]{:S(2)}) collective-permute-start(bf16[64,1024]{1,0:T(8,128)(2,1)S(1)} %collective-permute-done.2.refs_1_), channel_id=1, source_target_pairs={{0,1},{1,0},{2,3},{3,2},{4,5},{5,4},{6,7},{7,6},{8,9},{9,8},{10,11... | collective-permute-start | bytes 393224 | tf_op jit(solution)/shard_map/ppermute | solution.py:259
  26.5 1.5 %collective-permute-start.13 = (bf16[64,1024]{1,0:T(8,128)(2,1)S(1)}, bf16[64,1024]{1,0:T(8,128)(2,1)S(1)}, u32[]{:S(2)}, u32[]{:S(2)}) collective-permute-start(bf16[64,1024]{1,0:T(8,128)(2,1)S(1)} %collective-permute-done.9.refs_2_), channel_id=1, source_target_pairs={{0,1},{1,0},{2,3},{3,2},{4,5},{5,4},{6,7},{7,6},{8,9},{9,8},{10,11... | collective-permute-start | bytes 393224 | tf_op jit(solution)/shard_map/ppermute | solution.py:259
  27.0 1.3 %collective-permute-start.14 = (bf16[64,1024]{1,0:T(8,128)(2,1)S(1)}, bf16[64,1024]{1,0:T(8,128)(2,1)S(1)}, u32[]{:S(2)}, u32[]{:S(2)}) collective-permute-start(bf16[64,1024]{1,0:T(8,128)(2,1)S(1)} %collective-permute-done.10.refs_3_), channel_id=1, source_target_pairs={{0,1},{1,0},{2,3},{3,2},{4,5},{5,4},{6,7},{7,6},{8,9},{9,8},{10,11... | collective-permute-start | bytes 393224 | tf_op jit(solution)/shard_map/ppermute | solution.py:259

commit v3 on v2

--- a/solution.py
+++ b/solution.py
@@ -29,7 +29,7 @@
 
 
 def pack_kernel(experts, parts, tok_hbm, grad_hbm, ids_hbm, weight_hbm, *refs):
-    out_refs, (source_ref, ids_ref, weight_ref, sems) = refs[:experts], refs[experts:]
+    *out_refs, source_ref, ids_ref, weight_ref, sems = refs
     me = lax.axis_index("expert")
     first = lax.axis_index("tensor") == 0
     tokens = ids_ref.shape[1]
@@ -96,7 +96,10 @@
         packed = dot(pick.astype(BF16), source) * scale
         count = jnp.sum(members[step], axis=1, keepdims=True)
         packed = jnp.where((rows == CAP) & first, count, packed)
-        out_refs[step][...] = packed.astype(BF16)
+        packed = packed.astype(BF16)
+        for out in out_refs[step:] if step == experts - 1 else out_refs[step : step + 1]:
+            out[...] = packed[: out.shape[0], :]
+            packed = packed[out.shape[0] :, :]
 
 
 def in_hbm(array):
@@ -104,7 +107,7 @@
 
 
 def load_kernel(count, *refs):
-    sources, targets, sems = refs[:count], refs[count + 1 : 2 * count + 1], refs[-1]
+    sources, targets, sems = refs[:count], refs[count + 2 : 2 * count + 2], refs[-1]
     copies = [
         pltpu.make_async_copy(source, target, sems.at[index])
         for index, (source, target) in enumerate(zip(sources, targets))
@@ -115,30 +118,50 @@
         copy.wait()
 
 
-def load(arrays, after):
+def load(arrays, fragment, after):
     count = len(arrays)
     return pl.pallas_call(
         functools.partial(load_kernel, count),
         out_shape=[pltpu.VMEM(array.shape, array.dtype) for array in arrays],
-        in_specs=[HBM] * count + [ANY],
+        in_specs=[HBM] * count + [SMEM, ANY],
         out_specs=[VMEM] * count,
         scratch_shapes=[pltpu.SemaphoreType.DMA((count,))],
         compiler_params=pltpu.CompilerParams(vmem_limit_bytes=8 << 20),
         name="load",
-    )(*[in_hbm(array) for array in arrays], after)
-
-
-def pack(experts, tokens, out_grad, ids, weight):
-    count, width = tokens.shape
-    parts = 5 if count % 80 == 0 else 1
+    )(*[in_hbm(array) for array in arrays], fragment, after)
+
+
+def stack_kernel(*refs):
+    *parts, whole = refs
+    at = 0
+    for part in parts:
+        whole[pl.ds(at, part.shape[0]), :] = part[...]
+        at += part.shape[0]
+
+
+def stack(parts):
+    rows = sum(part.shape[0] for part in parts)
+    return pl.pallas_call(
+        stack_kernel,
+        out_shape=pltpu.VMEM((rows, parts[0].shape[1]), parts[0].dtype),
+        in_specs=[VMEM] * len(parts),
+        out_specs=VMEM,
+        compiler_params=pltpu.CompilerParams(vmem_limit_bytes=8 << 20),
+        name="stack",
+    )(*parts)
+
+
+def pack(experts, rows, tokens, out_grad, ids, weight):
+    width = tokens.shape[1]
+    parts = 5 if tokens.shape[0] % 80 == 0 else 1
     inputs = [in_hbm(array) for array in (tokens, out_grad, ids.T, weight.T)]
     return pl.pallas_call(
         functools.partial(pack_kernel, experts, parts),
-        out_shape=[pltpu.VMEM((SLOTS, width), BF16)] * experts,
+        out_shape=[pltpu.VMEM((count, width), BF16) for count in rows],
         in_specs=[HBM] * 4,
-        out_specs=[VMEM] * experts,
+        out_specs=[VMEM] * len(rows),
         scratch_shapes=[
-            pltpu.VMEM((count, width), BF16),
+            pltpu.VMEM((tokens.shape[0], width), BF16),
             pltpu.VMEM(ids.shape[::-1], jnp.int32),
             pltpu.VMEM(ids.shape[::-1], F32),
             pltpu.SemaphoreType.DMA((parts + 2,)),
@@ -150,10 +173,12 @@
 
 def join(mine, theirs, x_rows, q_rows):
     first = lax.axis_index("tensor") == 0
-    for step, (here, there) in enumerate(zip(mine, theirs)):
-        place = pl.ds(step * SLOTS, SLOTS)
+    at = 0
+    for here, there in zip(mine, theirs):
+        place = pl.ds(at, here.shape[0])
         x_rows[place, :] = jnp.where(first, here[...], there[...])
         q_rows[place, :] = jnp.where(first, there[...], here[...])
+        at += here.shape[0]
 
 
 def activations(x_rows, q_rows, w_gate, w_up, w_down):
@@ -168,11 +193,11 @@
     return gate_grad, up_grad, hidden
 
 
-def own_kernel(experts, frag_ref, *refs):
-    mine, theirs = refs[:experts], refs[experts : 2 * experts]
-    w_gate, w_up, w_down = refs[2 * experts : 2 * experts + 3]
-    outs = refs[2 * experts + 3 : 2 * experts + 6]
-    frag_out, load_out, x_rows, q_rows, stage, sems = refs[2 * experts + 6 :]
+def own_kernel(experts, pieces, frag_ref, *refs):
+    mine, theirs = refs[:pieces], refs[pieces : 2 * pieces]
+    w_gate, w_up, w_down = refs[2 * pieces : 2 * pieces + 3]
+    outs = refs[2 * pieces + 3 : 2 * pieces + 6]
+    frag_out, load_out, x_rows, q_rows, stage, sems = refs[2 * pieces + 6 :]
     join(mine, theirs, x_rows, q_rows)
     total = jnp.zeros((1, 128), F32)
     for step in range(experts):
@@ -188,6 +213,7 @@
             stage[piece, :, columns] = dot(act, rows[:, columns]).astype(BF16)
         copies.append(pltpu.make_async_copy(stage.at[piece], out, sems.at[piece]))
         copies[-1].start()
+    for piece, (act, rows) in enumerate(zip(acts, (x_rows, x_rows, q_rows))):
         frag_out[piece] = dot(act, rows[:, frag_columns])
     for copy in copies:
         copy.wait()
@@ -196,11 +222,12 @@
 def own(experts, fragment, mine, theirs, weights):
     units, width = weights[0].shape
     cut = width // FRAGS
-    return pl.pallas_call(
-        functools.partial(own_kernel, experts),
+    pieces = len(mine)
+    return pl.pallas_call(
+        functools.partial(own_kernel, experts, pieces),
         out_shape=[jax.ShapeDtypeStruct((units, width), BF16)] * 3
         + [pltpu.VMEM((3, units, cut), F32), jax.ShapeDtypeStruct((1, 128), F32)],
-        in_specs=[SMEM] + [VMEM] * (2 * experts + 3),
+        in_specs=[SMEM] + [VMEM] * (2 * pieces + 3),
         out_specs=[HBM] * 3 + [VMEM] * 2,
         scratch_shapes=[pltpu.VMEM((experts * SLOTS, width), BF16)] * 2
         + [pltpu.VMEM((3, units, width), BF16), pltpu.SemaphoreType.DMA((3,))],
@@ -212,12 +239,12 @@
     )(fragment, *mine, *theirs, *weights)
 
 
-def other_kernel(experts, frag_ref, *refs):
-    mine, theirs = refs[:experts], refs[experts : 2 * experts]
-    w_gate, w_up, w_down = refs[2 * experts : 2 * experts + 3]
-    frag_in = refs[2 * experts + 3]
-    outs = refs[2 * experts + 7 : 2 * experts + 10]
-    x_rows, q_rows, cuts, sems = refs[2 * experts + 10 :]
+def other_kernel(pieces, frag_ref, *refs):
+    mine, theirs = refs[:pieces], refs[pieces : 2 * pieces]
+    w_gate, w_up, w_down = refs[2 * pieces : 2 * pieces + 3]
+    frag_in = refs[2 * pieces + 3]
+    outs = refs[2 * pieces + 7 : 2 * pieces + 10]
+    x_rows, q_rows, cuts, sems = refs[2 * pieces + 10 :]
     join(mine, theirs, x_rows, q_rows)
     acts = activations(x_rows, q_rows, w_gate, w_up, w_down)
     cut = frag_in.shape[2]
@@ -234,22 +261,24 @@
         copy.wait()
 
 
-def other(experts, fragment, mine, theirs, weights, frag_grad, grads):
+def other(fragment, mine, theirs, weights, frag_grad, grads):
     units, width = weights[0].shape
     cut = width // FRAGS
-    at = 1 + 2 * experts + 4
-    return pl.pallas_call(
-        functools.partial(other_kernel, experts),
+    pieces = len(mine)
+    rows = sum(part.shape[0] for part in mine)
+    at = 1 + 2 * pieces + 4
+    return pl.pallas_call(
+        functools.partial(other_kernel, pieces),
         out_shape=[jax.ShapeDtypeStruct((units, width), BF16)] * 3,
-        in_specs=[SMEM] + [VMEM] * (2 * experts + 4) + [ANY] * 3,
+        in_specs=[SMEM] + [VMEM] * (2 * pieces + 4) + [ANY] * 3,
         out_specs=[ANY] * 3,
-        scratch_shapes=[pltpu.VMEM((experts * SLOTS, width), BF16)] * 2
+        scratch_shapes=[pltpu.VMEM((rows, width), BF16)] * 2
         + [pltpu.VMEM((3, units, cut), BF16), pltpu.SemaphoreType.DMA((3,))],
         input_output_aliases={at: 0, at + 1: 1, at + 2: 2},
         name="other",
         compiler_params=pltpu.CompilerParams(vmem_limit_bytes=32 << 20),
         cost_estimate=pl.CostEstimate(
-            flops=8 * units * width * experts * SLOTS, bytes_accessed=8 * units * width, transcendentals=0
+            flops=8 * units * width * rows, bytes_accessed=8 * units * width, transcendentals=0
         ),
     )(fragment, *mine, *theirs, *weights, frag_grad, *grads)
 
@@ -265,32 +294,25 @@
 
 def two_replicas(fragment, packed, weights):
     r0 = packed[0]
-    r2 = send(packed[2], "expert", 2)
+    r3 = send(packed[3], "expert", 3)
     x0 = send(r0, "replica", 1)
     r1 = send(packed[1], "expert", 1)
-    r3 = send(packed[3], "expert", 3)
     x1 = send(packed[1], ("expert", "replica"), 3)
-    weights = load(weights, r0)
-    r2, x0, x1, *weights = tie(r2, x0, x1, *weights)
-    c0 = send(r0, "tensor", 1)
-    c1 = send(r1, "tensor", 1)
-    f0 = send(x0, "tensor", 1)
-    c2 = send(r2, "tensor", 1)
+    r2 = send(packed[2], "expert", 2)
+    weights = load(weights, fragment, r0)
+    r3, x0, *weights = tie(r3, x0, *weights)
+    x3 = send(r3, "replica", 1)
+    r2, x3, r1, x1 = tie(r2, x3, r1, x1)
     x2 = send(r2, "replica", 1)
-    r3, c0, c1, f0, x1 = tie(r3, c0, c1, f0, x1)
-    c3 = send(r3, "tensor", 1)
-    x3 = send(r3, "replica", 1)
-    c3, x2 = tie(c3, x2)
-    mine = [r0, r1, r2, r3]
-    theirs = [c0, c1, c2, c3]
+    near = stack([r0, r1, r3, r2])
+    c0 = send(near, "tensor", 1)
+    far = stack([x0, x1, x3])
+    f0 = send(far, "tensor", 1)
+    mine, theirs = [near], [c0]
     *grads, frag_grad, filled = own(4, fragment, mine, theirs, weights)
-    x1, x2, x3, filled = tie(x1, x2, x3, filled)
-    f1 = send(x1, "tensor", 1)
-    f2 = send(x2, "tensor", 1)
-    f3 = send(x3, "tensor", 1)
-    far = [x0, x1, x2, x3]
-    far_theirs = [f0, f1, f2, f3]
-    grads = other(4, fragment, far, far_theirs, weights, frag_grad, grads)
+    x2, filled = tie(x2, filled)
+    f3 = send(x2, "tensor", 1)
+    grads = other(fragment, [far, x2], [f0, f3], weights, frag_grad, grads)
     return grads, filled
 
 
@@ -311,7 +333,8 @@
     experts = lax.axis_size("expert")
     replicas = lax.axis_size("replica")
     weights = (gate_proj[0], up_proj[0], down_proj[0])
-    packed = pack(experts, tokens[0], out_grad[0], expert_ids[0], route_weight[0])
+    parts = [SLOTS] * experts
+    packed = pack(experts, parts, tokens[0], out_grad[0], expert_ids[0], route_weight[0])
     if replicas == 2 and experts == 4:
         grads, filled = two_replicas(fragment, packed, weights)
     else:

time: 30.7 us -> 29.6 us (0.964)
  starting transfers between devices: 15.5 us -> 13.2 us
  waiting for transfers between devices: 4.61 us -> 5.91 us
    ppermute x15 -> x10, starting transfers between devices: 15.5 us -> 13.2 us  [send(): lax.ppermute(array, axis, [(index, peer(index, step, size)) for index in...]
    ppermute x15 -> x10, waiting for transfers between devices: 4.61 us -> 5.91 us  [send(): lax.ppermute(array, axis, [(index, peer(index, step, size)) for index in...]
    pallas_call x2 -> x4, Pallas kernels: 5.71 us -> 5.65 us  [the longest x1 3.48 us: own(): pl.pallas_call(functools.partial(own_kernel, experts, pieces), out_shape=...]
  transfers between devices with their start and end apart: 15 -> 10, of which waited for: 6 -> 4; matrix products, arithmetic and copies ran while one was open for 0% -> 0% of each run, Pallas kernels for 17% -> 18%
where the time goes in v3:
time: 29.6 us; the launch traced here: 29.4 us
  starting transfers between devices  13.2 us (45%)
  Pallas kernels  8.96 us (30%)
  waiting for transfers between devices  5.91 us (20%)
  between operations  1.35 us (5%)
    ppermute x10, starting transfers between devices, send(): lax.ppermute(array, axis, [(index, peer(index, step, size)) for index in...  13.2 us
    ppermute x10, waiting for transfers between devices, send(): lax.ppermute(array, axis, [(index, peer(index, step, size)) for index in...  5.91 us
    pallas_call x1, Pallas kernels, own(): pl.pallas_call(functools.partial(own_kernel, experts, pieces), out_shape=...  3.48 us
    pallas_call x1, Pallas kernels, other(): pl.pallas_call(functools.partial(other_kernel, pieces), out_shape=[jax.Sh...  2.11 us
    pallas_call x1, Pallas kernels, pack(): pl.pallas_call(functools.partial(pack_kernel, experts, parts), out_shape=...  1.67 us
    pallas_call x1, Pallas kernels, load(): pl.pallas_call(functools.partial(load_kernel, count), out_shape=[pltpu.VM...  1.64 us
  transfers between devices with their start and end apart: 10, of which 4 were waited for; matrix products, arithmetic and copies ran while one was open for 0% of the time, Pallas kernels for 18%

profile of v3, /device:TPU:0, one launch (start us, length us, event | category | flops | bytes accessed | tf_op | source)
XLA Modules:
  0.0 29.4 jit_solution(3257425646240761897)
XLA Ops:
  0.6 1.7 %pack.1 = (bf16[64,1024]{1,0:T(8,128)(2,1)S(1)}, bf16[64,1024]{1,0:T(8,128)(2,1)S(1)}, bf16[64,1024]{1,0:T(8,128)(2,1)S(1)}, bf16[64,1024]{1,0:T(8,128)(2,1)S(1)}) custom-call(bf16[240,1024]{1,0:T(8,128)(2,1)} %bitcast.21, bf16[240,1024]{1,0:T(8,128)(2,1)} %bitcast.22, s32[8,240]{1,0:T(8,128)} %bitcast.23, f32[8,240]{1,0:T(8,128)} %bitcast.24), custom_call_target="tpu_custom_call" | custom-call | tf_op jit(solution)/shard_map/pack/pallas_call | solution.py:158
  2.3 5.1 %collective-permute-start = (bf16[64,1024]{1,0:T(8,128)(2,1)S(1)}, bf16[64,1024]{1,0:T(8,128)(2,1)S(1)}, u32[]{:S(2)}, u32[]{:S(2)}) collective-permute-start(bf16[64,1024]{1,0:T(8,128)(2,1)S(1)} %get-tuple-element.30), channel_id=1, source_target_pairs={{0,12},{4,8},{8,4},{12,0},{1,13},{5,9},{9,5},{13,1},{2,14},{6,10},... | collective-permute-start | bytes 393224 | tf_op jit(solution)/shard_map/ppermute | solution.py:288
  7.4 1.5 %collective-permute-start.1 = (bf16[64,1024]{1,0:T(8,128)(2,1)S(1)}, bf16[64,1024]{1,0:T(8,128)(2,1)S(1)}, u32[]{:S(2)}, u32[]{:S(2)}) collective-permute-start(bf16[64,1024]{1,0:T(8,128)(2,1)S(1)} %get-tuple-element.31.refs_4_.refs_0_), channel_id=1, source_target_pairs={{0,2},{2,0},{1,3},{3,1},{4,6},{6,4},{5,7},{7,5},{8,10},{10,8},{9,1... | collective-permute-start | bytes 393224 | tf_op jit(solution)/shard_map/ppermute | solution.py:288
  8.9 0.0 collective-permute-start.5
  8.9 2.0 %collective-permute-start.4 = (bf16[64,1024]{1,0:T(8,128)(2,1)S(1)}, bf16[64,1024]{1,0:T(8,128)(2,1)S(1)}, u32[]{:S(2)}, u32[]{:S(2)}) collective-permute-start(bf16[64,1024]{1,0:T(8,128)(2,1)S(1)} %get-tuple-element.38), channel_id=1, source_target_pairs={{0,4},{4,0},{8,12},{12,8},{1,5},{5,1},{9,13},{13,9},{2,6},{6,2},{1... | collective-permute-start | bytes 393224 | tf_op jit(solution)/shard_map/ppermute | solution.py:288
  10.9 0.0 collective-permute-start.2
  11.6 1.6 %load.1 = (bf16[384,1024]{1,0:T(8,128)(2,1)S(1)}, bf16[384,1024]{1,0:T(8,128)(2,1)S(1)}, bf16[384,1024]{1,0:T(8,128)(2,1)S(1)}) custom-call(bf16[384,1024]{1,0:T(8,128)(2,1)} %bitcast.15, bf16[384,1024]{1,0:T(8,128)(2,1)} %bitcast.16, bf16[384,1024]{1,0:T(8,128)(2,1)} %bitcast.17, s32[1]{0:T(128)S(6)} %copy.18.refs_3_.frag_ref, ...), custom_call_target="tpu_custom_call" | custom-call | tf_op jit(solution)/shard_map/load/pallas_call | solution.py:123
  13.2 0.0 collective-permute-done.refs_2_
  13.2 0.0 collective-permute-done.1.refs_0_
  13.2 2.4 %collective-permute-start.3 = (bf16[64,1024]{1,0:T(8,128)(2,1)S(1)}, bf16[64,1024]{1,0:T(8,128)(2,1)S(1)}, u32[]{:S(2)}, u32[]{:S(2)}) collective-permute-start(bf16[64,1024]{1,0:T(8,128)(2,1)S(1)} %collective-permute-done.refs_2_), channel_id=1, source_target_pairs={{0,2},{2,0},{1,3},{3,1},{4,6},{6,4},{5,7},{7,5},{8,10},{10,8},{9,1... | collective-permute-start | bytes 393224 | tf_op jit(solution)/shard_map/ppermute | solution.py:288
  15.6 4.1 %collective-permute-done.2.refs_3_ = bf16[64,1024]{1,0:T(8,128)(2,1)S(1)} collective-permute-done((bf16[64,1024]{1,0:T(8,128)(2,1)S(1)}, bf16[64,1024]{1,0:T(8,128)(2,1)S(1)}, u32[]{:S(2)}, u32[]{:S(2)}) %collective-permute-start.2) | collective-permute-done | bytes 131104 | tf_op jit(solution)/shard_map/ppermute | solution.py:288
  19.7 0.0 collective-permute-done.5.refs_1_
  19.7 0.1 collective-permute-done.4.refs_1_
  19.8 0.0 collective-permute-done.3.refs_2_
  19.8 0.1 collective-permute-start.7
  19.9 0.6 %collective-permute-start.8 = (bf16[192,1024]{1,0:T(8,128)(2,1)S(1)}, bf16[192,1024]{1,0:T(8,128)(2,1)S(1)}, u32[]{:S(2)}, u32[]{:S(2)}) collective-permute-start(bf16[192,1024]{1,0:T(8,128)(2,1)S(1)} %stack.2.refs_0_), channel_id=1, source_target_pairs={{0,1},{1,0},{2,3},{3,2},{4,5},{5,4},{6,7},{7,6},{8,9},{9,8},{10,11... | collective-permute-start | bytes 1179656 | tf_op jit(solution)/shard_map/ppermute | solution.py:288
  20.5 1.6 %collective-permute-start.6 = (bf16[64,1024]{1,0:T(8,128)(2,1)S(1)}, bf16[64,1024]{1,0:T(8,128)(2,1)S(1)}, u32[]{:S(2)}, u32[]{:S(2)}) collective-permute-start(bf16[64,1024]{1,0:T(8,128)(2,1)S(1)} %collective-permute-done.2.refs_3_), channel_id=1, source_target_pairs={{0,2},{2,0},{1,3},{3,1},{4,6},{6,4},{5,7},{7,5},{8,10},{10,8},{9,1... | collective-permute-start | bytes 393224 | tf_op jit(solution)/shard_map/ppermute | solution.py:288
  22.0 0.0 collective-permute-done.7.refs_1_
  22.0 3.5 %own.1 = (bf16[384,1024]{1,0:T(8,128)(2,1)}, bf16[384,1024]{1,0:T(8,128)(2,1)}, bf16[384,1024]{1,0:T(8,128)(2,1)}, f32[3,384,256]{2,1,0:T(8,128)S(1)}, f32[1,128]{1,0:T(1,128)}) custom-call(s32[1]{0:T(128)S(6)} %copy.18.refs_3_.frag_ref, bf16[256,1024]{1,0:T(8,128)(2,1)S(1)} %stack.3.refs_0_, bf16[256,1024]{1,0:T(8,128)(2,1)S(1)} %collective-permute-done.7.refs_1_, ...), custom_call_target="tpu_custom_call" | custom-call | flops 1207959552 | bytes 4718592 | tf_op jit(solution)/shard_map/own/pallas_call | solution.py:226
  25.5 0.4 %collective-permute-done.6.refs_1_ = bf16[64,1024]{1,0:T(8,128)(2,1)S(1)} collective-permute-done((bf16[64,1024]{1,0:T(8,128)(2,1)S(1)}, bf16[64,1024]{1,0:T(8,128)(2,1)S(1)}, u32[]{:S(2)}, u32[]{:S(2)}) %collective-permute-start.6) | collective-permute-done | bytes 131104 | tf_op jit(solution)/shard_map/ppermute | solution.py:288
  25.9 0.0 collective-permute-start.9
  25.9 0.0 collective-permute-done.8.refs_2_
  26.0 1.3 %collective-permute-done.9.refs_3_ = bf16[64,1024]{1,0:T(8,128)(2,1)S(1)} collective-permute-done((bf16[64,1024]{1,0:T(8,128)(2,1)S(1)}, bf16[64,1024]{1,0:T(8,128)(2,1)S(1)}, u32[]{:S(2)}, u32[]{:S(2)}) %collective-permute-start.9) | collective-permute-done | bytes 131104 | tf_op jit(solution)/shard_map/ppermute | solution.py:288
  27.3 2.1 %other.1 = (bf16[384,1024]{1,0:T(8,128)(2,1)}, bf16[384,1024]{1,0:T(8,128)(2,1)}, bf16[384,1024]{1,0:T(8,128)(2,1)}) custom-call(s32[1]{0:T(128)S(6)} %copy.18.refs_3_.frag_ref, bf16[192,1024]{1,0:T(8,128)(2,1)S(1)} %stack.2.refs_0_, ...), custom_call_target="tpu_custom_call", output_to_operand_aliasing={{0}: (9, {}), {1}: (10, {}), {2}: (11, {})} | custom-call | flops 805306368 | bytes 3145728 | tf_op jit(solution)/shard_map/other/pallas_call | solution.py:270
  (2 shorter events, 0.1 us)
Async XLA Ops:
  2.3 10.9 %collective-permute-start = (bf16[64,1024]{1,0:T(8,128)(2,1)S(1)}, bf16[64,1024]{1,0:T(8,128)(2,1)S(1)}, u32[]{:S(2)}, u32[]{:S(2)}) collective-permute-start(bf16[64,1024]{1,0:T(8,128)(2,1)S(1)} %get-tuple-element.30), channel_id=1, source_target_pairs={{0,12},{4,8},{8,4},{12,0},{1,13},{5,9},{9,5},{13,1},{2,14},{6,10},... | collective-permute-start | bytes 393224 | tf_op jit(solution)/shard_map/ppermute | solution.py:288
  7.4 5.8 %collective-permute-start.1 = (bf16[64,1024]{1,0:T(8,128)(2,1)S(1)}, bf16[64,1024]{1,0:T(8,128)(2,1)S(1)}, u32[]{:S(2)}, u32[]{:S(2)}) collective-permute-start(bf16[64,1024]{1,0:T(8,128)(2,1)S(1)} %get-tuple-element.31.refs_4_.refs_0_), channel_id=1, source_target_pairs={{0,2},{2,0},{1,3},{3,1},{4,6},{6,4},{5,7},{7,5},{8,10},{10,8},{9,1... | collective-permute-start | bytes 393224 | tf_op jit(solution)/shard_map/ppermute | solution.py:288
  8.9 10.8 %collective-permute-start.5 = (bf16[64,1024]{1,0:T(8,128)(2,1)S(1)}, bf16[64,1024]{1,0:T(8,128)(2,1)S(1)}, u32[]{:S(2)}, u32[]{:S(2)}) collective-permute-start(bf16[64,1024]{1,0:T(8,128)(2,1)S(1)} %get-tuple-element.38), channel_id=1, source_target_pairs={{0,6},{2,4},{4,2},{6,0},{8,14},{10,12},{12,10},{14,8},{1,7},{3,5},... | collective-permute-start | bytes 393224 | tf_op jit(solution)/shard_map/ppermute | solution.py:288
  8.9 10.8 %collective-permute-start.4 = (bf16[64,1024]{1,0:T(8,128)(2,1)S(1)}, bf16[64,1024]{1,0:T(8,128)(2,1)S(1)}, u32[]{:S(2)}, u32[]{:S(2)}) collective-permute-start(bf16[64,1024]{1,0:T(8,128)(2,1)S(1)} %get-tuple-element.38), channel_id=1, source_target_pairs={{0,4},{4,0},{8,12},{12,8},{1,5},{5,1},{9,13},{13,9},{2,6},{6,2},{1... | collective-permute-start | bytes 393224 | tf_op jit(solution)/shard_map/ppermute | solution.py:288
  10.9 8.8 %collective-permute-start.2 = (bf16[64,1024]{1,0:T(8,128)(2,1)S(1)}, bf16[64,1024]{1,0:T(8,128)(2,1)S(1)}, u32[]{:S(2)}, u32[]{:S(2)}) collective-permute-start(bf16[64,1024]{1,0:T(8,128)(2,1)S(1)} %get-tuple-element.36), channel_id=1, source_target_pairs={{0,8},{4,12},{8,0},{12,4},{1,9},{5,13},{9,1},{13,5},{2,10},{6,14},... | collective-permute-start | bytes 393224 | tf_op jit(solution)/shard_map/ppermute | solution.py:288
  13.2 6.5 %collective-permute-start.3 = (bf16[64,1024]{1,0:T(8,128)(2,1)S(1)}, bf16[64,1024]{1,0:T(8,128)(2,1)S(1)}, u32[]{:S(2)}, u32[]{:S(2)}) collective-permute-start(bf16[64,1024]{1,0:T(8,128)(2,1)S(1)} %collective-permute-done.refs_2_), channel_id=1, source_target_pairs={{0,2},{2,0},{1,3},{3,1},{4,6},{6,4},{5,7},{7,5},{8,10},{10,8},{9,1... | collective-permute-start | bytes 393224 | tf_op jit(solution)/shard_map/ppermute | solution.py:288
  19.8 2.3 %collective-permute-start.7 = (bf16[256,1024]{1,0:T(8,128)(2,1)S(1)}, bf16[256,1024]{1,0:T(8,128)(2,1)S(1)}, u32[]{:S(2)}, u32[]{:S(2)}) collective-permute-start(bf16[256,1024]{1,0:T(8,128)(2,1)S(1)} %stack.3.refs_0_), channel_id=1, source_target_pairs={{0,1},{1,0},{2,3},{3,2},{4,5},{5,4},{6,7},{7,6},{8,9},{9,8},{10,11... | collective-permute-start | bytes 1572872 | tf_op jit(solution)/shard_map/ppermute | solution.py:288
  19.9 6.0 %collective-permute-start.8 = (bf16[192,1024]{1,0:T(8,128)(2,1)S(1)}, bf16[192,1024]{1,0:T(8,128)(2,1)S(1)}, u32[]{:S(2)}, u32[]{:S(2)}) collective-permute-start(bf16[192,1024]{1,0:T(8,128)(2,1)S(1)} %stack.2.refs_0_), channel_id=1, source_target_pairs={{0,1},{1,0},{2,3},{3,2},{4,5},{5,4},{6,7},{7,6},{8,9},{9,8},{10,11... | collective-permute-start | bytes 1179656 | tf_op jit(solution)/shard_map/ppermute | solution.py:288
  20.5 5.5 %collective-permute-start.6 = (bf16[64,1024]{1,0:T(8,128)(2,1)S(1)}, bf16[64,1024]{1,0:T(8,128)(2,1)S(1)}, u32[]{:S(2)}, u32[]{:S(2)}) collective-permute-start(bf16[64,1024]{1,0:T(8,128)(2,1)S(1)} %collective-permute-done.2.refs_3_), channel_id=1, source_target_pairs={{0,2},{2,0},{1,3},{3,1},{4,6},{6,4},{5,7},{7,5},{8,10},{10,8},{9,1... | collective-permute-start | bytes 393224 | tf_op jit(solution)/shard_map/ppermute | solution.py:288
  25.9 1.3 %collective-permute-start.9 = (bf16[64,1024]{1,0:T(8,128)(2,1)S(1)}, bf16[64,1024]{1,0:T(8,128)(2,1)S(1)}, u32[]{:S(2)}, u32[]{:S(2)}) collective-permute-start(bf16[64,1024]{1,0:T(8,128)(2,1)S(1)} %collective-permute-done.6.refs_1_), channel_id=1, source_target_pairs={{0,1},{1,0},{2,3},{3,2},{4,5},{5,4},{6,7},{7,6},{8,9},{9,8},{10,11... | collective-permute-start | bytes 393224 | tf_op jit(solution)/shard_map/ppermute | solution.py:288

commit v4 on v3

--- a/solution.py
+++ b/solution.py
@@ -10,6 +10,10 @@
 FRAGS = 4
 CAP = 60
 SLOTS = 64
+BLOCKS = 4
+MAIN = CAP // 16 * 16
+REST = CAP - MAIN
+EMPTY = 64.0
 F32 = jnp.float32
 BF16 = jnp.bfloat16
 VMEM = pl.BlockSpec(memory_space=pltpu.VMEM)
@@ -28,36 +32,26 @@
     return index ^ step if size & (size - 1) == 0 else (index + step) % size
 
 
-def pack_kernel(experts, parts, tok_hbm, grad_hbm, ids_hbm, weight_hbm, *refs):
+def pack_kernel(experts, tok_hbm, grad_hbm, ids_hbm, weight_hbm, *refs):
     *out_refs, source_ref, ids_ref, weight_ref, sems = refs
     me = lax.axis_index("expert")
     first = lax.axis_index("tensor") == 0
     tokens = ids_ref.shape[1]
-    ids_copy = pltpu.make_async_copy(ids_hbm, ids_ref, sems.at[parts])
-    weight_copy = pltpu.make_async_copy(weight_hbm, weight_ref, sems.at[parts + 1])
+    ids_copy = pltpu.make_async_copy(ids_hbm, ids_ref, sems.at[0])
+    weight_copy = pltpu.make_async_copy(weight_hbm, weight_ref, sems.at[1])
     ids_copy.start()
     weight_copy.start()
-    step_rows = tokens // parts
-
-    def fetch(hbm):
-        return [
-            pltpu.make_async_copy(
-                hbm.at[pl.ds(part * step_rows, step_rows), :],
-                source_ref.at[pl.ds(part * step_rows, step_rows), :],
-                sems.at[part],
-            )
-            for part in range(parts)
-        ]
+    cut = source_ref.shape[1] // BLOCKS
+    tok_copy = pltpu.make_async_copy(tok_hbm, source_ref, sems.at[2])
+    grad_copy = pltpu.make_async_copy(grad_hbm, source_ref, sems.at[2])
 
     @pl.when(first)
     def _():
-        for copy in fetch(tok_hbm):
-            copy.start()
+        tok_copy.start()
 
     @pl.when(jnp.logical_not(first))
     def _():
-        for copy in fetch(grad_hbm):
-            copy.start()
+        grad_copy.start()
 
     ids_copy.wait()
     weight_copy.wait()
@@ -75,31 +69,38 @@
     ).astype(F32).astype(BF16)
     position = dot(member.astype(BF16), earlier)
     slot = lax.broadcasted_iota(jnp.int32, (SLOTS, tokens), 0).astype(F32)
-    rows = lax.broadcasted_iota(jnp.int32, (SLOTS, 1), 0)
-
-    @pl.when(first)
-    def _():
-        for copy in fetch(tok_hbm):
-            copy.wait()
-
-    @pl.when(jnp.logical_not(first))
-    def _():
-        for copy in fetch(grad_hbm):
-            copy.wait()
-
-    source = source_ref[...]
+    rows = lax.broadcasted_iota(jnp.int32, (SLOTS, 1), 0).astype(F32)
+    picks, scales, fills = [], [], []
     for step in range(experts):
         hit = (slot == position[step : step + 1, :]) & (member[step : step + 1, :] > 0.5)
         pick = jnp.where(hit, 1.0, 0.0)
         scale = jnp.sum(pick * weights[step], axis=1, keepdims=True)
-        scale = jnp.where(first, 1.0, scale)
-        packed = dot(pick.astype(BF16), source) * scale
+        scales.append(jnp.where(first, 1.0, scale))
         count = jnp.sum(members[step], axis=1, keepdims=True)
-        packed = jnp.where((rows == CAP) & first, count, packed)
-        packed = packed.astype(BF16)
-        for out in out_refs[step:] if step == experts - 1 else out_refs[step : step + 1]:
-            out[...] = packed[: out.shape[0], :]
-            packed = packed[out.shape[0] :, :]
+        fills.append(jnp.where((rows >= count) & first, EMPTY, 0.0))
+        picks.append(pick.astype(BF16))
+    picks = jnp.concatenate(picks, axis=0)
+    scales = jnp.concatenate(scales, axis=0)
+    fills = jnp.concatenate(fills, axis=0)
+    places = rest_places((BLOCKS * REST, BLOCKS * 16), 0, 1)
+    tok_copy.wait()
+    packed = (dot(picks, source_ref[...]) * scales + fills).astype(BF16)
+    rests = []
+    for block in range(BLOCKS):
+        for step in range(experts):
+            tile = packed[step * SLOTS : (step + 1) * SLOTS, block * cut : (block + 1) * cut]
+            out_refs[step][pl.ds(block * MAIN, MAIN), :] = tile[:MAIN]
+            rests.append(tile[MAIN:])
+    for step in range(experts):
+        rest = dot(places, jnp.concatenate(rests[step::experts], axis=0))
+        out_refs[step][pl.ds(BLOCKS * MAIN, BLOCKS * REST), :] = rest.astype(BF16)
+
+
+def rest_places(shape, wire, block):
+    left = lax.broadcasted_iota(jnp.int32, shape, wire)
+    right = lax.broadcasted_iota(jnp.int32, shape, block)
+    hit = (lax.rem(right, 16) < REST) & (left == right // 16 * REST + lax.rem(right, 16))
+    return hit.astype(F32).astype(BF16)
 
 
 def in_hbm(array):
@@ -151,20 +152,19 @@
     )(*parts)
 
 
-def pack(experts, rows, tokens, out_grad, ids, weight):
+def pack(experts, tokens, out_grad, ids, weight):
     width = tokens.shape[1]
-    parts = 5 if tokens.shape[0] % 80 == 0 else 1
     inputs = [in_hbm(array) for array in (tokens, out_grad, ids.T, weight.T)]
     return pl.pallas_call(
-        functools.partial(pack_kernel, experts, parts),
-        out_shape=[pltpu.VMEM((count, width), BF16) for count in rows],
+        functools.partial(pack_kernel, experts),
+        out_shape=[pltpu.VMEM((BLOCKS * CAP, width // BLOCKS), BF16)] * experts,
         in_specs=[HBM] * 4,
-        out_specs=[VMEM] * len(rows),
+        out_specs=[VMEM] * experts,
         scratch_shapes=[
             pltpu.VMEM((tokens.shape[0], width), BF16),
             pltpu.VMEM(ids.shape[::-1], jnp.int32),
             pltpu.VMEM(ids.shape[::-1], F32),
-            pltpu.SemaphoreType.DMA((parts + 2,)),
+            pltpu.SemaphoreType.DMA((3,)),
         ],
         name="pack",
         compiler_params=pltpu.CompilerParams(vmem_limit_bytes=16 << 20),
@@ -173,12 +173,26 @@
 
 def join(mine, theirs, x_rows, q_rows):
     first = lax.axis_index("tensor") == 0
-    at = 0
+    width = x_rows.shape[1]
+    cut = width // BLOCKS
+    places = rest_places((BLOCKS * 16, BLOCKS * REST), 1, 0)
+    chunk = 0
     for here, there in zip(mine, theirs):
-        place = pl.ds(at, here.shape[0])
-        x_rows[place, :] = jnp.where(first, here[...], there[...])
-        q_rows[place, :] = jnp.where(first, there[...], here[...])
-        at += here.shape[0]
+        for at in range(0, here.shape[0], BLOCKS * CAP):
+            for block in range(BLOCKS):
+                source = pl.ds(at + block * MAIN, MAIN)
+                target = (pl.ds(chunk * SLOTS, MAIN), pl.ds(block * cut, cut))
+                x_rows[target] = jnp.where(first, here[source, :], there[source, :])
+                q_rows[target] = jnp.where(first, there[source, :], here[source, :])
+            source = pl.ds(at + BLOCKS * MAIN, BLOCKS * REST)
+            here_rest = dot(places, here[source, :]).astype(BF16)
+            there_rest = dot(places, there[source, :]).astype(BF16)
+            for block in range(BLOCKS):
+                rows = slice(block * 16, block * 16 + 16)
+                target = (pl.ds(chunk * SLOTS + MAIN, 16), pl.ds(block * cut, cut))
+                x_rows[target] = jnp.where(first, here_rest[rows], there_rest[rows])
+                q_rows[target] = jnp.where(first, there_rest[rows], here_rest[rows])
+            chunk += 1
 
 
 def activations(x_rows, q_rows, w_gate, w_up, w_down):
@@ -201,7 +215,9 @@
     join(mine, theirs, x_rows, q_rows)
     total = jnp.zeros((1, 128), F32)
     for step in range(experts):
-        total += x_rows[pl.ds(step * SLOTS + CAP, 1), pl.ds(0, 128)].astype(F32)
+        full = x_rows[pl.ds(step * SLOTS, SLOTS), pl.ds(0, 128)].astype(F32) < EMPTY / 2
+        valid = lax.broadcasted_iota(jnp.int32, full.shape, 0) < CAP
+        total += jnp.sum(jnp.where(full & valid, 1.0, 0.0), axis=0, keepdims=True)
     load_out[...] = total / (experts * CAP)
     acts = activations(x_rows, q_rows, w_gate, w_up, w_down)
     cut = frag_out.shape[2]
@@ -265,7 +281,7 @@
     units, width = weights[0].shape
     cut = width // FRAGS
     pieces = len(mine)
-    rows = sum(part.shape[0] for part in mine)
+    rows = sum(part.shape[0] for part in mine) // (BLOCKS * CAP) * SLOTS
     at = 1 + 2 * pieces + 4
     return pl.pallas_call(
         functools.partial(other_kernel, pieces),
@@ -333,8 +349,7 @@
     experts = lax.axis_size("expert")
     replicas = lax.axis_size("replica")
     weights = (gate_proj[0], up_proj[0], down_proj[0])
-    parts = [SLOTS] * experts
-    packed = pack(experts, parts, tokens[0], out_grad[0], expert_ids[0], route_weight[0])
+    packed = pack(experts, tokens[0], out_grad[0], expert_ids[0], route_weight[0])
     if replicas == 2 and experts == 4:
         grads, filled = two_replicas(fragment, packed, weights)
     else:

time: 29.6 us -> 28.9 us (0.976)
  waiting for transfers between devices: 5.91 us -> 5.51 us
  starting transfers between devices: 13.2 us -> 12.8 us
    ppermute x10, starting transfers between devices: 13.2 us -> 12.8 us  [send(): lax.ppermute(array, axis, [(index, peer(index, step, size)) for index in...]
    ppermute x10, waiting for transfers between devices: 5.91 us -> 5.51 us  [send(): lax.ppermute(array, axis, [(index, peer(index, step, size)) for index in...]
  transfers between devices with their start and end apart: 10 -> 10, of which waited for: 4 -> 3; matrix products, arithmetic and copies ran while one was open for 0% -> 0% of each run, Pallas kernels for 18% -> 18%
where the time goes in v4:
time: 28.9 us; the launch traced here: 28.7 us
  starting transfers between devices  12.8 us (44%)
  Pallas kernels  9.09 us (31%)
  waiting for transfers between devices  5.51 us (19%)
  between operations  1.36 us (5%)
    ppermute x10, starting transfers between devices, send(): lax.ppermute(array, axis, [(index, peer(index, step, size)) for index in...  12.8 us
    ppermute x10, waiting for transfers between devices, send(): lax.ppermute(array, axis, [(index, peer(index, step, size)) for index in...  5.51 us
    pallas_call x1, Pallas kernels, own(): pl.pallas_call(functools.partial(own_kernel, experts, pieces), out_shape=...  3.63 us
    pallas_call x1, Pallas kernels, other(): pl.pallas_call(functools.partial(other_kernel, pieces), out_shape=[jax.Sh...  2.24 us
    pallas_call x1, Pallas kernels, load(): pl.pallas_call(functools.partial(load_kernel, count), out_shape=[pltpu.VM...  1.64 us
    pallas_call x1, Pallas kernels, pack(): pl.pallas_call(functools.partial(pack_kernel, experts), out_shape=[pltpu....  1.52 us
  transfers between devices with their start and end apart: 10, of which 3 were waited for; matrix products, arithmetic and copies ran while one was open for 0% of the time, Pallas kernels for 18%

profile of v4, /device:TPU:0, one launch (start us, length us, event | category | flops | bytes accessed | tf_op | source)
XLA Modules:
  0.0 28.7 jit_solution(3816685701968360230)
XLA Ops:
  0.6 1.5 %pack.1 = (bf16[240,256]{1,0:T(8,128)(2,1)S(1)}, bf16[240,256]{1,0:T(8,128)(2,1)S(1)}, bf16[240,256]{1,0:T(8,128)(2,1)S(1)}, bf16[240,256]{1,0:T(8,128)(2,1)S(1)}) custom-call(bf16[240,1024]{1,0:T(8,128)(2,1)} %bitcast.21, bf16[240,1024]{1,0:T(8,128)(2,1)} %bitcast.22, s32[8,240]{1,0:T(8,128)} %bitcast.23, f32[8,240]{1,0:T(8,128)} %bitcast.24), custom_call_target="tpu_custom_call" | custom-call | tf_op jit(solution)/shard_map/pack/pallas_call | solution.py:158
  2.2 5.1 %collective-permute-start = (bf16[240,256]{1,0:T(8,128)(2,1)S(1)}, bf16[240,256]{1,0:T(8,128)(2,1)S(1)}, u32[]{:S(2)}, u32[]{:S(2)}) collective-permute-start(bf16[240,256]{1,0:T(8,128)(2,1)S(1)} %get-tuple-element.30), channel_id=1, source_target_pairs={{0,12},{4,8},{8,4},{12,0},{1,13},{5,9},{9,5},{13,1},{2,14},{6,10},... | collective-permute-start | bytes 368648 | tf_op jit(solution)/shard_map/ppermute | solution.py:304
  7.3 1.5 %collective-permute-start.1 = (bf16[240,256]{1,0:T(8,128)(2,1)S(1)}, bf16[240,256]{1,0:T(8,128)(2,1)S(1)}, u32[]{:S(2)}, u32[]{:S(2)}) collective-permute-start(bf16[240,256]{1,0:T(8,128)(2,1)S(1)} %get-tuple-element.31.refs_4_.refs_0_), channel_id=1, source_target_pairs={{0,2},{2,0},{1,3},{3,1},{4,6},{6,4},{5,7},{7,5},{8,10},{10,8},{9,1... | collective-permute-start | bytes 368648 | tf_op jit(solution)/shard_map/ppermute | solution.py:304
  8.8 0.0 collective-permute-start.5
  8.8 2.0 %collective-permute-start.4 = (bf16[240,256]{1,0:T(8,128)(2,1)S(1)}, bf16[240,256]{1,0:T(8,128)(2,1)S(1)}, u32[]{:S(2)}, u32[]{:S(2)}) collective-permute-start(bf16[240,256]{1,0:T(8,128)(2,1)S(1)} %get-tuple-element.38), channel_id=1, source_target_pairs={{0,4},{4,0},{8,12},{12,8},{1,5},{5,1},{9,13},{13,9},{2,6},{6,2},{1... | collective-permute-start | bytes 368648 | tf_op jit(solution)/shard_map/ppermute | solution.py:304
  10.8 0.0 collective-permute-start.2
  11.4 1.6 %load.1 = (bf16[384,1024]{1,0:T(8,128)(2,1)S(1)}, bf16[384,1024]{1,0:T(8,128)(2,1)S(1)}, bf16[384,1024]{1,0:T(8,128)(2,1)S(1)}) custom-call(bf16[384,1024]{1,0:T(8,128)(2,1)} %bitcast.15, bf16[384,1024]{1,0:T(8,128)(2,1)} %bitcast.16, bf16[384,1024]{1,0:T(8,128)(2,1)} %bitcast.17, s32[1]{0:T(128)S(6)} %copy.18.refs_3_.frag_ref, ...), custom_call_target="tpu_custom_call" | custom-call | tf_op jit(solution)/shard_map/load/pallas_call | solution.py:124
  13.1 0.0 collective-permute-done.refs_2_
  13.1 0.0 collective-permute-done.1.refs_0_
  13.1 2.1 %collective-permute-start.3 = (bf16[240,256]{1,0:T(8,128)(2,1)S(1)}, bf16[240,256]{1,0:T(8,128)(2,1)S(1)}, u32[]{:S(2)}, u32[]{:S(2)}) collective-permute-start(bf16[240,256]{1,0:T(8,128)(2,1)S(1)} %collective-permute-done.refs_2_), channel_id=1, source_target_pairs={{0,2},{2,0},{1,3},{3,1},{4,6},{6,4},{5,7},{7,5},{8,10},{10,8},{9,1... | collective-permute-start | bytes 368648 | tf_op jit(solution)/shard_map/ppermute | solution.py:304
  15.2 3.9 %collective-permute-done.2.refs_3_ = bf16[240,256]{1,0:T(8,128)(2,1)S(1)} collective-permute-done((bf16[240,256]{1,0:T(8,128)(2,1)S(1)}, bf16[240,256]{1,0:T(8,128)(2,1)S(1)}, u32[]{:S(2)}, u32[]{:S(2)}) %collective-permute-start.2) | collective-permute-done | bytes 122912 | tf_op jit(solution)/shard_map/ppermute | solution.py:304
  19.1 0.0 collective-permute-done.5.refs_1_
  19.1 0.0 collective-permute-done.4.refs_1_
  19.1 0.0 collective-permute-done.3.refs_2_
  19.2 0.1 collective-permute-start.7
  19.3 0.6 %collective-permute-start.8 = (bf16[720,256]{1,0:T(8,128)(2,1)S(1)}, bf16[720,256]{1,0:T(8,128)(2,1)S(1)}, u32[]{:S(2)}, u32[]{:S(2)}) collective-permute-start(bf16[720,256]{1,0:T(8,128)(2,1)S(1)} %stack.2.refs_0_), channel_id=1, source_target_pairs={{0,1},{1,0},{2,3},{3,2},{4,5},{5,4},{6,7},{7,6},{8,9},{9,8},{10,11... | collective-permute-start | bytes 1105928 | tf_op jit(solution)/shard_map/ppermute | solution.py:304
  19.8 1.4 %collective-permute-start.6 = (bf16[240,256]{1,0:T(8,128)(2,1)S(1)}, bf16[240,256]{1,0:T(8,128)(2,1)S(1)}, u32[]{:S(2)}, u32[]{:S(2)}) collective-permute-start(bf16[240,256]{1,0:T(8,128)(2,1)S(1)} %collective-permute-done.2.refs_3_), channel_id=1, source_target_pairs={{0,2},{2,0},{1,3},{3,1},{4,6},{6,4},{5,7},{7,5},{8,10},{10,8},{9,1... | collective-permute-start | bytes 368648 | tf_op jit(solution)/shard_map/ppermute | solution.py:304
  21.3 0.0 collective-permute-done.7.refs_1_
  21.3 3.6 %own.1 = (bf16[384,1024]{1,0:T(8,128)(2,1)}, bf16[384,1024]{1,0:T(8,128)(2,1)}, bf16[384,1024]{1,0:T(8,128)(2,1)}, f32[3,384,256]{2,1,0:T(8,128)S(1)}, f32[1,128]{1,0:T(1,128)}) custom-call(s32[1]{0:T(128)S(6)} %copy.18.refs_3_.frag_ref, bf16[960,256]{1,0:T(8,128)(2,1)S(1)} %stack.3.refs_0_, bf16[960,256]{1,0:T(8,128)(2,1)S(1)} %collective-permute-done.7.refs_1_, ...), custom_call_target="tpu_custom_call" | custom-call | flops 1207959552 | bytes 4718592 | tf_op jit(solution)/shard_map/own/pallas_call | solution.py:242
  24.9 0.3 collective-permute-done.6.refs_1_
  25.2 0.0 collective-permute-start.9
  25.2 0.0 collective-permute-done.8.refs_2_
  25.2 1.3 %collective-permute-done.9.refs_3_ = bf16[240,256]{1,0:T(8,128)(2,1)S(1)} collective-permute-done((bf16[240,256]{1,0:T(8,128)(2,1)S(1)}, bf16[240,256]{1,0:T(8,128)(2,1)S(1)}, u32[]{:S(2)}, u32[]{:S(2)}) %collective-permute-start.9) | collective-permute-done | bytes 122912 | tf_op jit(solution)/shard_map/ppermute | solution.py:304
  26.5 2.2 %other.1 = (bf16[384,1024]{1,0:T(8,128)(2,1)}, bf16[384,1024]{1,0:T(8,128)(2,1)}, bf16[384,1024]{1,0:T(8,128)(2,1)}) custom-call(s32[1]{0:T(128)S(6)} %copy.18.refs_3_.frag_ref, bf16[720,256]{1,0:T(8,128)(2,1)S(1)} %stack.2.refs_0_, ...), custom_call_target="tpu_custom_call", output_to_operand_aliasing={{0}: (9, {}), {1}: (10, {}), {2}: (11, {})} | custom-call | flops 805306368 | bytes 3145728 | tf_op jit(solution)/shard_map/other/pallas_call | solution.py:286
  (2 shorter events, 0.1 us)
Async XLA Ops:
  2.2 10.9 %collective-permute-start = (bf16[240,256]{1,0:T(8,128)(2,1)S(1)}, bf16[240,256]{1,0:T(8,128)(2,1)S(1)}, u32[]{:S(2)}, u32[]{:S(2)}) collective-permute-start(bf16[240,256]{1,0:T(8,128)(2,1)S(1)} %get-tuple-element.30), channel_id=1, source_target_pairs={{0,12},{4,8},{8,4},{12,0},{1,13},{5,9},{9,5},{13,1},{2,14},{6,10},... | collective-permute-start | bytes 368648 | tf_op jit(solution)/shard_map/ppermute | solution.py:304
  7.3 5.8 %collective-permute-start.1 = (bf16[240,256]{1,0:T(8,128)(2,1)S(1)}, bf16[240,256]{1,0:T(8,128)(2,1)S(1)}, u32[]{:S(2)}, u32[]{:S(2)}) collective-permute-start(bf16[240,256]{1,0:T(8,128)(2,1)S(1)} %get-tuple-element.31.refs_4_.refs_0_), channel_id=1, source_target_pairs={{0,2},{2,0},{1,3},{3,1},{4,6},{6,4},{5,7},{7,5},{8,10},{10,8},{9,1... | collective-permute-start | bytes 368648 | tf_op jit(solution)/shard_map/ppermute | solution.py:304
  8.8 10.4 %collective-permute-start.5 = (bf16[240,256]{1,0:T(8,128)(2,1)S(1)}, bf16[240,256]{1,0:T(8,128)(2,1)S(1)}, u32[]{:S(2)}, u32[]{:S(2)}) collective-permute-start(bf16[240,256]{1,0:T(8,128)(2,1)S(1)} %get-tuple-element.38), channel_id=1, source_target_pairs={{0,6},{2,4},{4,2},{6,0},{8,14},{10,12},{12,10},{14,8},{1,7},{3,5},... | collective-permute-start | bytes 368648 | tf_op jit(solution)/shard_map/ppermute | solution.py:304
  8.8 10.4 %collective-permute-start.4 = (bf16[240,256]{1,0:T(8,128)(2,1)S(1)}, bf16[240,256]{1,0:T(8,128)(2,1)S(1)}, u32[]{:S(2)}, u32[]{:S(2)}) collective-permute-start(bf16[240,256]{1,0:T(8,128)(2,1)S(1)} %get-tuple-element.38), channel_id=1, source_target_pairs={{0,4},{4,0},{8,12},{12,8},{1,5},{5,1},{9,13},{13,9},{2,6},{6,2},{1... | collective-permute-start | bytes 368648 | tf_op jit(solution)/shard_map/ppermute | solution.py:304
  10.8 8.4 %collective-permute-start.2 = (bf16[240,256]{1,0:T(8,128)(2,1)S(1)}, bf16[240,256]{1,0:T(8,128)(2,1)S(1)}, u32[]{:S(2)}, u32[]{:S(2)}) collective-permute-start(bf16[240,256]{1,0:T(8,128)(2,1)S(1)} %get-tuple-element.36), channel_id=1, source_target_pairs={{0,8},{4,12},{8,0},{12,4},{1,9},{5,13},{9,1},{13,5},{2,10},{6,14},... | collective-permute-start | bytes 368648 | tf_op jit(solution)/shard_map/ppermute | solution.py:304
  13.1 6.0 %collective-permute-start.3 = (bf16[240,256]{1,0:T(8,128)(2,1)S(1)}, bf16[240,256]{1,0:T(8,128)(2,1)S(1)}, u32[]{:S(2)}, u32[]{:S(2)}) collective-permute-start(bf16[240,256]{1,0:T(8,128)(2,1)S(1)} %collective-permute-done.refs_2_), channel_id=1, source_target_pairs={{0,2},{2,0},{1,3},{3,1},{4,6},{6,4},{5,7},{7,5},{8,10},{10,8},{9,1... | collective-permute-start | bytes 368648 | tf_op jit(solution)/shard_map/ppermute | solution.py:304
  19.2 2.1 %collective-permute-start.7 = (bf16[960,256]{1,0:T(8,128)(2,1)S(1)}, bf16[960,256]{1,0:T(8,128)(2,1)S(1)}, u32[]{:S(2)}, u32[]{:S(2)}) collective-permute-start(bf16[960,256]{1,0:T(8,128)(2,1)S(1)} %stack.3.refs_0_), channel_id=1, source_target_pairs={{0,1},{1,0},{2,3},{3,2},{4,5},{5,4},{6,7},{7,6},{8,9},{9,8},{10,11... | collective-permute-start | bytes 1474568 | tf_op jit(solution)/shard_map/ppermute | solution.py:304
  19.3 5.9 %collective-permute-start.8 = (bf16[720,256]{1,0:T(8,128)(2,1)S(1)}, bf16[720,256]{1,0:T(8,128)(2,1)S(1)}, u32[]{:S(2)}, u32[]{:S(2)}) collective-permute-start(bf16[720,256]{1,0:T(8,128)(2,1)S(1)} %stack.2.refs_0_), channel_id=1, source_target_pairs={{0,1},{1,0},{2,3},{3,2},{4,5},{5,4},{6,7},{7,6},{8,9},{9,8},{10,11... | collective-permute-start | bytes 1105928 | tf_op jit(solution)/shard_map/ppermute | solution.py:304
  19.8 5.3 %collective-permute-start.6 = (bf16[240,256]{1,0:T(8,128)(2,1)S(1)}, bf16[240,256]{1,0:T(8,128)(2,1)S(1)}, u32[]{:S(2)}, u32[]{:S(2)}) collective-permute-start(bf16[240,256]{1,0:T(8,128)(2,1)S(1)} %collective-permute-done.2.refs_3_), channel_id=1, source_target_pairs={{0,2},{2,0},{1,3},{3,1},{4,6},{6,4},{5,7},{7,5},{8,10},{10,8},{9,1... | collective-permute-start | bytes 368648 | tf_op jit(solution)/shard_map/ppermute | solution.py:304
  25.2 1.3 %collective-permute-start.9 = (bf16[240,256]{1,0:T(8,128)(2,1)S(1)}, bf16[240,256]{1,0:T(8,128)(2,1)S(1)}, u32[]{:S(2)}, u32[]{:S(2)}) collective-permute-start(bf16[240,256]{1,0:T(8,128)(2,1)S(1)} %collective-permute-done.6.refs_1_), channel_id=1, source_target_pairs={{0,1},{1,0},{2,3},{3,2},{4,5},{5,4},{6,7},{7,6},{8,9},{9,8},{10,11... | collective-permute-start | bytes 368648 | tf_op jit(solution)/shard_map/ppermute | solution.py:304

commit v5 on v4

--- a/solution.py
+++ b/solution.py
@@ -94,6 +94,9 @@
     for step in range(experts):
         rest = dot(places, jnp.concatenate(rests[step::experts], axis=0))
         out_refs[step][pl.ds(BLOCKS * MAIN, BLOCKS * REST), :] = rest.astype(BF16)
+        more = out_refs[step].shape[0] - BLOCKS * CAP
+        if more:
+            out_refs[step][pl.ds(BLOCKS * CAP, more), :] = jnp.zeros((more, cut), BF16)
 
 
 def rest_places(shape, wire, block):
@@ -134,14 +137,12 @@
 
 def stack_kernel(*refs):
     *parts, whole = refs
-    at = 0
-    for part in parts:
-        whole[pl.ds(at, part.shape[0]), :] = part[...]
-        at += part.shape[0]
+    for step, part in enumerate(parts):
+        whole[pl.ds(step * BLOCKS * CAP, BLOCKS * CAP), :] = part[pl.ds(0, BLOCKS * CAP), :]
 
 
 def stack(parts):
-    rows = sum(part.shape[0] for part in parts)
+    rows = len(parts) * BLOCKS * CAP
     return pl.pallas_call(
         stack_kernel,
         out_shape=pltpu.VMEM((rows, parts[0].shape[1]), parts[0].dtype),
@@ -152,14 +153,14 @@
     )(*parts)
 
 
-def pack(experts, tokens, out_grad, ids, weight):
+def pack(rows, tokens, out_grad, ids, weight):
     width = tokens.shape[1]
     inputs = [in_hbm(array) for array in (tokens, out_grad, ids.T, weight.T)]
     return pl.pallas_call(
-        functools.partial(pack_kernel, experts),
-        out_shape=[pltpu.VMEM((BLOCKS * CAP, width // BLOCKS), BF16)] * experts,
+        functools.partial(pack_kernel, len(rows)),
+        out_shape=[pltpu.VMEM((count, width // BLOCKS), BF16) for count in rows],
         in_specs=[HBM] * 4,
-        out_specs=[VMEM] * experts,
+        out_specs=[VMEM] * len(rows),
         scratch_shapes=[
             pltpu.VMEM((tokens.shape[0], width), BF16),
             pltpu.VMEM(ids.shape[::-1], jnp.int32),
@@ -171,28 +172,27 @@
     )(*inputs)
 
 
-def join(mine, theirs, x_rows, q_rows):
+def join(parts, x_rows, q_rows):
     first = lax.axis_index("tensor") == 0
-    width = x_rows.shape[1]
-    cut = width // BLOCKS
+    cut = x_rows.shape[1] // BLOCKS
     places = rest_places((BLOCKS * 16, BLOCKS * REST), 1, 0)
-    chunk = 0
-    for here, there in zip(mine, theirs):
-        for at in range(0, here.shape[0], BLOCKS * CAP):
+    row = 0
+    for here, there, begin, count in parts:
+        for at in range(begin * BLOCKS * CAP, (begin + count) * BLOCKS * CAP, BLOCKS * CAP):
             for block in range(BLOCKS):
                 source = pl.ds(at + block * MAIN, MAIN)
-                target = (pl.ds(chunk * SLOTS, MAIN), pl.ds(block * cut, cut))
+                target = (pl.ds(row, MAIN), pl.ds(block * cut, cut))
                 x_rows[target] = jnp.where(first, here[source, :], there[source, :])
                 q_rows[target] = jnp.where(first, there[source, :], here[source, :])
             source = pl.ds(at + BLOCKS * MAIN, BLOCKS * REST)
             here_rest = dot(places, here[source, :]).astype(BF16)
             there_rest = dot(places, there[source, :]).astype(BF16)
             for block in range(BLOCKS):
-                rows = slice(block * 16, block * 16 + 16)
-                target = (pl.ds(chunk * SLOTS + MAIN, 16), pl.ds(block * cut, cut))
-                x_rows[target] = jnp.where(first, here_rest[rows], there_rest[rows])
-                q_rows[target] = jnp.where(first, there_rest[rows], here_rest[rows])
-            chunk += 1
+                rest = slice(block * 16, block * 16 + 16)
+                target = (pl.ds(row + MAIN, 16), pl.ds(block * cut, cut))
+                x_rows[target] = jnp.where(first, here_rest[rest], there_rest[rest])
+                q_rows[target] = jnp.where(first, there_rest[rest], here_rest[rest])
+            row += SLOTS
 
 
 def activations(x_rows, q_rows, w_gate, w_up, w_down):
@@ -207,12 +207,9 @@
     return gate_grad, up_grad, hidden
 
 
-def own_kernel(experts, pieces, frag_ref, *refs):
-    mine, theirs = refs[:pieces], refs[pieces : 2 * pieces]
-    w_gate, w_up, w_down = refs[2 * pieces : 2 * pieces + 3]
-    outs = refs[2 * pieces + 3 : 2 * pieces + 6]
-    frag_out, load_out, x_rows, q_rows, stage, sems = refs[2 * pieces + 6 :]
-    join(mine, theirs, x_rows, q_rows)
+def own_kernel(experts, frag_ref, mine, theirs, w_gate, w_up, w_down, *refs):
+    grads, frag_out, load_out, x_rows, q_rows = refs
+    join([(mine, theirs, 0, experts)], x_rows, q_rows)
     total = jnp.zeros((1, 128), F32)
     for step in range(experts):
         full = x_rows[pl.ds(step * SLOTS, SLOTS), pl.ds(0, 128)].astype(F32) < EMPTY / 2
@@ -222,81 +219,84 @@
     acts = activations(x_rows, q_rows, w_gate, w_up, w_down)
     cut = frag_out.shape[2]
     frag_columns = pl.ds(pl.multiple_of(frag_ref[0] * cut, cut), cut)
-    copies = []
-    for piece, (act, rows, out) in enumerate(zip(acts, (x_rows, x_rows, q_rows), outs)):
-        for at in range(FRAGS):
-            columns = pl.ds(at * cut, cut)
-            stage[piece, :, columns] = dot(act, rows[:, columns]).astype(BF16)
-        copies.append(pltpu.make_async_copy(stage.at[piece], out, sems.at[piece]))
-        copies[-1].start()
     for piece, (act, rows) in enumerate(zip(acts, (x_rows, x_rows, q_rows))):
+        grads[piece] = dot(act, rows[...]).astype(BF16)
         frag_out[piece] = dot(act, rows[:, frag_columns])
-    for copy in copies:
-        copy.wait()
 
 
 def own(experts, fragment, mine, theirs, weights):
     units, width = weights[0].shape
     cut = width // FRAGS
-    pieces = len(mine)
-    return pl.pallas_call(
-        functools.partial(own_kernel, experts, pieces),
-        out_shape=[jax.ShapeDtypeStruct((units, width), BF16)] * 3
-        + [pltpu.VMEM((3, units, cut), F32), jax.ShapeDtypeStruct((1, 128), F32)],
-        in_specs=[SMEM] + [VMEM] * (2 * pieces + 3),
-        out_specs=[HBM] * 3 + [VMEM] * 2,
-        scratch_shapes=[pltpu.VMEM((experts * SLOTS, width), BF16)] * 2
-        + [pltpu.VMEM((3, units, width), BF16), pltpu.SemaphoreType.DMA((3,))],
+    rows = experts * SLOTS
+    return pl.pallas_call(
+        functools.partial(own_kernel, experts),
+        out_shape=[
+            pltpu.VMEM((3, units, width), BF16),
+            pltpu.VMEM((3, units, cut), F32),
+            jax.ShapeDtypeStruct((1, 128), F32),
+        ],
+        in_specs=[SMEM] + [VMEM] * 5,
+        out_specs=[VMEM] * 3,
+        scratch_shapes=[pltpu.VMEM((rows, width), BF16)] * 2,
         name="own",
-        compiler_params=pltpu.CompilerParams(vmem_limit_bytes=32 << 20),
+        compiler_params=pltpu.CompilerParams(vmem_limit_bytes=24 << 20),
         cost_estimate=pl.CostEstimate(
-            flops=12 * units * width * experts * SLOTS, bytes_accessed=12 * units * width, transcendentals=0
+            flops=12 * units * width * rows, bytes_accessed=12 * units * width, transcendentals=0
         ),
-    )(fragment, *mine, *theirs, *weights)
-
-
-def other_kernel(pieces, frag_ref, *refs):
+    )(fragment, mine, theirs, *weights)
+
+
+def other_kernel(ranges, frag_ref, *refs):
+    pieces = len(ranges)
     mine, theirs = refs[:pieces], refs[pieces : 2 * pieces]
-    w_gate, w_up, w_down = refs[2 * pieces : 2 * pieces + 3]
-    frag_in = refs[2 * pieces + 3]
-    outs = refs[2 * pieces + 7 : 2 * pieces + 10]
-    x_rows, q_rows, cuts, sems = refs[2 * pieces + 10 :]
-    join(mine, theirs, x_rows, q_rows)
+    w_gate, w_up, w_down, grads, frag_in = refs[2 * pieces : 2 * pieces + 5]
+    outs = refs[2 * pieces + 5 : 2 * pieces + 8]
+    x_rows, q_rows, cuts, sems = refs[2 * pieces + 8 :]
+    cut = frag_in.shape[2]
+    frag = frag_ref[0]
+    copies = []
+    for piece, out in enumerate(outs):
+        for step in range(1, FRAGS):
+            block = lax.rem(frag + step, FRAGS)
+            columns = pl.ds(pl.multiple_of(block * cut, cut), cut)
+            copies.append(
+                pltpu.make_async_copy(
+                    grads.at[piece, :, columns], out.at[:, columns], sems.at[piece, step]
+                )
+            )
+            copies[-1].start()
+    join([(*pair, *span) for *pair, span in zip(mine, theirs, ranges)], x_rows, q_rows)
     acts = activations(x_rows, q_rows, w_gate, w_up, w_down)
-    cut = frag_in.shape[2]
-    columns = pl.ds(pl.multiple_of(frag_ref[0] * cut, cut), cut)
-    copies = []
+    columns = pl.ds(pl.multiple_of(frag * cut, cut), cut)
     for piece, (act, rows) in enumerate(zip(acts, (x_rows, x_rows, q_rows))):
         grad = dot(act, rows[:, columns])
         cuts[piece] = ((frag_in[piece] + grad) * 0.5).astype(BF16)
         copies.append(
-            pltpu.make_async_copy(cuts.at[piece], outs[piece].at[:, columns], sems.at[piece])
+            pltpu.make_async_copy(cuts.at[piece], outs[piece].at[:, columns], sems.at[piece, 0])
         )
         copies[-1].start()
     for copy in copies:
         copy.wait()
 
 
-def other(fragment, mine, theirs, weights, frag_grad, grads):
+def other(fragment, mine, theirs, ranges, weights, grads, frag_grad):
     units, width = weights[0].shape
     cut = width // FRAGS
     pieces = len(mine)
-    rows = sum(part.shape[0] for part in mine) // (BLOCKS * CAP) * SLOTS
-    at = 1 + 2 * pieces + 4
-    return pl.pallas_call(
-        functools.partial(other_kernel, pieces),
+    rows = sum(count for _, count in ranges) * SLOTS
+    return pl.pallas_call(
+        functools.partial(other_kernel, ranges),
         out_shape=[jax.ShapeDtypeStruct((units, width), BF16)] * 3,
-        in_specs=[SMEM] + [VMEM] * (2 * pieces + 4) + [ANY] * 3,
-        out_specs=[ANY] * 3,
+        in_specs=[SMEM] + [VMEM] * (2 * pieces + 5),
+        out_specs=[HBM] * 3,
         scratch_shapes=[pltpu.VMEM((rows, width), BF16)] * 2
-        + [pltpu.VMEM((3, units, cut), BF16), pltpu.SemaphoreType.DMA((3,))],
-        input_output_aliases={at: 0, at + 1: 1, at + 2: 2},
+        + [pltpu.VMEM((3, units, cut), BF16), pltpu.SemaphoreType.DMA((3, FRAGS))],
         name="other",
-        compiler_params=pltpu.CompilerParams(vmem_limit_bytes=32 << 20),
+        compiler_params=pltpu.CompilerParams(vmem_limit_bytes=24 << 20),
         cost_estimate=pl.CostEstimate(
             flops=8 * units * width * rows, bytes_accessed=8 * units * width, transcendentals=0
         ),
-    )(fragment, *mine, *theirs, *weights, frag_grad, *grads)
+    )(fragment, *mine, *theirs, *weights, grads, frag_grad)
 
 
 def send(array, axis, step):
@@ -316,28 +316,26 @@
     x1 = send(packed[1], ("expert", "replica"), 3)
     r2 = send(packed[2], "expert", 2)
     weights = load(weights, fragment, r0)
-    r3, x0, *weights = tie(r3, x0, *weights)
+    r3, *weights = tie(r3, *weights)
     x3 = send(r3, "replica", 1)
-    r2, x3, r1, x1 = tie(r2, x3, r1, x1)
     x2 = send(r2, "replica", 1)
-    near = stack([r0, r1, r3, r2])
+    r1, x1, x3, x0 = tie(r1, x1, x3, x0)
+    near = stack([r0, r1, r2, r3])
     c0 = send(near, "tensor", 1)
-    far = stack([x0, x1, x3])
+    far = stack([x0, x1, x2, x3])
     f0 = send(far, "tensor", 1)
-    mine, theirs = [near], [c0]
-    *grads, frag_grad, filled = own(4, fragment, mine, theirs, weights)
-    x2, filled = tie(x2, filled)
-    f3 = send(x2, "tensor", 1)
-    grads = other(fragment, [far, x2], [f0, f3], weights, frag_grad, grads)
+    grads, frag_grad, filled = own(4, fragment, near, c0, weights)
+    grads = other(fragment, [far], [f0], [(0, 4)], weights, grads, frag_grad)
     return grads, filled
 
 
 def any_replicas(experts, replicas, fragment, packed, weights):
     mine = [packed[0]] + [send(packed[step], "expert", step) for step in range(1, experts)]
-    theirs = [send(rows, "tensor", 1) for rows in mine]
-    *grads, frag_grad, filled = own(experts, fragment, mine, theirs, weights)
+    mine = stack(mine)
+    theirs = send(mine, "tensor", 1)
+    grads, frag_grad, filled = own(experts, fragment, mine, theirs, weights)
     synced = lax.psum(frag_grad.astype(BF16), "replica").astype(F32)
-    begin = fragment[0] * (weights[0].shape[1] // FRAGS)
+    begin = fragment[0] * synced.shape[2]
     grads = [
         lax.dynamic_update_slice_in_dim(grad, (piece / replicas).astype(BF16), begin, 1)
         for grad, piece in zip(grads, synced)
@@ -349,7 +347,10 @@
     experts = lax.axis_size("expert")
     replicas = lax.axis_size("replica")
     weights = (gate_proj[0], up_proj[0], down_proj[0])
-    packed = pack(experts, tokens[0], out_grad[0], expert_ids[0], route_weight[0])
+    rows = [BLOCKS * CAP] * experts
+    if replicas == 2 and experts == 4:
+        rows[2] += 16
+    packed = pack(rows, tokens[0], out_grad[0], expert_ids[0], route_weight[0])
     if replicas == 2 and experts == 4:
         grads, filled = two_replicas(fragment, packed, weights)
     else:

time: 28.9 us -> 28.3 us (0.979)
  waiting for transfers between devices: 5.51 us -> 6.82 us
  starting transfers between devices: 12.8 us -> 11.8 us
  Pallas kernels: 9.09 us -> 8.1 us
    ppermute x10 -> x9, waiting for transfers between devices: 5.51 us -> 6.82 us  [send(): lax.ppermute(array, axis, [(index, peer(index, step, size)) for index in...]
    pallas_call x3, Pallas kernels: 7.39 us -> 6.4 us  [the longest x1 2.71 us: other(): pl.pallas_call(functools.partial(other_kernel, ranges), out_shape=[jax.Sh...]
    ppermute x10 -> x9, starting transfers between devices: 12.8 us -> 11.8 us  [send(): lax.ppermute(array, axis, [(index, peer(index, step, size)) for index in...]
  transfers between devices with their start and end apart: 10 -> 9, of which waited for: 3 -> 2; matrix products, arithmetic and copies ran while one was open for 0% -> 0% of each run, Pallas kernels for 18% -> 14%
where the time goes in v5:
time: 28.3 us; the launch traced here: 28.1 us
  starting transfers between devices  11.8 us (42%)
  Pallas kernels  8.1 us (29%)
  waiting for transfers between devices  6.82 us (24%)
  between operations  1.37 us (5%)
    ppermute x9, starting transfers between devices, send(): lax.ppermute(array, axis, [(index, peer(index, step, size)) for index in...  11.8 us
    ppermute x9, waiting for transfers between devices, send(): lax.ppermute(array, axis, [(index, peer(index, step, size)) for index in...  6.82 us
    pallas_call x1, Pallas kernels, other(): pl.pallas_call(functools.partial(other_kernel, ranges), out_shape=[jax.Sh...  2.71 us
    pallas_call x1, Pallas kernels, own(): pl.pallas_call(functools.partial(own_kernel, experts), out_shape=[pltpu.V...  2.17 us
    pallas_call x1, Pallas kernels, load(): pl.pallas_call(functools.partial(load_kernel, count), out_shape=[pltpu.VM...  1.64 us
    pallas_call x1, Pallas kernels, pack(): pl.pallas_call(functools.partial(pack_kernel, len(rows)), out_shape=[pltp...  1.52 us
  transfers between devices with their start and end apart: 9, of which 2 were waited for; matrix products, arithmetic and copies ran while one was open for 0% of the time, Pallas kernels for 14%

profile of v5, /device:TPU:0, one launch (start us, length us, event | category | flops | bytes accessed | tf_op | source)
XLA Modules:
  0.0 28.1 jit_solution(2118554116685889637)
XLA Ops:
  0.6 1.5 %pack.1 = (bf16[240,256]{1,0:T(8,128)(2,1)S(1)}, bf16[240,256]{1,0:T(8,128)(2,1)S(1)}, bf16[256,256]{1,0:T(8,128)(2,1)S(1)}, bf16[240,256]{1,0:T(8,128)(2,1)S(1)}) custom-call(bf16[240,1024]{1,0:T(8,128)(2,1)} %bitcast.18, bf16[240,1024]{1,0:T(8,128)(2,1)} %bitcast.19, s32[8,240]{1,0:T(8,128)} %bitcast.20, f32[8,240]{1,0:T(8,128)} %bitcast.21), custom_call_target="tpu_custom_call" | custom-call | tf_op jit(solution)/shard_map/pack/pallas_call | solution.py:159
  2.2 5.1 %collective-permute-start.2 = (bf16[240,256]{1,0:T(8,128)(2,1)S(1)}, bf16[240,256]{1,0:T(8,128)(2,1)S(1)}, u32[]{:S(2)}, u32[]{:S(2)}) collective-permute-start(bf16[240,256]{1,0:T(8,128)(2,1)S(1)} %get-tuple-element.26), channel_id=1, source_target_pairs={{0,12},{4,8},{8,4},{12,0},{1,13},{5,9},{9,5},{13,1},{2,14},{6,10},... | collective-permute-start | bytes 368648 | tf_op jit(solution)/shard_map/ppermute | solution.py:304
  7.3 0.0 collective-permute-start.5
  7.3 1.7 %collective-permute-start.1 = (bf16[240,256]{1,0:T(8,128)(2,1)S(1)}, bf16[240,256]{1,0:T(8,128)(2,1)S(1)}, u32[]{:S(2)}, u32[]{:S(2)}) collective-permute-start(bf16[240,256]{1,0:T(8,128)(2,1)S(1)} %get-tuple-element.25), channel_id=1, source_target_pairs={{0,6},{2,4},{4,2},{6,0},{8,14},{10,12},{12,10},{14,8},{1,7},{3,5},... | collective-permute-start | bytes 368648 | tf_op jit(solution)/shard_map/ppermute | solution.py:304
  9.0 1.2 %collective-permute-start = (bf16[240,256]{1,0:T(8,128)(2,1)S(1)}, bf16[240,256]{1,0:T(8,128)(2,1)S(1)}, u32[]{:S(2)}, u32[]{:S(2)}) collective-permute-start(bf16[240,256]{1,0:T(8,128)(2,1)S(1)} %get-tuple-element.25), channel_id=1, source_target_pairs={{0,4},{4,0},{8,12},{12,8},{1,5},{5,1},{9,13},{13,9},{2,6},{6,2},{1... | collective-permute-start | bytes 368648 | tf_op jit(solution)/shard_map/ppermute | solution.py:304
  10.2 0.5 %collective-permute-start.4 = (bf16[240,256]{1,0:T(8,128)(2,1)S(1)}, bf16[240,256]{1,0:T(8,128)(2,1)S(1)}, u32[]{:S(2)}, u32[]{:S(2)}) collective-permute-start(bf16[240,256]{1,0:T(8,128)(2,1)S(1)} %get-tuple-element.27.refs_4_.refs_0_), channel_id=1, source_target_pairs={{0,2},{2,0},{1,3},{3,1},{4,6},{6,4},{5,7},{7,5},{8,10},{10,8},{9,1... | collective-permute-start | bytes 368648 | tf_op jit(solution)/shard_map/ppermute | solution.py:304
  11.4 1.6 %load.1 = (bf16[384,1024]{1,0:T(8,128)(2,1)S(1)}, bf16[384,1024]{1,0:T(8,128)(2,1)S(1)}, bf16[384,1024]{1,0:T(8,128)(2,1)S(1)}) custom-call(bf16[384,1024]{1,0:T(8,128)(2,1)} %bitcast.15, bf16[384,1024]{1,0:T(8,128)(2,1)} %bitcast.16, bf16[384,1024]{1,0:T(8,128)(2,1)} %bitcast.17, s32[1]{0:T(128)S(6)} %copy.12.refs_3_.frag_ref, ...), custom_call_target="tpu_custom_call" | custom-call | tf_op jit(solution)/shard_map/load/pallas_call | solution.py:127
  13.1 0.0 collective-permute-done.2.refs_3_
  13.1 1.6 %collective-permute-start.3 = (bf16[240,256]{1,0:T(8,128)(2,1)S(1)}, bf16[240,256]{1,0:T(8,128)(2,1)S(1)}, u32[]{:S(2)}, u32[]{:S(2)}) collective-permute-start(bf16[240,256]{1,0:T(8,128)(2,1)S(1)} %collective-permute-done.2.refs_3_), channel_id=1, source_target_pairs={{0,2},{2,0},{1,3},{3,1},{4,6},{6,4},{5,7},{7,5},{8,10},{10,8},{9,1... | collective-permute-start | bytes 368648 | tf_op jit(solution)/shard_map/ppermute | solution.py:304
  14.6 3.5 %collective-permute-done.5.refs_2_ = bf16[256,256]{1,0:T(8,128)(2,1)S(1)} collective-permute-done((bf16[256,256]{1,0:T(8,128)(2,1)S(1)}, bf16[256,256]{1,0:T(8,128)(2,1)S(1)}, u32[]{:S(2)}, u32[]{:S(2)}) %collective-permute-start.5) | collective-permute-done | bytes 131104 | tf_op jit(solution)/shard_map/ppermute | solution.py:304
  18.1 1.5 %collective-permute-start.6 = (bf16[256,256]{1,0:T(8,128)(2,1)S(1)}, bf16[256,256]{1,0:T(8,128)(2,1)S(1)}, u32[]{:S(2)}, u32[]{:S(2)}) collective-permute-start(bf16[256,256]{1,0:T(8,128)(2,1)S(1)} %collective-permute-done.5.refs_2_), channel_id=1, source_target_pairs={{0,2},{2,0},{1,3},{3,1},{4,6},{6,4},{5,7},{7,5},{8,10},{10,8},{9,1... | collective-permute-start | bytes 393224 | tf_op jit(solution)/shard_map/ppermute | solution.py:304
  19.6 0.0 collective-permute-done.1.refs_1_
  19.6 0.0 collective-permute-done.refs_1_
  19.6 0.0 collective-permute-done.4.refs_0_
  19.6 0.0 collective-permute-done.3.refs_3_
  19.7 0.1 collective-permute-start.8
  19.7 3.3 %collective-permute-done.6.refs_2_ = bf16[256,256]{1,0:T(8,128)(2,1)S(1)} collective-permute-done((bf16[256,256]{1,0:T(8,128)(2,1)S(1)}, bf16[256,256]{1,0:T(8,128)(2,1)S(1)}, u32[]{:S(2)}, u32[]{:S(2)}) %collective-permute-start.6) | collective-permute-done | bytes 131104 | tf_op jit(solution)/shard_map/ppermute | solution.py:304
  23.1 0.1 collective-permute-start.7
  23.2 0.0 collective-permute-done.8.theirs
  23.2 2.2 %own.1 = (bf16[3,384,1024]{2,1,0:T(8,128)(2,1)S(1)}, f32[3,384,256]{2,1,0:T(8,128)S(1)}, f32[1,128]{1,0:T(1,128)}) custom-call(s32[1]{0:T(128)S(6)} %copy.12.refs_3_.frag_ref, bf16[960,256]{1,0:T(8,128)(2,1)S(1)} %stack.3.mine, bf16[960,256]{1,0:T(8,128)(2,1)S(1)} %collective-permute-done.8.theirs, bf16[384,1024]{1,0:T(8,128)(2,1)S(1)} %get-tuple-element.36.w_gate.refs_2_, ...), custom_call_target="tpu_custom_call" | custom-call | flops 1207959552 | bytes 4718592 | tf_op jit(solution)/shard_map/own/pallas_call | solution.py:231
  25.4 0.0 collective-permute-done.7.refs_1_
  25.4 2.7 %other.1 = (bf16[384,1024]{1,0:T(8,128)(2,1)}, bf16[384,1024]{1,0:T(8,128)(2,1)}, bf16[384,1024]{1,0:T(8,128)(2,1)}) custom-call(s32[1]{0:T(128)S(6)} %copy.12.refs_3_.frag_ref, bf16[960,256]{1,0:T(8,128)(2,1)S(1)} %stack.2.refs_0_, bf16[960,256]{1,0:T(8,128)(2,1)S(1)} %collective-permute-done.7.refs_1_, ...), custom_call_target="tpu_custom_call" | custom-call | flops 805306368 | bytes 3145728 | tf_op jit(solution)/shard_map/other/pallas_call | solution.py:287
  (2 shorter events, 0.1 us)
Async XLA Ops:
  2.2 10.9 %collective-permute-start.2 = (bf16[240,256]{1,0:T(8,128)(2,1)S(1)}, bf16[240,256]{1,0:T(8,128)(2,1)S(1)}, u32[]{:S(2)}, u32[]{:S(2)}) collective-permute-start(bf16[240,256]{1,0:T(8,128)(2,1)S(1)} %get-tuple-element.26), channel_id=1, source_target_pairs={{0,12},{4,8},{8,4},{12,0},{1,13},{5,9},{9,5},{13,1},{2,14},{6,10},... | collective-permute-start | bytes 368648 | tf_op jit(solution)/shard_map/ppermute | solution.py:304
  7.3 10.8 %collective-permute-start.5 = (bf16[256,256]{1,0:T(8,128)(2,1)S(1)}, bf16[256,256]{1,0:T(8,128)(2,1)S(1)}, u32[]{:S(2)}, u32[]{:S(2)}) collective-permute-start(bf16[256,256]{1,0:T(8,128)(2,1)S(1)} %get-tuple-element.34), channel_id=1, source_target_pairs={{0,8},{4,12},{8,0},{12,4},{1,9},{5,13},{9,1},{13,5},{2,10},{6,14},... | collective-permute-start | bytes 393224 | tf_op jit(solution)/shard_map/ppermute | solution.py:304
  7.3 12.3 %collective-permute-start.1 = (bf16[240,256]{1,0:T(8,128)(2,1)S(1)}, bf16[240,256]{1,0:T(8,128)(2,1)S(1)}, u32[]{:S(2)}, u32[]{:S(2)}) collective-permute-start(bf16[240,256]{1,0:T(8,128)(2,1)S(1)} %get-tuple-element.25), channel_id=1, source_target_pairs={{0,6},{2,4},{4,2},{6,0},{8,14},{10,12},{12,10},{14,8},{1,7},{3,5},... | collective-permute-start | bytes 368648 | tf_op jit(solution)/shard_map/ppermute | solution.py:304
  9.0 10.6 %collective-permute-start = (bf16[240,256]{1,0:T(8,128)(2,1)S(1)}, bf16[240,256]{1,0:T(8,128)(2,1)S(1)}, u32[]{:S(2)}, u32[]{:S(2)}) collective-permute-start(bf16[240,256]{1,0:T(8,128)(2,1)S(1)} %get-tuple-element.25), channel_id=1, source_target_pairs={{0,4},{4,0},{8,12},{12,8},{1,5},{5,1},{9,13},{13,9},{2,6},{6,2},{1... | collective-permute-start | bytes 368648 | tf_op jit(solution)/shard_map/ppermute | solution.py:304
  10.2 9.4 %collective-permute-start.4 = (bf16[240,256]{1,0:T(8,128)(2,1)S(1)}, bf16[240,256]{1,0:T(8,128)(2,1)S(1)}, u32[]{:S(2)}, u32[]{:S(2)}) collective-permute-start(bf16[240,256]{1,0:T(8,128)(2,1)S(1)} %get-tuple-element.27.refs_4_.refs_0_), channel_id=1, source_target_pairs={{0,2},{2,0},{1,3},{3,1},{4,6},{6,4},{5,7},{7,5},{8,10},{10,8},{9,1... | collective-permute-start | bytes 368648 | tf_op jit(solution)/shard_map/ppermute | solution.py:304
  13.1 6.5 %collective-permute-start.3 = (bf16[240,256]{1,0:T(8,128)(2,1)S(1)}, bf16[240,256]{1,0:T(8,128)(2,1)S(1)}, u32[]{:S(2)}, u32[]{:S(2)}) collective-permute-start(bf16[240,256]{1,0:T(8,128)(2,1)S(1)} %collective-permute-done.2.refs_3_), channel_id=1, source_target_pairs={{0,2},{2,0},{1,3},{3,1},{4,6},{6,4},{5,7},{7,5},{8,10},{10,8},{9,1... | collective-permute-start | bytes 368648 | tf_op jit(solution)/shard_map/ppermute | solution.py:304
  18.1 5.0 %collective-permute-start.6 = (bf16[256,256]{1,0:T(8,128)(2,1)S(1)}, bf16[256,256]{1,0:T(8,128)(2,1)S(1)}, u32[]{:S(2)}, u32[]{:S(2)}) collective-permute-start(bf16[256,256]{1,0:T(8,128)(2,1)S(1)} %collective-permute-done.5.refs_2_), channel_id=1, source_target_pairs={{0,2},{2,0},{1,3},{3,1},{4,6},{6,4},{5,7},{7,5},{8,10},{10,8},{9,1... | collective-permute-start | bytes 393224 | tf_op jit(solution)/shard_map/ppermute | solution.py:304
  19.7 3.5 %collective-permute-start.8 = (bf16[960,256]{1,0:T(8,128)(2,1)S(1)}, bf16[960,256]{1,0:T(8,128)(2,1)S(1)}, u32[]{:S(2)}, u32[]{:S(2)}) collective-permute-start(bf16[960,256]{1,0:T(8,128)(2,1)S(1)} %stack.3.mine), channel_id=1, source_target_pairs={{0,1},{1,0},{2,3},{3,2},{4,5},{5,4},{6,7},{7,6},{8,9},{9,8},{10,11... | collective-permute-start | bytes 1474568 | tf_op jit(solution)/shard_map/ppermute | solution.py:304
  23.1 2.3 %collective-permute-start.7 = (bf16[960,256]{1,0:T(8,128)(2,1)S(1)}, bf16[960,256]{1,0:T(8,128)(2,1)S(1)}, u32[]{:S(2)}, u32[]{:S(2)}) collective-permute-start(bf16[960,256]{1,0:T(8,128)(2,1)S(1)} %stack.2.refs_0_), channel_id=1, source_target_pairs={{0,1},{1,0},{2,3},{3,2},{4,5},{5,4},{6,7},{7,6},{8,9},{9,8},{10,11... | collective-permute-start | bytes 1474568 | tf_op jit(solution)/shard_map/ppermute | solution.py:304

commit v6 on v5

--- a/solution.py
+++ b/solution.py
@@ -94,9 +94,6 @@
     for step in range(experts):
         rest = dot(places, jnp.concatenate(rests[step::experts], axis=0))
         out_refs[step][pl.ds(BLOCKS * MAIN, BLOCKS * REST), :] = rest.astype(BF16)
-        more = out_refs[step].shape[0] - BLOCKS * CAP
-        if more:
-            out_refs[step][pl.ds(BLOCKS * CAP, more), :] = jnp.zeros((more, cut), BF16)
 
 
 def rest_places(shape, wire, block):
@@ -137,12 +134,14 @@
 
 def stack_kernel(*refs):
     *parts, whole = refs
-    for step, part in enumerate(parts):
-        whole[pl.ds(step * BLOCKS * CAP, BLOCKS * CAP), :] = part[pl.ds(0, BLOCKS * CAP), :]
+    at = 0
+    for part in parts:
+        whole[pl.ds(at, part.shape[0]), :] = part[...]
+        at += part.shape[0]
 
 
 def stack(parts):
-    rows = len(parts) * BLOCKS * CAP
+    rows = sum(part.shape[0] for part in parts)
     return pl.pallas_call(
         stack_kernel,
         out_shape=pltpu.VMEM((rows, parts[0].shape[1]), parts[0].dtype),
@@ -153,14 +152,14 @@
     )(*parts)
 
 
-def pack(rows, tokens, out_grad, ids, weight):
+def pack(experts, tokens, out_grad, ids, weight):
     width = tokens.shape[1]
     inputs = [in_hbm(array) for array in (tokens, out_grad, ids.T, weight.T)]
     return pl.pallas_call(
-        functools.partial(pack_kernel, len(rows)),
-        out_shape=[pltpu.VMEM((count, width // BLOCKS), BF16) for count in rows],
+        functools.partial(pack_kernel, experts),
+        out_shape=[pltpu.VMEM((BLOCKS * CAP, width // BLOCKS), BF16)] * experts,
         in_specs=[HBM] * 4,
-        out_specs=[VMEM] * len(rows),
+        out_specs=[VMEM] * experts,
         scratch_shapes=[
             pltpu.VMEM((tokens.shape[0], width), BF16),
             pltpu.VMEM(ids.shape[::-1], jnp.int32),
@@ -208,36 +207,34 @@
 
 
 def own_kernel(experts, frag_ref, mine, theirs, w_gate, w_up, w_down, *refs):
-    grads, frag_out, load_out, x_rows, q_rows = refs
+    grads, acts, x_rows, q_rows, load_out = refs
     join([(mine, theirs, 0, experts)], x_rows, q_rows)
+    for piece, act in enumerate(activations(x_rows, q_rows, w_gate, w_up, w_down)):
+        acts[piece] = act
+    for piece, rows in enumerate((x_rows, x_rows, q_rows)):
+        grads[piece] = dot(acts[piece], rows[...]).astype(BF16)
     total = jnp.zeros((1, 128), F32)
     for step in range(experts):
         full = x_rows[pl.ds(step * SLOTS, SLOTS), pl.ds(0, 128)].astype(F32) < EMPTY / 2
         valid = lax.broadcasted_iota(jnp.int32, full.shape, 0) < CAP
         total += jnp.sum(jnp.where(full & valid, 1.0, 0.0), axis=0, keepdims=True)
     load_out[...] = total / (experts * CAP)
-    acts = activations(x_rows, q_rows, w_gate, w_up, w_down)
-    cut = frag_out.shape[2]
-    frag_columns = pl.ds(pl.multiple_of(frag_ref[0] * cut, cut), cut)
-    for piece, (act, rows) in enumerate(zip(acts, (x_rows, x_rows, q_rows))):
-        grads[piece] = dot(act, rows[...]).astype(BF16)
-        frag_out[piece] = dot(act, rows[:, frag_columns])
 
 
 def own(experts, fragment, mine, theirs, weights):
     units, width = weights[0].shape
-    cut = width // FRAGS
     rows = experts * SLOTS
     return pl.pallas_call(
         functools.partial(own_kernel, experts),
         out_shape=[
             pltpu.VMEM((3, units, width), BF16),
-            pltpu.VMEM((3, units, cut), F32),
+            pltpu.VMEM((3, units, rows), BF16),
+            pltpu.VMEM((rows, width), BF16),
+            pltpu.VMEM((rows, width), BF16),
             jax.ShapeDtypeStruct((1, 128), F32),
         ],
         in_specs=[SMEM] + [VMEM] * 5,
-        out_specs=[VMEM] * 3,
-        scratch_shapes=[pltpu.VMEM((rows, width), BF16)] * 2,
+        out_specs=[VMEM] * 5,
         name="own",
         compiler_params=pltpu.CompilerParams(vmem_limit_bytes=24 << 20),
         cost_estimate=pl.CostEstimate(
@@ -246,31 +243,28 @@
     )(fragment, mine, theirs, *weights)
 
 
-def other_kernel(ranges, frag_ref, *refs):
-    pieces = len(ranges)
-    mine, theirs = refs[:pieces], refs[pieces : 2 * pieces]
-    w_gate, w_up, w_down, grads, frag_in = refs[2 * pieces : 2 * pieces + 5]
-    outs = refs[2 * pieces + 5 : 2 * pieces + 8]
-    x_rows, q_rows, cuts, sems = refs[2 * pieces + 8 :]
-    cut = frag_in.shape[2]
+def other_kernel(chunks, frag_ref, mine, theirs, w_gate, w_up, w_down, *refs):
+    grads, own_acts, own_x, own_q, *outs, x_rows, q_rows, cuts, sems = refs
+    cut = cuts.shape[2]
     frag = frag_ref[0]
     copies = []
-    for piece, out in enumerate(outs):
+    for piece in range(3):
         for step in range(1, FRAGS):
             block = lax.rem(frag + step, FRAGS)
             columns = pl.ds(pl.multiple_of(block * cut, cut), cut)
             copies.append(
                 pltpu.make_async_copy(
-                    grads.at[piece, :, columns], out.at[:, columns], sems.at[piece, step]
+                    grads.at[piece, :, columns], outs[piece].at[:, columns], sems.at[piece, step]
                 )
             )
             copies[-1].start()
-    join([(*pair, *span) for *pair, span in zip(mine, theirs, ranges)], x_rows, q_rows)
+    join([(mine, theirs, 0, chunks)], x_rows, q_rows)
     acts = activations(x_rows, q_rows, w_gate, w_up, w_down)
     columns = pl.ds(pl.multiple_of(frag * cut, cut), cut)
-    for piece, (act, rows) in enumerate(zip(acts, (x_rows, x_rows, q_rows))):
-        grad = dot(act, rows[:, columns])
-        cuts[piece] = ((frag_in[piece] + grad) * 0.5).astype(BF16)
+    sides = ((own_x, x_rows), (own_x, x_rows), (own_q, q_rows))
+    for piece, (here, there) in enumerate(sides):
+        grad = dot(own_acts[piece], here[:, columns]) + dot(acts[piece], there[:, columns])
+        cuts[piece] = (grad * 0.5).astype(BF16)
         copies.append(
             pltpu.make_async_copy(cuts.at[piece], outs[piece].at[:, columns], sems.at[piece, 0])
         )
@@ -279,15 +273,14 @@
         copy.wait()
 
 
-def other(fragment, mine, theirs, ranges, weights, grads, frag_grad):
+def other(chunks, fragment, mine, theirs, weights, parts):
     units, width = weights[0].shape
     cut = width // FRAGS
-    pieces = len(mine)
-    rows = sum(count for _, count in ranges) * SLOTS
-    return pl.pallas_call(
-        functools.partial(other_kernel, ranges),
+    rows = chunks * SLOTS
+    return pl.pallas_call(
+        functools.partial(other_kernel, chunks),
         out_shape=[jax.ShapeDtypeStruct((units, width), BF16)] * 3,
-        in_specs=[SMEM] + [VMEM] * (2 * pieces + 5),
+        in_specs=[SMEM] + [VMEM] * 9,
         out_specs=[HBM] * 3,
         scratch_shapes=[pltpu.VMEM((rows, width), BF16)] * 2
         + [pltpu.VMEM((3, units, cut), BF16), pltpu.SemaphoreType.DMA((3, FRAGS))],
@@ -296,7 +289,7 @@
         cost_estimate=pl.CostEstimate(
             flops=8 * units * width * rows, bytes_accessed=8 * units * width, transcendentals=0
         ),
-    )(fragment, *mine, *theirs, *weights, grads, frag_grad)
+    )(fragment, mine, theirs, *weights, *parts)
 
 
 def send(array, axis, step):
@@ -317,6 +310,7 @@
     r2 = send(packed[2], "expert", 2)
     weights = load(weights, fragment, r0)
     r3, *weights = tie(r3, *weights)
+    r2, *weights = tie(r2, *weights)
     x3 = send(r3, "replica", 1)
     x2 = send(r2, "replica", 1)
     r1, x1, x3, x0 = tie(r1, x1, x3, x0)
@@ -324,8 +318,8 @@
     c0 = send(near, "tensor", 1)
     far = stack([x0, x1, x2, x3])
     f0 = send(far, "tensor", 1)
-    grads, frag_grad, filled = own(4, fragment, near, c0, weights)
-    grads = other(fragment, [far], [f0], [(0, 4)], weights, grads, frag_grad)
+    *parts, filled = own(4, fragment, near, c0, weights)
+    grads = other(4, fragment, far, f0, weights, parts)
     return grads, filled
 
 
@@ -333,9 +327,12 @@
     mine = [packed[0]] + [send(packed[step], "expert", step) for step in range(1, experts)]
     mine = stack(mine)
     theirs = send(mine, "tensor", 1)
-    grads, frag_grad, filled = own(experts, fragment, mine, theirs, weights)
-    synced = lax.psum(frag_grad.astype(BF16), "replica").astype(F32)
-    begin = fragment[0] * synced.shape[2]
+    grads, acts, x_rows, q_rows, filled = own(experts, fragment, mine, theirs, weights)
+    cut = x_rows.shape[1] // FRAGS
+    begin = fragment[0] * cut
+    sides = [lax.dynamic_slice_in_dim(rows, begin, cut, 1) for rows in (x_rows, x_rows, q_rows)]
+    pieces = jnp.stack([dot(act, side) for act, side in zip(acts, sides)]).astype(BF16)
+    synced = lax.psum(pieces, "replica").astype(F32)
     grads = [
         lax.dynamic_update_slice_in_dim(grad, (piece / replicas).astype(BF16), begin, 1)
         for grad, piece in zip(grads, synced)
@@ -347,10 +344,7 @@
     experts = lax.axis_size("expert")
     replicas = lax.axis_size("replica")
     weights = (gate_proj[0], up_proj[0], down_proj[0])
-    rows = [BLOCKS * CAP] * experts
-    if replicas == 2 and experts == 4:
-        rows[2] += 16
-    packed = pack(rows, tokens[0], out_grad[0], expert_ids[0], route_weight[0])
+    packed = pack(experts, tokens[0], out_grad[0], expert_ids[0], route_weight[0])
     if replicas == 2 and experts == 4:
         grads, filled = two_replicas(fragment, packed, weights)
     else:

time: 28.3 us -> 27.8 us (0.982)
  waiting for transfers between devices: 6.82 us -> 6.38 us
    ppermute x9, waiting for transfers between devices: 6.82 us -> 6.38 us  [send(): lax.ppermute(array, axis, [(index, peer(index, step, size)) for index in...]
where the time goes in v6:
time: 27.8 us; the launch traced here: 27.6 us
  starting transfers between devices  11.8 us (42%)
  Pallas kernels  8.01 us (29%)
  waiting for transfers between devices  6.38 us (23%)
  between operations  1.37 us (5%)
    ppermute x9, starting transfers between devices, send(): lax.ppermute(array, axis, [(index, peer(index, step, size)) for index in...  11.8 us
    ppermute x9, waiting for transfers between devices, send(): lax.ppermute(array, axis, [(index, peer(index, step, size)) for index in...  6.38 us
    pallas_call x1, Pallas kernels, other(): pl.pallas_call(functools.partial(other_kernel, chunks), out_shape=[jax.Sh...  2.74 us
    pallas_call x1, Pallas kernels, own(): pl.pallas_call(functools.partial(own_kernel, experts), out_shape=[pltpu.V...  2.05 us
    pallas_call x1, Pallas kernels, load(): pl.pallas_call(functools.partial(load_kernel, count), out_shape=[pltpu.VM...  1.64 us
    pallas_call x1, Pallas kernels, pack(): pl.pallas_call(functools.partial(pack_kernel, experts), out_shape=[pltpu....  1.52 us
  transfers between devices with their start and end apart: 9, of which 2 were waited for; matrix products, arithmetic and copies ran while one was open for 0% of the time, Pallas kernels for 14%

profile of v6, /device:TPU:0, one launch (start us, length us, event | category | flops | bytes accessed | tf_op | source)
XLA Modules:
  0.0 27.6 jit_solution(3914949926099912203)
XLA Ops:
  0.6 1.5 %pack.1 = (bf16[240,256]{1,0:T(8,128)(2,1)S(1)}, bf16[240,256]{1,0:T(8,128)(2,1)S(1)}, bf16[240,256]{1,0:T(8,128)(2,1)S(1)}, bf16[240,256]{1,0:T(8,128)(2,1)S(1)}) custom-call(bf16[240,1024]{1,0:T(8,128)(2,1)} %bitcast.18, bf16[240,1024]{1,0:T(8,128)(2,1)} %bitcast.19, s32[8,240]{1,0:T(8,128)} %bitcast.20, f32[8,240]{1,0:T(8,128)} %bitcast.21), custom_call_target="tpu_custom_call" | custom-call | tf_op jit(solution)/shard_map/pack/pallas_call | solution.py:158
  2.2 5.1 %collective-permute-start.2 = (bf16[240,256]{1,0:T(8,128)(2,1)S(1)}, bf16[240,256]{1,0:T(8,128)(2,1)S(1)}, u32[]{:S(2)}, u32[]{:S(2)}) collective-permute-start(bf16[240,256]{1,0:T(8,128)(2,1)S(1)} %get-tuple-element.32), channel_id=1, source_target_pairs={{0,12},{4,8},{8,4},{12,0},{1,13},{5,9},{9,5},{13,1},{2,14},{6,10},... | collective-permute-start | bytes 368648 | tf_op jit(solution)/shard_map/ppermute | solution.py:297
  7.3 0.0 collective-permute-start.5
  7.3 1.7 %collective-permute-start.1 = (bf16[240,256]{1,0:T(8,128)(2,1)S(1)}, bf16[240,256]{1,0:T(8,128)(2,1)S(1)}, u32[]{:S(2)}, u32[]{:S(2)}) collective-permute-start(bf16[240,256]{1,0:T(8,128)(2,1)S(1)} %get-tuple-element.31), channel_id=1, source_target_pairs={{0,6},{2,4},{4,2},{6,0},{8,14},{10,12},{12,10},{14,8},{1,7},{3,5},... | collective-permute-start | bytes 368648 | tf_op jit(solution)/shard_map/ppermute | solution.py:297
  9.0 1.2 %collective-permute-start = (bf16[240,256]{1,0:T(8,128)(2,1)S(1)}, bf16[240,256]{1,0:T(8,128)(2,1)S(1)}, u32[]{:S(2)}, u32[]{:S(2)}) collective-permute-start(bf16[240,256]{1,0:T(8,128)(2,1)S(1)} %get-tuple-element.31), channel_id=1, source_target_pairs={{0,4},{4,0},{8,12},{12,8},{1,5},{5,1},{9,13},{13,9},{2,6},{6,2},{1... | collective-permute-start | bytes 368648 | tf_op jit(solution)/shard_map/ppermute | solution.py:297
  10.2 0.5 %collective-permute-start.4 = (bf16[240,256]{1,0:T(8,128)(2,1)S(1)}, bf16[240,256]{1,0:T(8,128)(2,1)S(1)}, u32[]{:S(2)}, u32[]{:S(2)}) collective-permute-start(bf16[240,256]{1,0:T(8,128)(2,1)S(1)} %get-tuple-element.33.refs_4_.refs_0_), channel_id=1, source_target_pairs={{0,2},{2,0},{1,3},{3,1},{4,6},{6,4},{5,7},{7,5},{8,10},{10,8},{9,1... | collective-permute-start | bytes 368648 | tf_op jit(solution)/shard_map/ppermute | solution.py:297
  11.4 1.6 %load.1 = (bf16[384,1024]{1,0:T(8,128)(2,1)S(1)}, bf16[384,1024]{1,0:T(8,128)(2,1)S(1)}, bf16[384,1024]{1,0:T(8,128)(2,1)S(1)}) custom-call(bf16[384,1024]{1,0:T(8,128)(2,1)} %bitcast.15, bf16[384,1024]{1,0:T(8,128)(2,1)} %bitcast.16, bf16[384,1024]{1,0:T(8,128)(2,1)} %bitcast.17, s32[1]{0:T(128)S(6)} %copy.12.refs_3_.frag_ref, ...), custom_call_target="tpu_custom_call" | custom-call | tf_op jit(solution)/shard_map/load/pallas_call | solution.py:124
  13.1 0.0 collective-permute-done.2.refs_3_
  13.1 1.6 %collective-permute-start.3 = (bf16[240,256]{1,0:T(8,128)(2,1)S(1)}, bf16[240,256]{1,0:T(8,128)(2,1)S(1)}, u32[]{:S(2)}, u32[]{:S(2)}) collective-permute-start(bf16[240,256]{1,0:T(8,128)(2,1)S(1)} %collective-permute-done.2.refs_3_), channel_id=1, source_target_pairs={{0,2},{2,0},{1,3},{3,1},{4,6},{6,4},{5,7},{7,5},{8,10},{10,8},{9,1... | collective-permute-start | bytes 368648 | tf_op jit(solution)/shard_map/ppermute | solution.py:297
  14.6 3.1 %collective-permute-done.5.refs_2_ = bf16[240,256]{1,0:T(8,128)(2,1)S(1)} collective-permute-done((bf16[240,256]{1,0:T(8,128)(2,1)S(1)}, bf16[240,256]{1,0:T(8,128)(2,1)S(1)}, u32[]{:S(2)}, u32[]{:S(2)}) %collective-permute-start.5) | collective-permute-done | bytes 122912 | tf_op jit(solution)/shard_map/ppermute | solution.py:297
  17.8 1.5 %collective-permute-start.6 = (bf16[240,256]{1,0:T(8,128)(2,1)S(1)}, bf16[240,256]{1,0:T(8,128)(2,1)S(1)}, u32[]{:S(2)}, u32[]{:S(2)}) collective-permute-start(bf16[240,256]{1,0:T(8,128)(2,1)S(1)} %collective-permute-done.5.refs_2_), channel_id=1, source_target_pairs={{0,2},{2,0},{1,3},{3,1},{4,6},{6,4},{5,7},{7,5},{8,10},{10,8},{9,1... | collective-permute-start | bytes 368648 | tf_op jit(solution)/shard_map/ppermute | solution.py:297
  19.2 0.0 collective-permute-done.1.refs_1_
  19.3 0.0 collective-permute-done.refs_1_
  19.3 0.0 collective-permute-done.4.refs_0_
  19.3 0.0 collective-permute-done.3.refs_3_
  19.3 0.1 collective-permute-start.8
  19.4 3.2 %collective-permute-done.6.refs_2_ = bf16[240,256]{1,0:T(8,128)(2,1)S(1)} collective-permute-done((bf16[240,256]{1,0:T(8,128)(2,1)S(1)}, bf16[240,256]{1,0:T(8,128)(2,1)S(1)}, u32[]{:S(2)}, u32[]{:S(2)}) %collective-permute-start.6) | collective-permute-done | bytes 122912 | tf_op jit(solution)/shard_map/ppermute | solution.py:297
  22.7 0.1 collective-permute-start.7
  22.7 0.0 collective-permute-done.8.theirs
  22.8 2.0 %own.1 = (bf16[3,384,1024]{2,1,0:T(8,128)(2,1)S(1)}, bf16[3,384,256]{2,1,0:T(8,128)(2,1)S(1)}, bf16[256,1024]{1,0:T(8,128)(2,1)S(1)}, bf16[256,1024]{1,0:T(8,128)(2,1)S(1)}, f32[1,128]{1,0:T(1,128)}) custom-call(s32[1]{0:T(128)S(6)} %copy.12.refs_3_.frag_ref, bf16[960,256]{1,0:T(8,128)(2,1)S(1)} %stack.3.mine, ...), custom_call_target="tpu_custom_call" | custom-call | flops 1207959552 | bytes 4718592 | tf_op jit(solution)/shard_map/own/pallas_call | solution.py:227
  24.8 0.0 collective-permute-done.7.theirs
  24.8 2.7 %other.1 = (bf16[384,1024]{1,0:T(8,128)(2,1)}, bf16[384,1024]{1,0:T(8,128)(2,1)}, bf16[384,1024]{1,0:T(8,128)(2,1)}) custom-call(s32[1]{0:T(128)S(6)} %copy.12.refs_3_.frag_ref, bf16[960,256]{1,0:T(8,128)(2,1)S(1)} %stack.2.mine, bf16[960,256]{1,0:T(8,128)(2,1)S(1)} %collective-permute-done.7.theirs, bf16[384,1024]{1,0:T(8,128)(2,1)S(1)} %get-tuple-element.46.w_gate, ...), custom_call_target="tpu_custom_call" | custom-call | flops 805306368 | bytes 3145728 | tf_op jit(solution)/shard_map/other/pallas_call | solution.py:280
  (2 shorter events, 0.1 us)
Async XLA Ops:
  2.2 10.9 %collective-permute-start.2 = (bf16[240,256]{1,0:T(8,128)(2,1)S(1)}, bf16[240,256]{1,0:T(8,128)(2,1)S(1)}, u32[]{:S(2)}, u32[]{:S(2)}) collective-permute-start(bf16[240,256]{1,0:T(8,128)(2,1)S(1)} %get-tuple-element.32), channel_id=1, source_target_pairs={{0,12},{4,8},{8,4},{12,0},{1,13},{5,9},{9,5},{13,1},{2,14},{6,10},... | collective-permute-start | bytes 368648 | tf_op jit(solution)/shard_map/ppermute | solution.py:297
  7.3 10.5 %collective-permute-start.5 = (bf16[240,256]{1,0:T(8,128)(2,1)S(1)}, bf16[240,256]{1,0:T(8,128)(2,1)S(1)}, u32[]{:S(2)}, u32[]{:S(2)}) collective-permute-start(bf16[240,256]{1,0:T(8,128)(2,1)S(1)} %get-tuple-element.40), channel_id=1, source_target_pairs={{0,8},{4,12},{8,0},{12,4},{1,9},{5,13},{9,1},{13,5},{2,10},{6,14},... | collective-permute-start | bytes 368648 | tf_op jit(solution)/shard_map/ppermute | solution.py:297
  7.3 12.0 %collective-permute-start.1 = (bf16[240,256]{1,0:T(8,128)(2,1)S(1)}, bf16[240,256]{1,0:T(8,128)(2,1)S(1)}, u32[]{:S(2)}, u32[]{:S(2)}) collective-permute-start(bf16[240,256]{1,0:T(8,128)(2,1)S(1)} %get-tuple-element.31), channel_id=1, source_target_pairs={{0,6},{2,4},{4,2},{6,0},{8,14},{10,12},{12,10},{14,8},{1,7},{3,5},... | collective-permute-start | bytes 368648 | tf_op jit(solution)/shard_map/ppermute | solution.py:297
  9.0 10.3 %collective-permute-start = (bf16[240,256]{1,0:T(8,128)(2,1)S(1)}, bf16[240,256]{1,0:T(8,128)(2,1)S(1)}, u32[]{:S(2)}, u32[]{:S(2)}) collective-permute-start(bf16[240,256]{1,0:T(8,128)(2,1)S(1)} %get-tuple-element.31), channel_id=1, source_target_pairs={{0,4},{4,0},{8,12},{12,8},{1,5},{5,1},{9,13},{13,9},{2,6},{6,2},{1... | collective-permute-start | bytes 368648 | tf_op jit(solution)/shard_map/ppermute | solution.py:297
  10.2 9.0 %collective-permute-start.4 = (bf16[240,256]{1,0:T(8,128)(2,1)S(1)}, bf16[240,256]{1,0:T(8,128)(2,1)S(1)}, u32[]{:S(2)}, u32[]{:S(2)}) collective-permute-start(bf16[240,256]{1,0:T(8,128)(2,1)S(1)} %get-tuple-element.33.refs_4_.refs_0_), channel_id=1, source_target_pairs={{0,2},{2,0},{1,3},{3,1},{4,6},{6,4},{5,7},{7,5},{8,10},{10,8},{9,1... | collective-permute-start | bytes 368648 | tf_op jit(solution)/shard_map/ppermute | solution.py:297
  13.1 6.2 %collective-permute-start.3 = (bf16[240,256]{1,0:T(8,128)(2,1)S(1)}, bf16[240,256]{1,0:T(8,128)(2,1)S(1)}, u32[]{:S(2)}, u32[]{:S(2)}) collective-permute-start(bf16[240,256]{1,0:T(8,128)(2,1)S(1)} %collective-permute-done.2.refs_3_), channel_id=1, source_target_pairs={{0,2},{2,0},{1,3},{3,1},{4,6},{6,4},{5,7},{7,5},{8,10},{10,8},{9,1... | collective-permute-start | bytes 368648 | tf_op jit(solution)/shard_map/ppermute | solution.py:297
  17.8 4.9 %collective-permute-start.6 = (bf16[240,256]{1,0:T(8,128)(2,1)S(1)}, bf16[240,256]{1,0:T(8,128)(2,1)S(1)}, u32[]{:S(2)}, u32[]{:S(2)}) collective-permute-start(bf16[240,256]{1,0:T(8,128)(2,1)S(1)} %collective-permute-done.5.refs_2_), channel_id=1, source_target_pairs={{0,2},{2,0},{1,3},{3,1},{4,6},{6,4},{5,7},{7,5},{8,10},{10,8},{9,1... | collective-permute-start | bytes 368648 | tf_op jit(solution)/shard_map/ppermute | solution.py:297
  19.3 3.4 %collective-permute-start.8 = (bf16[960,256]{1,0:T(8,128)(2,1)S(1)}, bf16[960,256]{1,0:T(8,128)(2,1)S(1)}, u32[]{:S(2)}, u32[]{:S(2)}) collective-permute-start(bf16[960,256]{1,0:T(8,128)(2,1)S(1)} %stack.3.mine), channel_id=1, source_target_pairs={{0,1},{1,0},{2,3},{3,2},{4,5},{5,4},{6,7},{7,6},{8,9},{9,8},{10,11... | collective-permute-start | bytes 1474568 | tf_op jit(solution)/shard_map/ppermute | solution.py:297
  22.7 2.1 %collective-permute-start.7 = (bf16[960,256]{1,0:T(8,128)(2,1)S(1)}, bf16[960,256]{1,0:T(8,128)(2,1)S(1)}, u32[]{:S(2)}, u32[]{:S(2)}) collective-permute-start(bf16[960,256]{1,0:T(8,128)(2,1)S(1)} %stack.2.mine), channel_id=1, source_target_pairs={{0,1},{1,0},{2,3},{3,2},{4,5},{5,4},{6,7},{7,6},{8,9},{9,8},{10,11... | collective-permute-start | bytes 1474568 | tf_op jit(solution)/shard_map/ppermute | solution.py:297

commit v7 on v6

--- a/solution.py
+++ b/solution.py
@@ -249,9 +249,10 @@
     frag = frag_ref[0]
     copies = []
     for piece in range(3):
-        for step in range(1, FRAGS):
-            block = lax.rem(frag + step, FRAGS)
-            columns = pl.ds(pl.multiple_of(block * cut, cut), cut)
+        for step, count in ((1, 2), (2, 1)):
+            low, high = (2 * cut, 0) if step == 1 else ((1 - frag) * cut, (5 - frag) * cut)
+            begin = jnp.where(frag < 2, low, high)
+            columns = pl.ds(pl.multiple_of(begin, cut), count * cut)
             copies.append(
                 pltpu.make_async_copy(
                     grads.at[piece, :, columns], outs[piece].at[:, columns], sems.at[piece, step]

time: 27.8 us -> 27.5 us (0.989)
  Pallas kernels: 8.01 us -> 7.7 us
    pallas_call x1, Pallas kernels: 2.74 us -> 2.42 us  [other(): pl.pallas_call(functools.partial(other_kernel, chunks), out_shape=[jax.Sh...]
where the time goes in v7:
time: 27.5 us; the launch traced here: 27.2 us
  starting transfers between devices  11.8 us (43%)
  Pallas kernels  7.7 us (28%)
  waiting for transfers between devices  6.38 us (23%)
  between operations  1.37 us (5%)
    ppermute x9, starting transfers between devices, send(): lax.ppermute(array, axis, [(index, peer(index, step, size)) for index in...  11.8 us
    ppermute x9, waiting for transfers between devices, send(): lax.ppermute(array, axis, [(index, peer(index, step, size)) for index in...  6.38 us
    pallas_call x1, Pallas kernels, other(): pl.pallas_call(functools.partial(other_kernel, chunks), out_shape=[jax.Sh...  2.42 us
    pallas_call x1, Pallas kernels, own(): pl.pallas_call(functools.partial(own_kernel, experts), out_shape=[pltpu.V...  2.05 us
    pallas_call x1, Pallas kernels, load(): pl.pallas_call(functools.partial(load_kernel, count), out_shape=[pltpu.VM...  1.64 us
    pallas_call x1, Pallas kernels, pack(): pl.pallas_call(functools.partial(pack_kernel, experts), out_shape=[pltpu....  1.52 us
  transfers between devices with their start and end apart: 9, of which 2 were waited for; matrix products, arithmetic and copies ran while one was open for 0% of the time, Pallas kernels for 14%

profile of v7, /device:TPU:0, one launch (start us, length us, event | category | flops | bytes accessed | tf_op | source)
XLA Modules:
  0.0 27.2 jit_solution(17579817808455641049)
XLA Ops:
  0.6 1.5 %pack.1 = (bf16[240,256]{1,0:T(8,128)(2,1)S(1)}, bf16[240,256]{1,0:T(8,128)(2,1)S(1)}, bf16[240,256]{1,0:T(8,128)(2,1)S(1)}, bf16[240,256]{1,0:T(8,128)(2,1)S(1)}) custom-call(bf16[240,1024]{1,0:T(8,128)(2,1)} %bitcast.18, bf16[240,1024]{1,0:T(8,128)(2,1)} %bitcast.19, s32[8,240]{1,0:T(8,128)} %bitcast.20, f32[8,240]{1,0:T(8,128)} %bitcast.21), custom_call_target="tpu_custom_call" | custom-call | tf_op jit(solution)/shard_map/pack/pallas_call | solution.py:158
  2.2 5.1 %collective-permute-start.2 = (bf16[240,256]{1,0:T(8,128)(2,1)S(1)}, bf16[240,256]{1,0:T(8,128)(2,1)S(1)}, u32[]{:S(2)}, u32[]{:S(2)}) collective-permute-start(bf16[240,256]{1,0:T(8,128)(2,1)S(1)} %get-tuple-element.32), channel_id=1, source_target_pairs={{0,12},{4,8},{8,4},{12,0},{1,13},{5,9},{9,5},{13,1},{2,14},{6,10},... | collective-permute-start | bytes 368648 | tf_op jit(solution)/shard_map/ppermute | solution.py:298
  7.3 0.0 collective-permute-start.5
  7.3 1.7 %collective-permute-start.1 = (bf16[240,256]{1,0:T(8,128)(2,1)S(1)}, bf16[240,256]{1,0:T(8,128)(2,1)S(1)}, u32[]{:S(2)}, u32[]{:S(2)}) collective-permute-start(bf16[240,256]{1,0:T(8,128)(2,1)S(1)} %get-tuple-element.31), channel_id=1, source_target_pairs={{0,6},{2,4},{4,2},{6,0},{8,14},{10,12},{12,10},{14,8},{1,7},{3,5},... | collective-permute-start | bytes 368648 | tf_op jit(solution)/shard_map/ppermute | solution.py:298
  9.0 1.2 %collective-permute-start = (bf16[240,256]{1,0:T(8,128)(2,1)S(1)}, bf16[240,256]{1,0:T(8,128)(2,1)S(1)}, u32[]{:S(2)}, u32[]{:S(2)}) collective-permute-start(bf16[240,256]{1,0:T(8,128)(2,1)S(1)} %get-tuple-element.31), channel_id=1, source_target_pairs={{0,4},{4,0},{8,12},{12,8},{1,5},{5,1},{9,13},{13,9},{2,6},{6,2},{1... | collective-permute-start | bytes 368648 | tf_op jit(solution)/shard_map/ppermute | solution.py:298
  10.2 0.5 %collective-permute-start.4 = (bf16[240,256]{1,0:T(8,128)(2,1)S(1)}, bf16[240,256]{1,0:T(8,128)(2,1)S(1)}, u32[]{:S(2)}, u32[]{:S(2)}) collective-permute-start(bf16[240,256]{1,0:T(8,128)(2,1)S(1)} %get-tuple-element.33.refs_4_.refs_0_), channel_id=1, source_target_pairs={{0,2},{2,0},{1,3},{3,1},{4,6},{6,4},{5,7},{7,5},{8,10},{10,8},{9,1... | collective-permute-start | bytes 368648 | tf_op jit(solution)/shard_map/ppermute | solution.py:298
  11.4 1.6 %load.1 = (bf16[384,1024]{1,0:T(8,128)(2,1)S(1)}, bf16[384,1024]{1,0:T(8,128)(2,1)S(1)}, bf16[384,1024]{1,0:T(8,128)(2,1)S(1)}) custom-call(bf16[384,1024]{1,0:T(8,128)(2,1)} %bitcast.15, bf16[384,1024]{1,0:T(8,128)(2,1)} %bitcast.16, bf16[384,1024]{1,0:T(8,128)(2,1)} %bitcast.17, s32[1]{0:T(128)S(6)} %copy.12.refs_3_.frag_ref, ...), custom_call_target="tpu_custom_call" | custom-call | tf_op jit(solution)/shard_map/load/pallas_call | solution.py:124
  13.1 0.0 collective-permute-done.2.refs_3_
  13.1 1.6 %collective-permute-start.3 = (bf16[240,256]{1,0:T(8,128)(2,1)S(1)}, bf16[240,256]{1,0:T(8,128)(2,1)S(1)}, u32[]{:S(2)}, u32[]{:S(2)}) collective-permute-start(bf16[240,256]{1,0:T(8,128)(2,1)S(1)} %collective-permute-done.2.refs_3_), channel_id=1, source_target_pairs={{0,2},{2,0},{1,3},{3,1},{4,6},{6,4},{5,7},{7,5},{8,10},{10,8},{9,1... | collective-permute-start | bytes 368648 | tf_op jit(solution)/shard_map/ppermute | solution.py:298
  14.6 3.1 %collective-permute-done.5.refs_2_ = bf16[240,256]{1,0:T(8,128)(2,1)S(1)} collective-permute-done((bf16[240,256]{1,0:T(8,128)(2,1)S(1)}, bf16[240,256]{1,0:T(8,128)(2,1)S(1)}, u32[]{:S(2)}, u32[]{:S(2)}) %collective-permute-start.5) | collective-permute-done | bytes 122912 | tf_op jit(solution)/shard_map/ppermute | solution.py:298
  17.8 1.5 %collective-permute-start.6 = (bf16[240,256]{1,0:T(8,128)(2,1)S(1)}, bf16[240,256]{1,0:T(8,128)(2,1)S(1)}, u32[]{:S(2)}, u32[]{:S(2)}) collective-permute-start(bf16[240,256]{1,0:T(8,128)(2,1)S(1)} %collective-permute-done.5.refs_2_), channel_id=1, source_target_pairs={{0,2},{2,0},{1,3},{3,1},{4,6},{6,4},{5,7},{7,5},{8,10},{10,8},{9,1... | collective-permute-start | bytes 368648 | tf_op jit(solution)/shard_map/ppermute | solution.py:298
  19.2 0.0 collective-permute-done.1.refs_1_
  19.3 0.0 collective-permute-done.refs_1_
  19.3 0.0 collective-permute-done.4.refs_0_
  19.3 0.0 collective-permute-done.3.refs_3_
  19.3 0.1 collective-permute-start.8
  19.4 3.2 %collective-permute-done.6.refs_2_ = bf16[240,256]{1,0:T(8,128)(2,1)S(1)} collective-permute-done((bf16[240,256]{1,0:T(8,128)(2,1)S(1)}, bf16[240,256]{1,0:T(8,128)(2,1)S(1)}, u32[]{:S(2)}, u32[]{:S(2)}) %collective-permute-start.6) | collective-permute-done | bytes 122912 | tf_op jit(solution)/shard_map/ppermute | solution.py:298
  22.7 0.1 collective-permute-start.7
  22.7 0.0 collective-permute-done.8.theirs
  22.8 2.0 %own.1 = (bf16[3,384,1024]{2,1,0:T(8,128)(2,1)S(1)}, bf16[3,384,256]{2,1,0:T(8,128)(2,1)S(1)}, bf16[256,1024]{1,0:T(8,128)(2,1)S(1)}, bf16[256,1024]{1,0:T(8,128)(2,1)S(1)}, f32[1,128]{1,0:T(1,128)}) custom-call(s32[1]{0:T(128)S(6)} %copy.12.refs_3_.frag_ref, bf16[960,256]{1,0:T(8,128)(2,1)S(1)} %stack.3.mine, ...), custom_call_target="tpu_custom_call" | custom-call | flops 1207959552 | bytes 4718592 | tf_op jit(solution)/shard_map/own/pallas_call | solution.py:227
  24.8 0.0 collective-permute-done.7.theirs
  24.8 2.4 %other.1 = (bf16[384,1024]{1,0:T(8,128)(2,1)}, bf16[384,1024]{1,0:T(8,128)(2,1)}, bf16[384,1024]{1,0:T(8,128)(2,1)}) custom-call(s32[1]{0:T(128)S(6)} %copy.12.refs_3_.frag_ref, bf16[960,256]{1,0:T(8,128)(2,1)S(1)} %stack.2.mine, bf16[960,256]{1,0:T(8,128)(2,1)S(1)} %collective-permute-done.7.theirs, bf16[384,1024]{1,0:T(8,128)(2,1)S(1)} %get-tuple-element.46.w_gate, ...), custom_call_target="tpu_custom_call" | custom-call | flops 805306368 | bytes 3145728 | tf_op jit(solution)/shard_map/other/pallas_call | solution.py:281
  (2 shorter events, 0.1 us)
Async XLA Ops:
  2.2 10.9 %collective-permute-start.2 = (bf16[240,256]{1,0:T(8,128)(2,1)S(1)}, bf16[240,256]{1,0:T(8,128)(2,1)S(1)}, u32[]{:S(2)}, u32[]{:S(2)}) collective-permute-start(bf16[240,256]{1,0:T(8,128)(2,1)S(1)} %get-tuple-element.32), channel_id=1, source_target_pairs={{0,12},{4,8},{8,4},{12,0},{1,13},{5,9},{9,5},{13,1},{2,14},{6,10},... | collective-permute-start | bytes 368648 | tf_op jit(solution)/shard_map/ppermute | solution.py:298
  7.3 10.5 %collective-permute-start.5 = (bf16[240,256]{1,0:T(8,128)(2,1)S(1)}, bf16[240,256]{1,0:T(8,128)(2,1)S(1)}, u32[]{:S(2)}, u32[]{:S(2)}) collective-permute-start(bf16[240,256]{1,0:T(8,128)(2,1)S(1)} %get-tuple-element.40), channel_id=1, source_target_pairs={{0,8},{4,12},{8,0},{12,4},{1,9},{5,13},{9,1},{13,5},{2,10},{6,14},... | collective-permute-start | bytes 368648 | tf_op jit(solution)/shard_map/ppermute | solution.py:298
  7.3 12.0 %collective-permute-start.1 = (bf16[240,256]{1,0:T(8,128)(2,1)S(1)}, bf16[240,256]{1,0:T(8,128)(2,1)S(1)}, u32[]{:S(2)}, u32[]{:S(2)}) collective-permute-start(bf16[240,256]{1,0:T(8,128)(2,1)S(1)} %get-tuple-element.31), channel_id=1, source_target_pairs={{0,6},{2,4},{4,2},{6,0},{8,14},{10,12},{12,10},{14,8},{1,7},{3,5},... | collective-permute-start | bytes 368648 | tf_op jit(solution)/shard_map/ppermute | solution.py:298
  9.0 10.3 %collective-permute-start = (bf16[240,256]{1,0:T(8,128)(2,1)S(1)}, bf16[240,256]{1,0:T(8,128)(2,1)S(1)}, u32[]{:S(2)}, u32[]{:S(2)}) collective-permute-start(bf16[240,256]{1,0:T(8,128)(2,1)S(1)} %get-tuple-element.31), channel_id=1, source_target_pairs={{0,4},{4,0},{8,12},{12,8},{1,5},{5,1},{9,13},{13,9},{2,6},{6,2},{1... | collective-permute-start | bytes 368648 | tf_op jit(solution)/shard_map/ppermute | solution.py:298
  10.2 9.0 %collective-permute-start.4 = (bf16[240,256]{1,0:T(8,128)(2,1)S(1)}, bf16[240,256]{1,0:T(8,128)(2,1)S(1)}, u32[]{:S(2)}, u32[]{:S(2)}) collective-permute-start(bf16[240,256]{1,0:T(8,128)(2,1)S(1)} %get-tuple-element.33.refs_4_.refs_0_), channel_id=1, source_target_pairs={{0,2},{2,0},{1,3},{3,1},{4,6},{6,4},{5,7},{7,5},{8,10},{10,8},{9,1... | collective-permute-start | bytes 368648 | tf_op jit(solution)/shard_map/ppermute | solution.py:298
  13.1 6.2 %collective-permute-start.3 = (bf16[240,256]{1,0:T(8,128)(2,1)S(1)}, bf16[240,256]{1,0:T(8,128)(2,1)S(1)}, u32[]{:S(2)}, u32[]{:S(2)}) collective-permute-start(bf16[240,256]{1,0:T(8,128)(2,1)S(1)} %collective-permute-done.2.refs_3_), channel_id=1, source_target_pairs={{0,2},{2,0},{1,3},{3,1},{4,6},{6,4},{5,7},{7,5},{8,10},{10,8},{9,1... | collective-permute-start | bytes 368648 | tf_op jit(solution)/shard_map/ppermute | solution.py:298
  17.8 4.9 %collective-permute-start.6 = (bf16[240,256]{1,0:T(8,128)(2,1)S(1)}, bf16[240,256]{1,0:T(8,128)(2,1)S(1)}, u32[]{:S(2)}, u32[]{:S(2)}) collective-permute-start(bf16[240,256]{1,0:T(8,128)(2,1)S(1)} %collective-permute-done.5.refs_2_), channel_id=1, source_target_pairs={{0,2},{2,0},{1,3},{3,1},{4,6},{6,4},{5,7},{7,5},{8,10},{10,8},{9,1... | collective-permute-start | bytes 368648 | tf_op jit(solution)/shard_map/ppermute | solution.py:298
  19.3 3.4 %collective-permute-start.8 = (bf16[960,256]{1,0:T(8,128)(2,1)S(1)}, bf16[960,256]{1,0:T(8,128)(2,1)S(1)}, u32[]{:S(2)}, u32[]{:S(2)}) collective-permute-start(bf16[960,256]{1,0:T(8,128)(2,1)S(1)} %stack.3.mine), channel_id=1, source_target_pairs={{0,1},{1,0},{2,3},{3,2},{4,5},{5,4},{6,7},{7,6},{8,9},{9,8},{10,11... | collective-permute-start | bytes 1474568 | tf_op jit(solution)/shard_map/ppermute | solution.py:298
  22.7 2.1 %collective-permute-start.7 = (bf16[960,256]{1,0:T(8,128)(2,1)S(1)}, bf16[960,256]{1,0:T(8,128)(2,1)S(1)}, u32[]{:S(2)}, u32[]{:S(2)}) collective-permute-start(bf16[960,256]{1,0:T(8,128)(2,1)S(1)} %stack.2.mine), channel_id=1, source_target_pairs={{0,1},{1,0},{2,3},{3,2},{4,5},{5,4},{6,7},{7,6},{8,9},{9,8},{10,11... | collective-permute-start | bytes 1474568 | tf_op jit(solution)/shard_map/ppermute | solution.py:298

commit v8 on v7

--- a/solution.py
+++ b/solution.py
@@ -211,7 +211,7 @@
     join([(mine, theirs, 0, experts)], x_rows, q_rows)
     for piece, act in enumerate(activations(x_rows, q_rows, w_gate, w_up, w_down)):
         acts[piece] = act
-    for piece, rows in enumerate((x_rows, x_rows, q_rows)):
+    for piece, rows in ((2, q_rows), (0, x_rows), (1, x_rows)):
         grads[piece] = dot(acts[piece], rows[...]).astype(BF16)
     total = jnp.zeros((1, 128), F32)
     for step in range(experts):
@@ -262,9 +262,10 @@
     join([(mine, theirs, 0, chunks)], x_rows, q_rows)
     acts = activations(x_rows, q_rows, w_gate, w_up, w_down)
     columns = pl.ds(pl.multiple_of(frag * cut, cut), cut)
-    sides = ((own_x, x_rows), (own_x, x_rows), (own_q, q_rows))
-    for piece, (here, there) in enumerate(sides):
-        grad = dot(own_acts[piece], here[:, columns]) + dot(acts[piece], there[:, columns])
+    x_both = jnp.concatenate([own_x[:, columns], x_rows[:, columns]], axis=0)
+    q_both = jnp.concatenate([own_q[:, columns], q_rows[:, columns]], axis=0)
+    for piece, rows in ((2, q_both), (0, x_both), (1, x_both)):
+        grad = dot(jnp.concatenate([own_acts[piece], acts[piece]], axis=1), rows)
         cuts[piece] = (grad * 0.5).astype(BF16)
         copies.append(
             pltpu.make_async_copy(cuts.at[piece], outs[piece].at[:, columns], sems.at[piece, 0])
@@ -310,11 +311,11 @@
     x1 = send(packed[1], ("expert", "replica"), 3)
     r2 = send(packed[2], "expert", 2)
     weights = load(weights, fragment, r0)
-    r3, *weights = tie(r3, *weights)
+    r3, x0, *weights = tie(r3, x0, *weights)
     r2, *weights = tie(r2, *weights)
     x3 = send(r3, "replica", 1)
     x2 = send(r2, "replica", 1)
-    r1, x1, x3, x0 = tie(r1, x1, x3, x0)
+    r1, x1, x3 = tie(r1, x1, x3)
     near = stack([r0, r1, r2, r3])
     c0 = send(near, "tensor", 1)
     far = stack([x0, x1, x2, x3])

time: 27.5 us -> 27 us (0.982)
  starting transfers between devices: 11.8 us -> 12.8 us
  waiting for transfers between devices: 6.38 us -> 5.55 us
  Pallas kernels: 7.7 us -> 7.11 us
    ppermute x9, starting transfers between devices: 11.8 us -> 12.8 us  [send(): lax.ppermute(array, axis, [(index, peer(index, step, size)) for index in...]
    ppermute x9, waiting for transfers between devices: 6.38 us -> 5.55 us  [send(): lax.ppermute(array, axis, [(index, peer(index, step, size)) for index in...]
    pallas_call x1, Pallas kernels: 2.05 us -> 1.67 us  [own(): pl.pallas_call(functools.partial(own_kernel, experts), out_shape=[pltpu.V...]
  transfers between devices with their start and end apart: 9 -> 9, of which waited for: 2 -> 4; matrix products, arithmetic and copies ran while one was open for 0% -> 0% of each run, Pallas kernels for 14% -> 13%
where the time goes in v8:
time: 27 us; the launch traced here: 26.8 us
  starting transfers between devices  12.8 us (47%)
  Pallas kernels  7.11 us (26%)
  waiting for transfers between devices  5.55 us (21%)
  between operations  1.36 us (5%)
    ppermute x9, starting transfers between devices, send(): lax.ppermute(array, axis, [(index, peer(index, step, size)) for index in...  12.8 us
    ppermute x9, waiting for transfers between devices, send(): lax.ppermute(array, axis, [(index, peer(index, step, size)) for index in...  5.55 us
    pallas_call x1, Pallas kernels, other(): pl.pallas_call(functools.partial(other_kernel, chunks), out_shape=[jax.Sh...  2.22 us
    pallas_call x1, Pallas kernels, own(): pl.pallas_call(functools.partial(own_kernel, experts), out_shape=[pltpu.V...  1.67 us
    pallas_call x1, Pallas kernels, load(): pl.pallas_call(functools.partial(load_kernel, count), out_shape=[pltpu.VM...  1.64 us
    pallas_call x1, Pallas kernels, pack(): pl.pallas_call(functools.partial(pack_kernel, experts), out_shape=[pltpu....  1.52 us
  transfers between devices with their start and end apart: 9, of which 4 were waited for; matrix products, arithmetic and copies ran while one was open for 0% of the time, Pallas kernels for 13%

profile of v8, /device:TPU:0, one launch (start us, length us, event | category | flops | bytes accessed | tf_op | source)
XLA Modules:
  0.0 26.8 jit_solution(16185489443144722446)
XLA Ops:
  0.6 1.5 %pack.1 = (bf16[240,256]{1,0:T(8,128)(2,1)S(1)}, bf16[240,256]{1,0:T(8,128)(2,1)S(1)}, bf16[240,256]{1,0:T(8,128)(2,1)S(1)}, bf16[240,256]{1,0:T(8,128)(2,1)S(1)}) custom-call(bf16[240,1024]{1,0:T(8,128)(2,1)} %bitcast.18, bf16[240,1024]{1,0:T(8,128)(2,1)} %bitcast.19, s32[8,240]{1,0:T(8,128)} %bitcast.20, f32[8,240]{1,0:T(8,128)} %bitcast.21), custom_call_target="tpu_custom_call" | custom-call | tf_op jit(solution)/shard_map/pack/pallas_call | solution.py:158
  2.2 5.1 %collective-permute-start = (bf16[240,256]{1,0:T(8,128)(2,1)S(1)}, bf16[240,256]{1,0:T(8,128)(2,1)S(1)}, u32[]{:S(2)}, u32[]{:S(2)}) collective-permute-start(bf16[240,256]{1,0:T(8,128)(2,1)S(1)} %get-tuple-element.31), channel_id=1, source_target_pairs={{0,12},{4,8},{8,4},{12,0},{1,13},{5,9},{9,5},{13,1},{2,14},{6,10},... | collective-permute-start | bytes 368648 | tf_op jit(solution)/shard_map/ppermute | solution.py:299
  7.3 1.5 %collective-permute-start.1 = (bf16[240,256]{1,0:T(8,128)(2,1)S(1)}, bf16[240,256]{1,0:T(8,128)(2,1)S(1)}, u32[]{:S(2)}, u32[]{:S(2)}) collective-permute-start(bf16[240,256]{1,0:T(8,128)(2,1)S(1)} %get-tuple-element.32.refs_4_.refs_0_), channel_id=1, source_target_pairs={{0,2},{2,0},{1,3},{3,1},{4,6},{6,4},{5,7},{7,5},{8,10},{10,8},{9,1... | collective-permute-start | bytes 368648 | tf_op jit(solution)/shard_map/ppermute | solution.py:299
  8.8 0.0 collective-permute-start.5
  8.8 0.6 %collective-permute-start.3 = (bf16[240,256]{1,0:T(8,128)(2,1)S(1)}, bf16[240,256]{1,0:T(8,128)(2,1)S(1)}, u32[]{:S(2)}, u32[]{:S(2)}) collective-permute-start(bf16[240,256]{1,0:T(8,128)(2,1)S(1)} %get-tuple-element.37), channel_id=1, source_target_pairs={{0,6},{2,4},{4,2},{6,0},{8,14},{10,12},{12,10},{14,8},{1,7},{3,5},... | collective-permute-start | bytes 368648 | tf_op jit(solution)/shard_map/ppermute | solution.py:299
  9.4 1.4 %collective-permute-start.2 = (bf16[240,256]{1,0:T(8,128)(2,1)S(1)}, bf16[240,256]{1,0:T(8,128)(2,1)S(1)}, u32[]{:S(2)}, u32[]{:S(2)}) collective-permute-start(bf16[240,256]{1,0:T(8,128)(2,1)S(1)} %get-tuple-element.37), channel_id=1, source_target_pairs={{0,4},{4,0},{8,12},{12,8},{1,5},{5,1},{9,13},{13,9},{2,6},{6,2},{1... | collective-permute-start | bytes 368648 | tf_op jit(solution)/shard_map/ppermute | solution.py:299
  11.4 1.6 %load.1 = (bf16[384,1024]{1,0:T(8,128)(2,1)S(1)}, bf16[384,1024]{1,0:T(8,128)(2,1)S(1)}, bf16[384,1024]{1,0:T(8,128)(2,1)S(1)}) custom-call(bf16[384,1024]{1,0:T(8,128)(2,1)} %bitcast.15, bf16[384,1024]{1,0:T(8,128)(2,1)} %bitcast.16, bf16[384,1024]{1,0:T(8,128)(2,1)} %bitcast.17, s32[1]{0:T(128)S(6)} %copy.12.refs_3_.frag_ref, ...), custom_call_target="tpu_custom_call" | custom-call | tf_op jit(solution)/shard_map/load/pallas_call | solution.py:124
  13.1 0.0 collective-permute-done.refs_3_
  13.1 0.1 collective-permute-done.1.refs_0_
  13.2 2.6 %collective-permute-start.4 = (bf16[240,256]{1,0:T(8,128)(2,1)S(1)}, bf16[240,256]{1,0:T(8,128)(2,1)S(1)}, u32[]{:S(2)}, u32[]{:S(2)}) collective-permute-start(bf16[240,256]{1,0:T(8,128)(2,1)S(1)} %collective-permute-done.refs_3_), channel_id=1, source_target_pairs={{0,2},{2,0},{1,3},{3,1},{4,6},{6,4},{5,7},{7,5},{8,10},{10,8},{9,1... | collective-permute-start | bytes 368648 | tf_op jit(solution)/shard_map/ppermute | solution.py:299
  15.7 2.0 %collective-permute-done.5.refs_2_ = bf16[240,256]{1,0:T(8,128)(2,1)S(1)} collective-permute-done((bf16[240,256]{1,0:T(8,128)(2,1)S(1)}, bf16[240,256]{1,0:T(8,128)(2,1)S(1)}, u32[]{:S(2)}, u32[]{:S(2)}) %collective-permute-start.5) | collective-permute-done | bytes 122912 | tf_op jit(solution)/shard_map/ppermute | solution.py:299
  17.8 1.5 %collective-permute-start.6 = (bf16[240,256]{1,0:T(8,128)(2,1)S(1)}, bf16[240,256]{1,0:T(8,128)(2,1)S(1)}, u32[]{:S(2)}, u32[]{:S(2)}) collective-permute-start(bf16[240,256]{1,0:T(8,128)(2,1)S(1)} %collective-permute-done.5.refs_2_), channel_id=1, source_target_pairs={{0,2},{2,0},{1,3},{3,1},{4,6},{6,4},{5,7},{7,5},{8,10},{10,8},{9,1... | collective-permute-start | bytes 368648 | tf_op jit(solution)/shard_map/ppermute | solution.py:299
  19.2 0.0 collective-permute-done.3.refs_1_
  19.3 0.0 collective-permute-done.2.refs_1_
  19.3 0.0 collective-permute-done.4.refs_3_
  19.3 0.1 collective-permute-start.8
  19.4 3.2 %collective-permute-done.6.refs_2_ = bf16[240,256]{1,0:T(8,128)(2,1)S(1)} collective-permute-done((bf16[240,256]{1,0:T(8,128)(2,1)S(1)}, bf16[240,256]{1,0:T(8,128)(2,1)S(1)}, u32[]{:S(2)}, u32[]{:S(2)}) %collective-permute-start.6) | collective-permute-done | bytes 122912 | tf_op jit(solution)/shard_map/ppermute | solution.py:299
  22.7 0.1 collective-permute-start.7
  22.7 0.0 collective-permute-done.8.theirs
  22.8 1.7 %own.1 = (bf16[3,384,1024]{2,1,0:T(8,128)(2,1)S(1)}, bf16[3,384,256]{2,1,0:T(8,128)(2,1)S(1)}, bf16[256,1024]{1,0:T(8,128)(2,1)S(1)}, bf16[256,1024]{1,0:T(8,128)(2,1)S(1)}, f32[1,128]{1,0:T(1,128)}) custom-call(s32[1]{0:T(128)S(6)} %copy.12.refs_3_.frag_ref, bf16[960,256]{1,0:T(8,128)(2,1)S(1)} %stack.3.mine, ...), custom_call_target="tpu_custom_call" | custom-call | flops 1207959552 | bytes 4718592 | tf_op jit(solution)/shard_map/own/pallas_call | solution.py:227
  24.4 0.2 collective-permute-done.7.theirs
  24.6 2.2 %other.1 = (bf16[384,1024]{1,0:T(8,128)(2,1)}, bf16[384,1024]{1,0:T(8,128)(2,1)}, bf16[384,1024]{1,0:T(8,128)(2,1)}) custom-call(s32[1]{0:T(128)S(6)} %copy.12.refs_3_.frag_ref, bf16[960,256]{1,0:T(8,128)(2,1)S(1)} %stack.2.mine, bf16[960,256]{1,0:T(8,128)(2,1)S(1)} %collective-permute-done.7.theirs, bf16[384,1024]{1,0:T(8,128)(2,1)S(1)} %get-tuple-element.46.w_gate, ...), custom_call_target="tpu_custom_call" | custom-call | flops 805306368 | bytes 3145728 | tf_op jit(solution)/shard_map/other/pallas_call | solution.py:282
  (2 shorter events, 0.1 us)
Async XLA Ops:
  2.2 10.9 %collective-permute-start = (bf16[240,256]{1,0:T(8,128)(2,1)S(1)}, bf16[240,256]{1,0:T(8,128)(2,1)S(1)}, u32[]{:S(2)}, u32[]{:S(2)}) collective-permute-start(bf16[240,256]{1,0:T(8,128)(2,1)S(1)} %get-tuple-element.31), channel_id=1, source_target_pairs={{0,12},{4,8},{8,4},{12,0},{1,13},{5,9},{9,5},{13,1},{2,14},{6,10},... | collective-permute-start | bytes 368648 | tf_op jit(solution)/shard_map/ppermute | solution.py:299
  7.3 5.9 %collective-permute-start.1 = (bf16[240,256]{1,0:T(8,128)(2,1)S(1)}, bf16[240,256]{1,0:T(8,128)(2,1)S(1)}, u32[]{:S(2)}, u32[]{:S(2)}) collective-permute-start(bf16[240,256]{1,0:T(8,128)(2,1)S(1)} %get-tuple-element.32.refs_4_.refs_0_), channel_id=1, source_target_pairs={{0,2},{2,0},{1,3},{3,1},{4,6},{6,4},{5,7},{7,5},{8,10},{10,8},{9,1... | collective-permute-start | bytes 368648 | tf_op jit(solution)/shard_map/ppermute | solution.py:299
  8.8 9.0 %collective-permute-start.5 = (bf16[240,256]{1,0:T(8,128)(2,1)S(1)}, bf16[240,256]{1,0:T(8,128)(2,1)S(1)}, u32[]{:S(2)}, u32[]{:S(2)}) collective-permute-start(bf16[240,256]{1,0:T(8,128)(2,1)S(1)} %get-tuple-element.40), channel_id=1, source_target_pairs={{0,8},{4,12},{8,0},{12,4},{1,9},{5,13},{9,1},{13,5},{2,10},{6,14},... | collective-permute-start | bytes 368648 | tf_op jit(solution)/shard_map/ppermute | solution.py:299
  8.8 10.5 %collective-permute-start.3 = (bf16[240,256]{1,0:T(8,128)(2,1)S(1)}, bf16[240,256]{1,0:T(8,128)(2,1)S(1)}, u32[]{:S(2)}, u32[]{:S(2)}) collective-permute-start(bf16[240,256]{1,0:T(8,128)(2,1)S(1)} %get-tuple-element.37), channel_id=1, source_target_pairs={{0,6},{2,4},{4,2},{6,0},{8,14},{10,12},{12,10},{14,8},{1,7},{3,5},... | collective-permute-start | bytes 368648 | tf_op jit(solution)/shard_map/ppermute | solution.py:299
  9.4 9.9 %collective-permute-start.2 = (bf16[240,256]{1,0:T(8,128)(2,1)S(1)}, bf16[240,256]{1,0:T(8,128)(2,1)S(1)}, u32[]{:S(2)}, u32[]{:S(2)}) collective-permute-start(bf16[240,256]{1,0:T(8,128)(2,1)S(1)} %get-tuple-element.37), channel_id=1, source_target_pairs={{0,4},{4,0},{8,12},{12,8},{1,5},{5,1},{9,13},{13,9},{2,6},{6,2},{1... | collective-permute-start | bytes 368648 | tf_op jit(solution)/shard_map/ppermute | solution.py:299
  13.2 6.1 %collective-permute-start.4 = (bf16[240,256]{1,0:T(8,128)(2,1)S(1)}, bf16[240,256]{1,0:T(8,128)(2,1)S(1)}, u32[]{:S(2)}, u32[]{:S(2)}) collective-permute-start(bf16[240,256]{1,0:T(8,128)(2,1)S(1)} %collective-permute-done.refs_3_), channel_id=1, source_target_pairs={{0,2},{2,0},{1,3},{3,1},{4,6},{6,4},{5,7},{7,5},{8,10},{10,8},{9,1... | collective-permute-start | bytes 368648 | tf_op jit(solution)/shard_map/ppermute | solution.py:299
  17.8 4.9 %collective-permute-start.6 = (bf16[240,256]{1,0:T(8,128)(2,1)S(1)}, bf16[240,256]{1,0:T(8,128)(2,1)S(1)}, u32[]{:S(2)}, u32[]{:S(2)}) collective-permute-start(bf16[240,256]{1,0:T(8,128)(2,1)S(1)} %collective-permute-done.5.refs_2_), channel_id=1, source_target_pairs={{0,2},{2,0},{1,3},{3,1},{4,6},{6,4},{5,7},{7,5},{8,10},{10,8},{9,1... | collective-permute-start | bytes 368648 | tf_op jit(solution)/shard_map/ppermute | solution.py:299
  19.3 3.4 %collective-permute-start.8 = (bf16[960,256]{1,0:T(8,128)(2,1)S(1)}, bf16[960,256]{1,0:T(8,128)(2,1)S(1)}, u32[]{:S(2)}, u32[]{:S(2)}) collective-permute-start(bf16[960,256]{1,0:T(8,128)(2,1)S(1)} %stack.3.mine), channel_id=1, source_target_pairs={{0,1},{1,0},{2,3},{3,2},{4,5},{5,4},{6,7},{7,6},{8,9},{9,8},{10,11... | collective-permute-start | bytes 1474568 | tf_op jit(solution)/shard_map/ppermute | solution.py:299
  22.7 1.9 %collective-permute-start.7 = (bf16[960,256]{1,0:T(8,128)(2,1)S(1)}, bf16[960,256]{1,0:T(8,128)(2,1)S(1)}, u32[]{:S(2)}, u32[]{:S(2)}) collective-permute-start(bf16[960,256]{1,0:T(8,128)(2,1)S(1)} %stack.2.mine), channel_id=1, source_target_pairs={{0,1},{1,0},{2,3},{3,2},{4,5},{5,4},{6,7},{7,6},{8,9},{9,8},{10,11... | collective-permute-start | bytes 1474568 | tf_op jit(solution)/shard_map/ppermute | solution.py:299

commit v9 on v8

--- a/solution.py
+++ b/solution.py
@@ -68,8 +68,9 @@
         < lax.broadcasted_iota(jnp.int32, (tokens, tokens), 1)
     ).astype(F32).astype(BF16)
     position = dot(member.astype(BF16), earlier)
-    slot = lax.broadcasted_iota(jnp.int32, (SLOTS, tokens), 0).astype(F32)
-    rows = lax.broadcasted_iota(jnp.int32, (SLOTS, 1), 0).astype(F32)
+    row = lax.broadcasted_iota(jnp.int32, (MAIN + BLOCKS * REST, 1), 0)
+    block_of = (row - MAIN) // REST
+    slot = jnp.where(row < MAIN, row, row - block_of * REST).astype(F32)
     picks, scales, fills = [], [], []
     for step in range(experts):
         hit = (slot == position[step : step + 1, :]) & (member[step : step + 1, :] > 0.5)
@@ -77,22 +78,21 @@
         scale = jnp.sum(pick * weights[step], axis=1, keepdims=True)
         scales.append(jnp.where(first, 1.0, scale))
         count = jnp.sum(members[step], axis=1, keepdims=True)
-        fills.append(jnp.where((rows >= count) & first, EMPTY, 0.0))
+        fills.append(jnp.where((slot >= count) & first, EMPTY, 0.0))
         picks.append(pick.astype(BF16))
     picks = jnp.concatenate(picks, axis=0)
     scales = jnp.concatenate(scales, axis=0)
     fills = jnp.concatenate(fills, axis=0)
-    places = rest_places((BLOCKS * REST, BLOCKS * 16), 0, 1)
     tok_copy.wait()
-    packed = (dot(picks, source_ref[...]) * scales + fills).astype(BF16)
-    rests = []
-    for block in range(BLOCKS):
-        for step in range(experts):
-            tile = packed[step * SLOTS : (step + 1) * SLOTS, block * cut : (block + 1) * cut]
-            out_refs[step][pl.ds(block * MAIN, MAIN), :] = tile[:MAIN]
-            rests.append(tile[MAIN:])
+    packed = dot(picks, source_ref[...]) * scales + fills
+    size = MAIN + BLOCKS * REST
     for step in range(experts):
-        rest = dot(places, jnp.concatenate(rests[step::experts], axis=0))
+        chunk = packed[step * size : step * size + size]
+        rest = chunk[MAIN:, :cut]
+        for block in range(BLOCKS):
+            columns = slice(block * cut, block * cut + cut)
+            out_refs[step][pl.ds(block * MAIN, MAIN), :] = chunk[:MAIN, columns].astype(BF16)
+            rest = jnp.where(block_of[MAIN:] == block, chunk[MAIN:, columns], rest)
         out_refs[step][pl.ds(BLOCKS * MAIN, BLOCKS * REST), :] = rest.astype(BF16)
 
 
@@ -197,12 +197,12 @@
 def activations(x_rows, q_rows, w_gate, w_up, w_down):
     gate_pre = dot(w_gate[...], x_rows[...], 1, 1)
     up_pre = dot(w_up[...], x_rows[...], 1, 1)
-    hidden_grad = dot(w_down[...], q_rows[...], 1, 1)
     gate_sig = jax.nn.sigmoid(gate_pre)
     gate_act = gate_pre * gate_sig
     hidden = (gate_act * up_pre).astype(BF16)
+    hidden_grad = dot(w_down[...], q_rows[...], 1, 1)
+    up_grad = (hidden_grad * gate_act).astype(BF16)
     gate_grad = (hidden_grad * up_pre * gate_sig * (1.0 + gate_pre * (1.0 - gate_sig))).astype(BF16)
-    up_grad = (hidden_grad * gate_act).astype(BF16)
     return gate_grad, up_grad, hidden
 
 
@@ -211,7 +211,7 @@
     join([(mine, theirs, 0, experts)], x_rows, q_rows)
     for piece, act in enumerate(activations(x_rows, q_rows, w_gate, w_up, w_down)):
         acts[piece] = act
-    for piece, rows in ((2, q_rows), (0, x_rows), (1, x_rows)):
+    for piece, rows in ((2, q_rows), (1, x_rows), (0, x_rows)):
         grads[piece] = dot(acts[piece], rows[...]).astype(BF16)
     total = jnp.zeros((1, 128), F32)
     for step in range(experts):
@@ -312,7 +312,7 @@
     r2 = send(packed[2], "expert", 2)
     weights = load(weights, fragment, r0)
     r3, x0, *weights = tie(r3, x0, *weights)
-    r2, *weights = tie(r2, *weights)
+    r2, r0 = tie(r2, r0)
     x3 = send(r3, "replica", 1)
     x2 = send(r2, "replica", 1)
     r1, x1, x3 = tie(r1, x1, x3)

time: 27 us -> 27 us (level)
  no operation moved by 1% of the time
where the time goes in v9:
time: 27 us; the launch traced here: 26.8 us
  starting transfers between devices  12.8 us (47%)
  Pallas kernels  7.07 us (26%)
  waiting for transfers between devices  5.56 us (21%)
  between operations  1.36 us (5%)
    ppermute x9, starting transfers between devices, send(): lax.ppermute(array, axis, [(index, peer(index, step, size)) for index in...  12.8 us
    ppermute x9, waiting for transfers between devices, send(): lax.ppermute(array, axis, [(index, peer(index, step, size)) for index in...  5.56 us
    pallas_call x1, Pallas kernels, other(): pl.pallas_call(functools.partial(other_kernel, chunks), out_shape=[jax.Sh...  2.21 us
    pallas_call x1, Pallas kernels, own(): pl.pallas_call(functools.partial(own_kernel, experts), out_shape=[pltpu.V...  1.67 us
    pallas_call x1, Pallas kernels, load(): pl.pallas_call(functools.partial(load_kernel, count), out_shape=[pltpu.VM...  1.64 us
    pallas_call x1, Pallas kernels, pack(): pl.pallas_call(functools.partial(pack_kernel, experts), out_shape=[pltpu....  1.49 us
  transfers between devices with their start and end apart: 9, of which 4 were waited for; matrix products, arithmetic and copies ran while one was open for 0% of the time, Pallas kernels for 13%

profile of v9, /device:TPU:0, one launch (start us, length us, event | category | flops | bytes accessed | tf_op | source)
XLA Modules:
  0.0 26.8 jit_solution(12007244139132676861)
XLA Ops:
  0.6 1.5 %pack.1 = (bf16[240,256]{1,0:T(8,128)(2,1)S(1)}, bf16[240,256]{1,0:T(8,128)(2,1)S(1)}, bf16[240,256]{1,0:T(8,128)(2,1)S(1)}, bf16[240,256]{1,0:T(8,128)(2,1)S(1)}) custom-call(bf16[240,1024]{1,0:T(8,128)(2,1)} %bitcast.18, bf16[240,1024]{1,0:T(8,128)(2,1)} %bitcast.19, s32[8,240]{1,0:T(8,128)} %bitcast.20, f32[8,240]{1,0:T(8,128)} %bitcast.21), custom_call_target="tpu_custom_call" | custom-call | tf_op jit(solution)/shard_map/pack/pallas_call | solution.py:158
  2.1 5.1 %collective-permute-start = (bf16[240,256]{1,0:T(8,128)(2,1)S(1)}, bf16[240,256]{1,0:T(8,128)(2,1)S(1)}, u32[]{:S(2)}, u32[]{:S(2)}) collective-permute-start(bf16[240,256]{1,0:T(8,128)(2,1)S(1)} %get-tuple-element.29), channel_id=1, source_target_pairs={{0,12},{4,8},{8,4},{12,0},{1,13},{5,9},{9,5},{13,1},{2,14},{6,10},... | collective-permute-start | bytes 368648 | tf_op jit(solution)/shard_map/ppermute | solution.py:299
  7.2 1.5 %collective-permute-start.1 = (bf16[240,256]{1,0:T(8,128)(2,1)S(1)}, bf16[240,256]{1,0:T(8,128)(2,1)S(1)}, u32[]{:S(2)}, u32[]{:S(2)}) collective-permute-start(bf16[240,256]{1,0:T(8,128)(2,1)S(1)} %get-tuple-element.44.refs_4_.refs_0_), channel_id=1, source_target_pairs={{0,2},{2,0},{1,3},{3,1},{4,6},{6,4},{5,7},{7,5},{8,10},{10,8},{9,1... | collective-permute-start | bytes 368648 | tf_op jit(solution)/shard_map/ppermute | solution.py:299
  8.7 0.0 collective-permute-start.5
  8.7 0.6 %collective-permute-start.3 = (bf16[240,256]{1,0:T(8,128)(2,1)S(1)}, bf16[240,256]{1,0:T(8,128)(2,1)S(1)}, u32[]{:S(2)}, u32[]{:S(2)}) collective-permute-start(bf16[240,256]{1,0:T(8,128)(2,1)S(1)} %get-tuple-element.35), channel_id=1, source_target_pairs={{0,6},{2,4},{4,2},{6,0},{8,14},{10,12},{12,10},{14,8},{1,7},{3,5},... | collective-permute-start | bytes 368648 | tf_op jit(solution)/shard_map/ppermute | solution.py:299
  9.3 1.4 %collective-permute-start.2 = (bf16[240,256]{1,0:T(8,128)(2,1)S(1)}, bf16[240,256]{1,0:T(8,128)(2,1)S(1)}, u32[]{:S(2)}, u32[]{:S(2)}) collective-permute-start(bf16[240,256]{1,0:T(8,128)(2,1)S(1)} %get-tuple-element.35), channel_id=1, source_target_pairs={{0,4},{4,0},{8,12},{12,8},{1,5},{5,1},{9,13},{13,9},{2,6},{6,2},{1... | collective-permute-start | bytes 368648 | tf_op jit(solution)/shard_map/ppermute | solution.py:299
  11.4 1.6 %load.1 = (bf16[384,1024]{1,0:T(8,128)(2,1)S(1)}, bf16[384,1024]{1,0:T(8,128)(2,1)S(1)}, bf16[384,1024]{1,0:T(8,128)(2,1)S(1)}) custom-call(bf16[384,1024]{1,0:T(8,128)(2,1)} %bitcast.15, bf16[384,1024]{1,0:T(8,128)(2,1)} %bitcast.16, bf16[384,1024]{1,0:T(8,128)(2,1)} %bitcast.17, s32[1]{0:T(128)S(6)} %copy.12.refs_3_.frag_ref, ...), custom_call_target="tpu_custom_call" | custom-call | tf_op jit(solution)/shard_map/load/pallas_call | solution.py:124
  13.0 0.0 collective-permute-done.refs_3_
  13.0 0.1 collective-permute-done.1.refs_0_
  13.1 2.6 %collective-permute-start.4 = (bf16[240,256]{1,0:T(8,128)(2,1)S(1)}, bf16[240,256]{1,0:T(8,128)(2,1)S(1)}, u32[]{:S(2)}, u32[]{:S(2)}) collective-permute-start(bf16[240,256]{1,0:T(8,128)(2,1)S(1)} %collective-permute-done.refs_3_), channel_id=1, source_target_pairs={{0,2},{2,0},{1,3},{3,1},{4,6},{6,4},{5,7},{7,5},{8,10},{10,8},{9,1... | collective-permute-start | bytes 368648 | tf_op jit(solution)/shard_map/ppermute | solution.py:299
  15.7 2.0 %collective-permute-done.5.refs_2_ = bf16[240,256]{1,0:T(8,128)(2,1)S(1)} collective-permute-done((bf16[240,256]{1,0:T(8,128)(2,1)S(1)}, bf16[240,256]{1,0:T(8,128)(2,1)S(1)}, u32[]{:S(2)}, u32[]{:S(2)}) %collective-permute-start.5) | collective-permute-done | bytes 122912 | tf_op jit(solution)/shard_map/ppermute | solution.py:299
  17.7 1.5 %collective-permute-start.6 = (bf16[240,256]{1,0:T(8,128)(2,1)S(1)}, bf16[240,256]{1,0:T(8,128)(2,1)S(1)}, u32[]{:S(2)}, u32[]{:S(2)}) collective-permute-start(bf16[240,256]{1,0:T(8,128)(2,1)S(1)} %collective-permute-done.5.refs_2_), channel_id=1, source_target_pairs={{0,2},{2,0},{1,3},{3,1},{4,6},{6,4},{5,7},{7,5},{8,10},{10,8},{9,1... | collective-permute-start | bytes 368648 | tf_op jit(solution)/shard_map/ppermute | solution.py:299
  19.2 0.0 collective-permute-done.3.refs_1_
  19.2 0.0 collective-permute-done.2.refs_1_
  19.2 0.0 collective-permute-done.4.refs_3_
  19.3 0.1 collective-permute-start.8
  19.3 3.3 %collective-permute-done.6.refs_2_ = bf16[240,256]{1,0:T(8,128)(2,1)S(1)} collective-permute-done((bf16[240,256]{1,0:T(8,128)(2,1)S(1)}, bf16[240,256]{1,0:T(8,128)(2,1)S(1)}, u32[]{:S(2)}, u32[]{:S(2)}) %collective-permute-start.6) | collective-permute-done | bytes 122912 | tf_op jit(solution)/shard_map/ppermute | solution.py:299
  22.6 0.1 collective-permute-start.7
  22.7 0.0 collective-permute-done.8.theirs
  22.7 1.7 %own.1 = (bf16[3,384,1024]{2,1,0:T(8,128)(2,1)S(1)}, bf16[3,384,256]{2,1,0:T(8,128)(2,1)S(1)}, bf16[256,1024]{1,0:T(8,128)(2,1)S(1)}, bf16[256,1024]{1,0:T(8,128)(2,1)S(1)}, f32[1,128]{1,0:T(1,128)}) custom-call(s32[1]{0:T(128)S(6)} %copy.12.refs_3_.frag_ref, bf16[960,256]{1,0:T(8,128)(2,1)S(1)} %stack.3.mine, ...), custom_call_target="tpu_custom_call" | custom-call | flops 1207959552 | bytes 4718592 | tf_op jit(solution)/shard_map/own/pallas_call | solution.py:227
  24.4 0.2 collective-permute-done.7.theirs
  24.6 2.2 %other.1 = (bf16[384,1024]{1,0:T(8,128)(2,1)}, bf16[384,1024]{1,0:T(8,128)(2,1)}, bf16[384,1024]{1,0:T(8,128)(2,1)}) custom-call(s32[1]{0:T(128)S(6)} %copy.12.refs_3_.frag_ref, bf16[960,256]{1,0:T(8,128)(2,1)S(1)} %stack.2.mine, bf16[960,256]{1,0:T(8,128)(2,1)S(1)} %collective-permute-done.7.theirs, bf16[384,1024]{1,0:T(8,128)(2,1)S(1)} %get-tuple-element.41.w_gate, ...), custom_call_target="tpu_custom_call" | custom-call | flops 805306368 | bytes 3145728 | tf_op jit(solution)/shard_map/other/pallas_call | solution.py:282
  (2 shorter events, 0.1 us)
Async XLA Ops:
  2.1 10.9 %collective-permute-start = (bf16[240,256]{1,0:T(8,128)(2,1)S(1)}, bf16[240,256]{1,0:T(8,128)(2,1)S(1)}, u32[]{:S(2)}, u32[]{:S(2)}) collective-permute-start(bf16[240,256]{1,0:T(8,128)(2,1)S(1)} %get-tuple-element.29), channel_id=1, source_target_pairs={{0,12},{4,8},{8,4},{12,0},{1,13},{5,9},{9,5},{13,1},{2,14},{6,10},... | collective-permute-start | bytes 368648 | tf_op jit(solution)/shard_map/ppermute | solution.py:299
  7.2 5.9 %collective-permute-start.1 = (bf16[240,256]{1,0:T(8,128)(2,1)S(1)}, bf16[240,256]{1,0:T(8,128)(2,1)S(1)}, u32[]{:S(2)}, u32[]{:S(2)}) collective-permute-start(bf16[240,256]{1,0:T(8,128)(2,1)S(1)} %get-tuple-element.44.refs_4_.refs_0_), channel_id=1, source_target_pairs={{0,2},{2,0},{1,3},{3,1},{4,6},{6,4},{5,7},{7,5},{8,10},{10,8},{9,1... | collective-permute-start | bytes 368648 | tf_op jit(solution)/shard_map/ppermute | solution.py:299
  8.7 9.0 %collective-permute-start.5 = (bf16[240,256]{1,0:T(8,128)(2,1)S(1)}, bf16[240,256]{1,0:T(8,128)(2,1)S(1)}, u32[]{:S(2)}, u32[]{:S(2)}) collective-permute-start(bf16[240,256]{1,0:T(8,128)(2,1)S(1)} %get-tuple-element.38), channel_id=1, source_target_pairs={{0,8},{4,12},{8,0},{12,4},{1,9},{5,13},{9,1},{13,5},{2,10},{6,14},... | collective-permute-start | bytes 368648 | tf_op jit(solution)/shard_map/ppermute | solution.py:299
  8.7 10.5 %collective-permute-start.3 = (bf16[240,256]{1,0:T(8,128)(2,1)S(1)}, bf16[240,256]{1,0:T(8,128)(2,1)S(1)}, u32[]{:S(2)}, u32[]{:S(2)}) collective-permute-start(bf16[240,256]{1,0:T(8,128)(2,1)S(1)} %get-tuple-element.35), channel_id=1, source_target_pairs={{0,6},{2,4},{4,2},{6,0},{8,14},{10,12},{12,10},{14,8},{1,7},{3,5},... | collective-permute-start | bytes 368648 | tf_op jit(solution)/shard_map/ppermute | solution.py:299
  9.3 9.9 %collective-permute-start.2 = (bf16[240,256]{1,0:T(8,128)(2,1)S(1)}, bf16[240,256]{1,0:T(8,128)(2,1)S(1)}, u32[]{:S(2)}, u32[]{:S(2)}) collective-permute-start(bf16[240,256]{1,0:T(8,128)(2,1)S(1)} %get-tuple-element.35), channel_id=1, source_target_pairs={{0,4},{4,0},{8,12},{12,8},{1,5},{5,1},{9,13},{13,9},{2,6},{6,2},{1... | collective-permute-start | bytes 368648 | tf_op jit(solution)/shard_map/ppermute | solution.py:299
  13.1 6.1 %collective-permute-start.4 = (bf16[240,256]{1,0:T(8,128)(2,1)S(1)}, bf16[240,256]{1,0:T(8,128)(2,1)S(1)}, u32[]{:S(2)}, u32[]{:S(2)}) collective-permute-start(bf16[240,256]{1,0:T(8,128)(2,1)S(1)} %collective-permute-done.refs_3_), channel_id=1, source_target_pairs={{0,2},{2,0},{1,3},{3,1},{4,6},{6,4},{5,7},{7,5},{8,10},{10,8},{9,1... | collective-permute-start | bytes 368648 | tf_op jit(solution)/shard_map/ppermute | solution.py:299
  17.7 4.9 %collective-permute-start.6 = (bf16[240,256]{1,0:T(8,128)(2,1)S(1)}, bf16[240,256]{1,0:T(8,128)(2,1)S(1)}, u32[]{:S(2)}, u32[]{:S(2)}) collective-permute-start(bf16[240,256]{1,0:T(8,128)(2,1)S(1)} %collective-permute-done.5.refs_2_), channel_id=1, source_target_pairs={{0,2},{2,0},{1,3},{3,1},{4,6},{6,4},{5,7},{7,5},{8,10},{10,8},{9,1... | collective-permute-start | bytes 368648 | tf_op jit(solution)/shard_map/ppermute | solution.py:299
  19.3 3.5 %collective-permute-start.8 = (bf16[960,256]{1,0:T(8,128)(2,1)S(1)}, bf16[960,256]{1,0:T(8,128)(2,1)S(1)}, u32[]{:S(2)}, u32[]{:S(2)}) collective-permute-start(bf16[960,256]{1,0:T(8,128)(2,1)S(1)} %stack.3.mine), channel_id=1, source_target_pairs={{0,1},{1,0},{2,3},{3,2},{4,5},{5,4},{6,7},{7,6},{8,9},{9,8},{10,11... | collective-permute-start | bytes 1474568 | tf_op jit(solution)/shard_map/ppermute | solution.py:299
  22.6 1.9 %collective-permute-start.7 = (bf16[960,256]{1,0:T(8,128)(2,1)S(1)}, bf16[960,256]{1,0:T(8,128)(2,1)S(1)}, u32[]{:S(2)}, u32[]{:S(2)}) collective-permute-start(bf16[960,256]{1,0:T(8,128)(2,1)S(1)} %stack.2.mine), channel_id=1, source_target_pairs={{0,1},{1,0},{2,3},{3,2},{4,5},{5,4},{6,7},{7,6},{8,9},{9,8},{10,11... | collective-permute-start | bytes 1474568 | tf_op jit(solution)/shard_map/ppermute | solution.py:299

commit v10 on v9

--- a/solution.py
+++ b/solution.py
@@ -207,12 +207,15 @@
 
 
 def own_kernel(experts, frag_ref, mine, theirs, w_gate, w_up, w_down, *refs):
-    grads, acts, x_rows, q_rows, load_out = refs
+    grads, sums, load_out, acts, x_rows, q_rows = refs
     join([(mine, theirs, 0, experts)], x_rows, q_rows)
     for piece, act in enumerate(activations(x_rows, q_rows, w_gate, w_up, w_down)):
         acts[piece] = act
+    cut = sums.shape[2]
+    frag_columns = pl.ds(pl.multiple_of(frag_ref[0] * cut, cut), cut)
     for piece, rows in ((2, q_rows), (1, x_rows), (0, x_rows)):
         grads[piece] = dot(acts[piece], rows[...]).astype(BF16)
+        sums[piece] = dot(acts[piece], rows[:, frag_columns])
     total = jnp.zeros((1, 128), F32)
     for step in range(experts):
         full = x_rows[pl.ds(step * SLOTS, SLOTS), pl.ds(0, 128)].astype(F32) < EMPTY / 2
@@ -228,13 +231,12 @@
         functools.partial(own_kernel, experts),
         out_shape=[
             pltpu.VMEM((3, units, width), BF16),
-            pltpu.VMEM((3, units, rows), BF16),
-            pltpu.VMEM((rows, width), BF16),
-            pltpu.VMEM((rows, width), BF16),
+            pltpu.VMEM((3, units, width // FRAGS), F32),
             jax.ShapeDtypeStruct((1, 128), F32),
         ],
         in_specs=[SMEM] + [VMEM] * 5,
-        out_specs=[VMEM] * 5,
+        out_specs=[VMEM] * 3,
+        scratch_shapes=[pltpu.VMEM((3, units, rows), BF16)] + [pltpu.VMEM((rows, width), BF16)] * 2,
         name="own",
         compiler_params=pltpu.CompilerParams(vmem_limit_bytes=24 << 20),
         cost_estimate=pl.CostEstimate(
@@ -244,7 +246,7 @@
 
 
 def other_kernel(chunks, frag_ref, mine, theirs, w_gate, w_up, w_down, *refs):
-    grads, own_acts, own_x, own_q, *outs, x_rows, q_rows, cuts, sems = refs
+    grads, sums, *outs, x_rows, q_rows, cuts, sems = refs
     cut = cuts.shape[2]
     frag = frag_ref[0]
     copies = []
@@ -262,10 +264,8 @@
     join([(mine, theirs, 0, chunks)], x_rows, q_rows)
     acts = activations(x_rows, q_rows, w_gate, w_up, w_down)
     columns = pl.ds(pl.multiple_of(frag * cut, cut), cut)
-    x_both = jnp.concatenate([own_x[:, columns], x_rows[:, columns]], axis=0)
-    q_both = jnp.concatenate([own_q[:, columns], q_rows[:, columns]], axis=0)
-    for piece, rows in ((2, q_both), (0, x_both), (1, x_both)):
-        grad = dot(jnp.concatenate([own_acts[piece], acts[piece]], axis=1), rows)
+    for piece, rows in ((2, q_rows), (0, x_rows), (1, x_rows)):
+        grad = sums[piece] + dot(acts[piece], rows[:, columns])
         cuts[piece] = (grad * 0.5).astype(BF16)
         copies.append(
             pltpu.make_async_copy(cuts.at[piece], outs[piece].at[:, columns], sems.at[piece, 0])
@@ -282,7 +282,7 @@
     return pl.pallas_call(
         functools.partial(other_kernel, chunks),
         out_shape=[jax.ShapeDtypeStruct((units, width), BF16)] * 3,
-        in_specs=[SMEM] + [VMEM] * 9,
+        in_specs=[SMEM] + [VMEM] * 7,
         out_specs=[HBM] * 3,
         scratch_shapes=[pltpu.VMEM((rows, width), BF16)] * 2
         + [pltpu.VMEM((3, units, cut), BF16), pltpu.SemaphoreType.DMA((3, FRAGS))],
@@ -329,12 +329,9 @@
     mine = [packed[0]] + [send(packed[step], "expert", step) for step in range(1, experts)]
     mine = stack(mine)
     theirs = send(mine, "tensor", 1)
-    grads, acts, x_rows, q_rows, filled = own(experts, fragment, mine, theirs, weights)
-    cut = x_rows.shape[1] // FRAGS
-    begin = fragment[0] * cut
-    sides = [lax.dynamic_slice_in_dim(rows, begin, cut, 1) for rows in (x_rows, x_rows, q_rows)]
-    pieces = jnp.stack([dot(act, side) for act, side in zip(acts, sides)]).astype(BF16)
-    synced = lax.psum(pieces, "replica").astype(F32)
+    grads, sums, filled = own(experts, fragment, mine, theirs, weights)
+    begin = fragment[0] * sums.shape[2]
+    synced = lax.psum(sums.astype(BF16), "replica").astype(F32)
     grads = [
         lax.dynamic_update_slice_in_dim(grad, (piece / replicas).astype(BF16), begin, 1)
         for grad, piece in zip(grads, synced)

time: 27 us -> 27 us (level)
  no operation moved by 1% of the time
where the time goes in v10:
time: 27 us; the launch traced here: 26.7 us
  starting transfers between devices  12.8 us (47%)
  Pallas kernels  7.16 us (27%)
  waiting for transfers between devices  5.45 us (20%)
  between operations  1.36 us (5%)
    ppermute x9, starting transfers between devices, send(): lax.ppermute(array, axis, [(index, peer(index, step, size)) for index in...  12.8 us
    ppermute x9, waiting for transfers between devices, send(): lax.ppermute(array, axis, [(index, peer(index, step, size)) for index in...  5.45 us
    pallas_call x1, Pallas kernels, other(): pl.pallas_call(functools.partial(other_kernel, chunks), out_shape=[jax.Sh...  2.19 us
    pallas_call x1, Pallas kernels, own(): pl.pallas_call(functools.partial(own_kernel, experts), out_shape=[pltpu.V...  1.78 us
    pallas_call x1, Pallas kernels, load(): pl.pallas_call(functools.partial(load_kernel, count), out_shape=[pltpu.VM...  1.64 us
    pallas_call x1, Pallas kernels, pack(): pl.pallas_call(functools.partial(pack_kernel, experts), out_shape=[pltpu....  1.49 us
  transfers between devices with their start and end apart: 9, of which 4 were waited for; matrix products, arithmetic and copies ran while one was open for 0% of the time, Pallas kernels for 13%

profile of v10, /device:TPU:0, one launch (start us, length us, event | category | flops | bytes accessed | tf_op | source)
XLA Modules:
  0.0 26.7 jit_solution(6820552333409048859)
XLA Ops:
  0.6 1.5 %pack.1 = (bf16[240,256]{1,0:T(8,128)(2,1)S(1)}, bf16[240,256]{1,0:T(8,128)(2,1)S(1)}, bf16[240,256]{1,0:T(8,128)(2,1)S(1)}, bf16[240,256]{1,0:T(8,128)(2,1)S(1)}) custom-call(bf16[240,1024]{1,0:T(8,128)(2,1)} %bitcast.18, bf16[240,1024]{1,0:T(8,128)(2,1)} %bitcast.19, s32[8,240]{1,0:T(8,128)} %bitcast.20, f32[8,240]{1,0:T(8,128)} %bitcast.21), custom_call_target="tpu_custom_call" | custom-call | tf_op jit(solution)/shard_map/pack/pallas_call | solution.py:158
  2.1 5.1 %collective-permute-start = (bf16[240,256]{1,0:T(8,128)(2,1)S(1)}, bf16[240,256]{1,0:T(8,128)(2,1)S(1)}, u32[]{:S(2)}, u32[]{:S(2)}) collective-permute-start(bf16[240,256]{1,0:T(8,128)(2,1)S(1)} %get-tuple-element.27), channel_id=1, source_target_pairs={{0,12},{4,8},{8,4},{12,0},{1,13},{5,9},{9,5},{13,1},{2,14},{6,10},... | collective-permute-start | bytes 368648 | tf_op jit(solution)/shard_map/ppermute | solution.py:299
  7.2 1.5 %collective-permute-start.1 = (bf16[240,256]{1,0:T(8,128)(2,1)S(1)}, bf16[240,256]{1,0:T(8,128)(2,1)S(1)}, u32[]{:S(2)}, u32[]{:S(2)}) collective-permute-start(bf16[240,256]{1,0:T(8,128)(2,1)S(1)} %get-tuple-element.42.refs_4_.refs_0_), channel_id=1, source_target_pairs={{0,2},{2,0},{1,3},{3,1},{4,6},{6,4},{5,7},{7,5},{8,10},{10,8},{9,1... | collective-permute-start | bytes 368648 | tf_op jit(solution)/shard_map/ppermute | solution.py:299
  8.7 0.0 collective-permute-start.5
  8.7 0.6 %collective-permute-start.3 = (bf16[240,256]{1,0:T(8,128)(2,1)S(1)}, bf16[240,256]{1,0:T(8,128)(2,1)S(1)}, u32[]{:S(2)}, u32[]{:S(2)}) collective-permute-start(bf16[240,256]{1,0:T(8,128)(2,1)S(1)} %get-tuple-element.33), channel_id=1, source_target_pairs={{0,6},{2,4},{4,2},{6,0},{8,14},{10,12},{12,10},{14,8},{1,7},{3,5},... | collective-permute-start | bytes 368648 | tf_op jit(solution)/shard_map/ppermute | solution.py:299
  9.3 1.4 %collective-permute-start.2 = (bf16[240,256]{1,0:T(8,128)(2,1)S(1)}, bf16[240,256]{1,0:T(8,128)(2,1)S(1)}, u32[]{:S(2)}, u32[]{:S(2)}) collective-permute-start(bf16[240,256]{1,0:T(8,128)(2,1)S(1)} %get-tuple-element.33), channel_id=1, source_target_pairs={{0,4},{4,0},{8,12},{12,8},{1,5},{5,1},{9,13},{13,9},{2,6},{6,2},{1... | collective-permute-start | bytes 368648 | tf_op jit(solution)/shard_map/ppermute | solution.py:299
  11.4 1.6 %load.1 = (bf16[384,1024]{1,0:T(8,128)(2,1)S(1)}, bf16[384,1024]{1,0:T(8,128)(2,1)S(1)}, bf16[384,1024]{1,0:T(8,128)(2,1)S(1)}) custom-call(bf16[384,1024]{1,0:T(8,128)(2,1)} %bitcast.15, bf16[384,1024]{1,0:T(8,128)(2,1)} %bitcast.16, bf16[384,1024]{1,0:T(8,128)(2,1)} %bitcast.17, s32[1]{0:T(128)S(6)} %copy.12.refs_3_.frag_ref, ...), custom_call_target="tpu_custom_call" | custom-call | tf_op jit(solution)/shard_map/load/pallas_call | solution.py:124
  13.0 0.0 collective-permute-done.refs_3_
  13.0 0.1 collective-permute-done.1.refs_0_
  13.1 2.6 %collective-permute-start.4 = (bf16[240,256]{1,0:T(8,128)(2,1)S(1)}, bf16[240,256]{1,0:T(8,128)(2,1)S(1)}, u32[]{:S(2)}, u32[]{:S(2)}) collective-permute-start(bf16[240,256]{1,0:T(8,128)(2,1)S(1)} %collective-permute-done.refs_3_), channel_id=1, source_target_pairs={{0,2},{2,0},{1,3},{3,1},{4,6},{6,4},{5,7},{7,5},{8,10},{10,8},{9,1... | collective-permute-start | bytes 368648 | tf_op jit(solution)/shard_map/ppermute | solution.py:299
  15.7 2.0 %collective-permute-done.5.refs_2_ = bf16[240,256]{1,0:T(8,128)(2,1)S(1)} collective-permute-done((bf16[240,256]{1,0:T(8,128)(2,1)S(1)}, bf16[240,256]{1,0:T(8,128)(2,1)S(1)}, u32[]{:S(2)}, u32[]{:S(2)}) %collective-permute-start.5) | collective-permute-done | bytes 122912 | tf_op jit(solution)/shard_map/ppermute | solution.py:299
  17.7 1.5 %collective-permute-start.6 = (bf16[240,256]{1,0:T(8,128)(2,1)S(1)}, bf16[240,256]{1,0:T(8,128)(2,1)S(1)}, u32[]{:S(2)}, u32[]{:S(2)}) collective-permute-start(bf16[240,256]{1,0:T(8,128)(2,1)S(1)} %collective-permute-done.5.refs_2_), channel_id=1, source_target_pairs={{0,2},{2,0},{1,3},{3,1},{4,6},{6,4},{5,7},{7,5},{8,10},{10,8},{9,1... | collective-permute-start | bytes 368648 | tf_op jit(solution)/shard_map/ppermute | solution.py:299
  19.2 0.0 collective-permute-done.3.refs_1_
  19.2 0.0 collective-permute-done.2.refs_1_
  19.2 0.0 collective-permute-done.4.refs_3_
  19.3 0.1 collective-permute-start.8
  19.3 3.3 %collective-permute-done.6.refs_2_ = bf16[240,256]{1,0:T(8,128)(2,1)S(1)} collective-permute-done((bf16[240,256]{1,0:T(8,128)(2,1)S(1)}, bf16[240,256]{1,0:T(8,128)(2,1)S(1)}, u32[]{:S(2)}, u32[]{:S(2)}) %collective-permute-start.6) | collective-permute-done | bytes 122912 | tf_op jit(solution)/shard_map/ppermute | solution.py:299
  22.6 0.1 collective-permute-start.7
  22.7 0.0 collective-permute-done.8.theirs
  22.7 1.8 %own.1 = (bf16[3,384,1024]{2,1,0:T(8,128)(2,1)S(1)}, f32[3,384,256]{2,1,0:T(8,128)S(1)}, f32[1,128]{1,0:T(1,128)}) custom-call(s32[1]{0:T(128)S(6)} %copy.12.refs_3_.frag_ref, bf16[960,256]{1,0:T(8,128)(2,1)S(1)} %stack.3.mine, bf16[960,256]{1,0:T(8,128)(2,1)S(1)} %collective-permute-done.8.theirs, bf16[384,1024]{1,0:T(8,128)(2,1)S(1)} %get-tuple-element.39.w_gate, ...), custom_call_target="tpu_custom_call" | custom-call | flops 1207959552 | bytes 4718592 | tf_op jit(solution)/shard_map/own/pallas_call | solution.py:230
  24.5 0.1 collective-permute-done.7.theirs
  24.6 2.2 %other.1 = (bf16[384,1024]{1,0:T(8,128)(2,1)}, bf16[384,1024]{1,0:T(8,128)(2,1)}, bf16[384,1024]{1,0:T(8,128)(2,1)}) custom-call(s32[1]{0:T(128)S(6)} %copy.12.refs_3_.frag_ref, bf16[960,256]{1,0:T(8,128)(2,1)S(1)} %stack.2.mine, bf16[960,256]{1,0:T(8,128)(2,1)S(1)} %collective-permute-done.7.theirs, bf16[384,1024]{1,0:T(8,128)(2,1)S(1)} %get-tuple-element.39.w_gate, ...), custom_call_target="tpu_custom_call" | custom-call | flops 805306368 | bytes 3145728 | tf_op jit(solution)/shard_map/other/pallas_call | solution.py:282
  (2 shorter events, 0.1 us)
Async XLA Ops:
  2.1 10.9 %collective-permute-start = (bf16[240,256]{1,0:T(8,128)(2,1)S(1)}, bf16[240,256]{1,0:T(8,128)(2,1)S(1)}, u32[]{:S(2)}, u32[]{:S(2)}) collective-permute-start(bf16[240,256]{1,0:T(8,128)(2,1)S(1)} %get-tuple-element.27), channel_id=1, source_target_pairs={{0,12},{4,8},{8,4},{12,0},{1,13},{5,9},{9,5},{13,1},{2,14},{6,10},... | collective-permute-start | bytes 368648 | tf_op jit(solution)/shard_map/ppermute | solution.py:299
  7.2 5.9 %collective-permute-start.1 = (bf16[240,256]{1,0:T(8,128)(2,1)S(1)}, bf16[240,256]{1,0:T(8,128)(2,1)S(1)}, u32[]{:S(2)}, u32[]{:S(2)}) collective-permute-start(bf16[240,256]{1,0:T(8,128)(2,1)S(1)} %get-tuple-element.42.refs_4_.refs_0_), channel_id=1, source_target_pairs={{0,2},{2,0},{1,3},{3,1},{4,6},{6,4},{5,7},{7,5},{8,10},{10,8},{9,1... | collective-permute-start | bytes 368648 | tf_op jit(solution)/shard_map/ppermute | solution.py:299
  8.7 9.0 %collective-permute-start.5 = (bf16[240,256]{1,0:T(8,128)(2,1)S(1)}, bf16[240,256]{1,0:T(8,128)(2,1)S(1)}, u32[]{:S(2)}, u32[]{:S(2)}) collective-permute-start(bf16[240,256]{1,0:T(8,128)(2,1)S(1)} %get-tuple-element.36), channel_id=1, source_target_pairs={{0,8},{4,12},{8,0},{12,4},{1,9},{5,13},{9,1},{13,5},{2,10},{6,14},... | collective-permute-start | bytes 368648 | tf_op jit(solution)/shard_map/ppermute | solution.py:299
  8.7 10.5 %collective-permute-start.3 = (bf16[240,256]{1,0:T(8,128)(2,1)S(1)}, bf16[240,256]{1,0:T(8,128)(2,1)S(1)}, u32[]{:S(2)}, u32[]{:S(2)}) collective-permute-start(bf16[240,256]{1,0:T(8,128)(2,1)S(1)} %get-tuple-element.33), channel_id=1, source_target_pairs={{0,6},{2,4},{4,2},{6,0},{8,14},{10,12},{12,10},{14,8},{1,7},{3,5},... | collective-permute-start | bytes 368648 | tf_op jit(solution)/shard_map/ppermute | solution.py:299
  9.3 9.9 %collective-permute-start.2 = (bf16[240,256]{1,0:T(8,128)(2,1)S(1)}, bf16[240,256]{1,0:T(8,128)(2,1)S(1)}, u32[]{:S(2)}, u32[]{:S(2)}) collective-permute-start(bf16[240,256]{1,0:T(8,128)(2,1)S(1)} %get-tuple-element.33), channel_id=1, source_target_pairs={{0,4},{4,0},{8,12},{12,8},{1,5},{5,1},{9,13},{13,9},{2,6},{6,2},{1... | collective-permute-start | bytes 368648 | tf_op jit(solution)/shard_map/ppermute | solution.py:299
  13.1 6.1 %collective-permute-start.4 = (bf16[240,256]{1,0:T(8,128)(2,1)S(1)}, bf16[240,256]{1,0:T(8,128)(2,1)S(1)}, u32[]{:S(2)}, u32[]{:S(2)}) collective-permute-start(bf16[240,256]{1,0:T(8,128)(2,1)S(1)} %collective-permute-done.refs_3_), channel_id=1, source_target_pairs={{0,2},{2,0},{1,3},{3,1},{4,6},{6,4},{5,7},{7,5},{8,10},{10,8},{9,1... | collective-permute-start | bytes 368648 | tf_op jit(solution)/shard_map/ppermute | solution.py:299
  17.7 4.9 %collective-permute-start.6 = (bf16[240,256]{1,0:T(8,128)(2,1)S(1)}, bf16[240,256]{1,0:T(8,128)(2,1)S(1)}, u32[]{:S(2)}, u32[]{:S(2)}) collective-permute-start(bf16[240,256]{1,0:T(8,128)(2,1)S(1)} %collective-permute-done.5.refs_2_), channel_id=1, source_target_pairs={{0,2},{2,0},{1,3},{3,1},{4,6},{6,4},{5,7},{7,5},{8,10},{10,8},{9,1... | collective-permute-start | bytes 368648 | tf_op jit(solution)/shard_map/ppermute | solution.py:299
  19.3 3.5 %collective-permute-start.8 = (bf16[960,256]{1,0:T(8,128)(2,1)S(1)}, bf16[960,256]{1,0:T(8,128)(2,1)S(1)}, u32[]{:S(2)}, u32[]{:S(2)}) collective-permute-start(bf16[960,256]{1,0:T(8,128)(2,1)S(1)} %stack.3.mine), channel_id=1, source_target_pairs={{0,1},{1,0},{2,3},{3,2},{4,5},{5,4},{6,7},{7,6},{8,9},{9,8},{10,11... | collective-permute-start | bytes 1474568 | tf_op jit(solution)/shard_map/ppermute | solution.py:299
  22.6 1.9 %collective-permute-start.7 = (bf16[960,256]{1,0:T(8,128)(2,1)S(1)}, bf16[960,256]{1,0:T(8,128)(2,1)S(1)}, u32[]{:S(2)}, u32[]{:S(2)}) collective-permute-start(bf16[960,256]{1,0:T(8,128)(2,1)S(1)} %stack.2.mine), channel_id=1, source_target_pairs={{0,1},{1,0},{2,3},{3,2},{4,5},{5,4},{6,7},{7,6},{8,9},{9,8},{10,11... | collective-permute-start | bytes 1474568 | tf_op jit(solution)/shard_map/ppermute | solution.py:299
